TPU v7x, 256 devices: a whole 4x4x8 slice. The times are simulated.
256 devices in a mesh: seq: 32 (over x, z), node: 4 (over y), dev: 2 (over core).
Axes of the slice: x: 4, y: 4, z: 8, core: 2. Of those that a mesh axis runs over, the one named last changes fastest.
Arguments:
- hidden: bfloat16 [8, 4096, 4096], P(('node', 'dev'), None, 'seq'), may hold values from -6 to 6
- out_grad: bfloat16 [8, 4096, 4096], P(('node', 'dev'), None, 'seq'), may hold values from -6 to 6
- queries: bfloat16 [8, 4096, 2, 128], P(('node', 'dev'), 'seq'), may hold values from -6 to 6
- key_heads: bfloat16 [8, 4096, 128], P(('node', 'dev'), 'seq'), may hold values from -6 to 6
- value_heads: bfloat16 [8, 4096, 128], P(('node', 'dev'), 'seq'), may hold values from -6 to 6
- routes: int32 [8, 4096, 2], P(('node', 'dev')), may hold values from 0 to 127, all different within a row; in each aligned block of 128 rows (0 to 127, 128 to 255, ..., all dimensions but the last counted through in order) at most 3 rows name the same one
- route_gates: float32 [8, 4096, 2], P(('node', 'dev'), 'seq'), may hold values from 0.05 to 0.5
- w_query: bfloat16 [128, 4096, 128], P(('node', 'dev'), 'seq'), may hold values from -0.09375 to 0.09375
- w_out: bfloat16 [128, 128, 4096], P(('node', 'dev'), None, 'seq'), may hold values from -0.5 to 0.5
- w_key: bfloat16 [4096, 128], P('seq'), may hold values from -0.09375 to 0.09375
- w_value: bfloat16 [4096, 128], P('seq'), may hold values from -0.09375 to 0.09375
Outputs:
- grad_hidden: bfloat16 [8, 4096, 4096], P(('node', 'dev'), None, 'seq')
- grad_wq: float32 [128, 4096, 128], P(('node', 'dev'), 'seq')
- grad_wo: float32 [128, 128, 4096], P(('node', 'dev'), None, 'seq')
- key_projection_gradient: float32 [4096, 128], P('seq')
- value_projection_gradient: float32 [4096, 128], P('seq')
Inputs may be any that keep to these rules, and one draw needn't show every extreme that they name: A token names 2 different experts. In each block of 128 consecutive positions of one sequence no expert is named by more than 3 routes, and in some blocks one expert is named by exactly 3.
All inputs are finite; a program needn't handle non-finite values.
Results may differ from a plain program's by a relative error of at most 0.018.
Values may be sent and summed in bfloat16 or wider, within the bound.
No kernel may reach another device: no remote copies, remote signals or barrier semaphores. Data moves between devices by JAX's collectives and lax.ppermute only.
A program may use at most 128 MiB of HBM per device.

v0:
```python
import math

import jax
import jax.numpy as jnp
from jax import lax
from jax.sharding import PartitionSpec as P

HD = 128
EXPERTS = 128
TOP = 2
CAP = 3


def block_onehots(route_table, block_len):
    n_blocks = route_table.shape[0] // block_len
    flat_routes = route_table.reshape(n_blocks, block_len * TOP)
    is_expert = (
        flat_routes[:, :, None] == jnp.arange(EXPERTS, dtype=jnp.int32)[None, None, :]
    ).astype(jnp.int32)
    earlier = jnp.cumsum(is_expert, axis=1) - is_expert
    slot_ids = jnp.sum(earlier * is_expert, axis=2)
    hot_expert = is_expert.astype(jnp.bfloat16).reshape(n_blocks, block_len, TOP, EXPERTS)
    hot_slot = (slot_ids[:, :, None] == jnp.arange(CAP, dtype=jnp.int32)[None, None, :]).astype(
        jnp.bfloat16
    )
    return (hot_expert, hot_slot.reshape(n_blocks, block_len, TOP, CAP))


def attend(query_rows, key_rows, value_rows, head_grad, gate_rows, start_pos):
    score_scale = 1.0 / math.sqrt(HD)
    flat_query = query_rows.reshape(-1, HD)
    n_query = flat_query.shape[0]
    query_pos = start_pos + jnp.arange(n_query, dtype=jnp.int32) // TOP
    key_pos = jnp.arange(key_rows.shape[0], dtype=jnp.int32)
    scores = jnp.dot(flat_query, key_rows.T, preferred_element_type=jnp.float32) * score_scale
    scores = jnp.where(key_pos[None, :] <= query_pos[:, None], scores, -jnp.inf)
    row_max = jnp.max(scores, axis=1, keepdims=True)
    weights = jnp.exp(scores - row_max)
    probability = weights / jnp.sum(weights, axis=1, keepdims=True)
    prob_bf = probability.astype(jnp.bfloat16)
    head_out = jnp.dot(prob_bf, value_rows, preferred_element_type=jnp.float32)
    gated_out = (gate_rows.reshape(-1, 1) * head_out).astype(jnp.bfloat16)
    grad_bf = head_grad.astype(jnp.bfloat16)
    value_sum = jnp.dot(prob_bf.T, grad_bf, preferred_element_type=jnp.float32)
    prob_grad = jnp.dot(grad_bf, value_rows.T, preferred_element_type=jnp.float32)
    row_delta = jnp.sum(head_grad * head_out, axis=1, keepdims=True)
    score_grad = (probability * (prob_grad - row_delta)).astype(jnp.bfloat16)
    query_grad = (
        jnp.dot(score_grad, key_rows, preferred_element_type=jnp.float32) * score_scale
    ).astype(jnp.bfloat16)
    key_sum = jnp.dot(score_grad.T, flat_query, preferred_element_type=jnp.float32) * score_scale
    return (query_grad, gated_out, key_sum, value_sum)


def per_device(
    hidden,
    out_grad,
    queries,
    key_heads,
    value_heads,
    routes,
    route_gates,
    w_query,
    w_out,
    w_key,
    w_value,
):
    n_blocks = lax.axis_size("seq")
    n_groups = lax.axis_size("node") * lax.axis_size("dev")
    local_experts = w_query.shape[0]
    seq_len = hidden.shape[1]
    slab_width = hidden.shape[2]
    block_len = seq_len // n_blocks
    seq_index = lax.axis_index("seq")
    key_all, value_all = (
        lax.all_gather(key_heads[0], "seq", axis=0, tiled=True),
        lax.all_gather(value_heads[0], "seq", axis=0, tiled=True),
    )
    hot_expert, hot_slot = block_onehots(routes[0], block_len)
    dispatch = jnp.einsum(
        "bpje,bpjc->becp", hot_expert, hot_slot, preferred_element_type=jnp.float32
    ).astype(jnp.bfloat16)

    def pack_rows(token_rows):
        blocked = token_rows.reshape(n_blocks, block_len, slab_width)
        packed = jnp.einsum(
            "becp,bpd->becd", dispatch, blocked, preferred_element_type=jnp.float32
        ).astype(jnp.bfloat16)
        return packed.reshape(n_blocks, n_groups, local_experts, CAP, slab_width)

    hid_packed = pack_rows(hidden[0])
    grad_packed = pack_rows(out_grad[0])
    hid_buf, grad_buf = (
        lax.all_to_all(hid_packed, ("node", "dev"), split_axis=1, concat_axis=1, tiled=True),
        lax.all_to_all(grad_packed, ("node", "dev"), split_axis=1, concat_axis=1, tiled=True),
    )
    head_part = lax.psum_scatter(
        jnp.einsum("bgkcd,khd->bgkch", grad_buf, w_out, preferred_element_type=jnp.float32),
        "seq",
        scatter_dimension=0,
        tiled=True,
    )
    head_home = lax.all_to_all(head_part, ("node", "dev"), split_axis=1, concat_axis=1, tiled=True)
    head_flat = head_home.reshape(EXPERTS * CAP, HD)
    own_expert = lax.dynamic_index_in_dim(hot_expert, seq_index, 0, keepdims=False)
    own_slot = lax.dynamic_index_in_dim(hot_slot, seq_index, 0, keepdims=False)
    selector = (own_expert[:, :, :, None] * own_slot[:, :, None, :]).reshape(
        block_len * TOP, EXPERTS * CAP
    )
    head_route = jnp.dot(selector.astype(jnp.float32), head_flat, precision=lax.Precision.HIGHEST)
    head_grad = route_gates[0].reshape(block_len * TOP, 1) * head_route
    query_grad, gated_out, key_sum, value_sum = attend(
        queries[0], key_all, value_all, head_grad, route_gates[0], seq_index * block_len
    )

    def to_slots(route_rows):
        slotted = jnp.dot(selector.T, route_rows, preferred_element_type=jnp.float32).astype(
            jnp.bfloat16
        )
        return slotted.reshape(1, n_groups, local_experts, CAP, HD)

    dq_slots = to_slots(query_grad)
    gated_slots = to_slots(gated_out)
    dq_mine, gated_mine = (
        lax.all_to_all(dq_slots, ("node", "dev"), split_axis=1, concat_axis=1, tiled=True),
        lax.all_to_all(gated_slots, ("node", "dev"), split_axis=1, concat_axis=1, tiled=True),
    )
    dq_buf, gated_buf = (
        lax.all_gather(dq_mine, "seq", axis=0, tiled=True),
        lax.all_gather(gated_mine, "seq", axis=0, tiled=True),
    )
    grad_wq = jnp.einsum("bgkcd,bgkch->kdh", hid_buf, dq_buf, preferred_element_type=jnp.float32)
    grad_wo = jnp.einsum(
        "bgkch,bgkcd->khd", gated_buf, grad_buf, preferred_element_type=jnp.float32
    )
    route_back = jnp.einsum(
        "bgkch,kdh->bgkcd", dq_buf, w_query, preferred_element_type=jnp.float32
    ).astype(jnp.bfloat16)
    back_home = lax.all_to_all(
        route_back, ("node", "dev"), split_axis=1, concat_axis=1, tiled=True
    ).reshape(n_blocks, EXPERTS, CAP, slab_width)
    token_total = jnp.einsum(
        "becp,becd->bpd", dispatch, back_home, preferred_element_type=jnp.float32
    ).reshape(seq_len, slab_width)
    key_own, value_own = (
        lax.psum_scatter(key_sum, "seq", scatter_dimension=0, tiled=True),
        lax.psum_scatter(value_sum, "seq", scatter_dimension=0, tiled=True),
    )
    shared_key_gradient, shared_value_gradient = (
        lax.all_gather(key_own.astype(jnp.bfloat16), "seq", axis=0, tiled=True),
        lax.all_gather(value_own.astype(jnp.bfloat16), "seq", axis=0, tiled=True),
    )
    token_total = token_total + jnp.dot(
        shared_key_gradient, w_key.T, preferred_element_type=jnp.float32
    )
    token_total = token_total + jnp.dot(
        shared_value_gradient, w_value.T, preferred_element_type=jnp.float32
    )
    grad_hidden = token_total.astype(jnp.bfloat16).reshape(1, seq_len, slab_width)
    key_part = jnp.einsum(
        "ld,lh->dh", hidden[0], shared_key_gradient, preferred_element_type=jnp.float32
    )
    value_part = jnp.einsum(
        "ld,lh->dh", hidden[0], shared_value_gradient, preferred_element_type=jnp.float32
    )
    key_projection_gradient, value_projection_gradient = (
        lax.psum(key_part.astype(jnp.bfloat16), ("node", "dev")).astype(jnp.float32),
        lax.psum(value_part.astype(jnp.bfloat16), ("node", "dev")).astype(jnp.float32),
    )
    return (grad_hidden, grad_wq, grad_wo, key_projection_gradient, value_projection_gradient)


def solution(mesh):
    in_specs = (
        P(("node", "dev"), None, "seq"),
        P(("node", "dev"), None, "seq"),
        P(("node", "dev"), "seq", None, None),
        P(("node", "dev"), "seq", None),
        P(("node", "dev"), "seq", None),
        P(("node", "dev"), None, None),
        P(("node", "dev"), "seq", None),
        P(("node", "dev"), "seq", None),
        P(("node", "dev"), None, "seq"),
        P("seq", None),
        P("seq", None),
    )
    out_specs = (
        P(("node", "dev"), None, "seq"),
        P(("node", "dev"), "seq", None),
        P(("node", "dev"), None, "seq"),
        P("seq", None),
        P("seq", None),
    )
    return jax.shard_map(
        per_device, mesh=mesh, in_specs=in_specs, out_specs=out_specs, check_vma=False
    )
```

profile of v0, /device:TPU:1, one launch (start us, length us, event | category | flops | bytes accessed | tf_op | source)
XLA Modules:
  0.0 1245.8 jit_solution(180413284017236127)
XLA Ops:
  7.2 1.5 copy.74
  8.7 1.2 eq.55
  9.9 1.2 eq.51
  11.2 1.3 fusion.6
  12.5 2.5 broadcast_add_fusion
  15.1 4.7 bitcast_subtract_fusion
  19.8 6.6 select_reduce_fusion
  26.4 3.0 copy.78
  29.4 22.7 %fusion.8 = bf16[32,128,3,128]{1,2,3,0:T(4,128)(2,1)S(1)} fusion(s32[32,128,2]{2,1,0:T(8,128)S(1)} %bitcast.111, s32[32,128,2]{2,1,0:T(8,128)} %copy.78), kind=kOutput, calls=%fused_computation.23 | convolution fusion | flops 11034624 | bytes 3211264 | tf_op jit(solution)/shard_map/bpje,bpjc->becp/dot_general | solution.py:80
  52.2 1.0 convolution_convert_fusion.2
  53.2 1.0 copy-done.1
  54.2 2.2 copy.82
  56.4 7.6 all-to-all-start
  64.0 0.7 all-gather.17.cloned.1.call-update
  64.7 36.9 %all-to-all-done = bf16[32,8,16,3,128]{4,2,3,0,1:T(8,128)(2,1)} async-done(((bf16[32,8,16,3,128]{4,2,3,0,1:T(8,128)(2,1)}), bf16[32,8,16,3,128]{4,2,3,0,1:T(8,128)(2,1)}, u32[]{:S(2)}, u32[]{:S(2)}) %all-to-all-start) | async-done | bytes 3145760 | tf_op jit(solution)/shard_map/all_to_all | solution.py:95
  101.7 6.5 fusion.18
  108.9 7.4 iota_compare_fusion.1
  116.3 6.3 fusion.5
  122.7 0.9 fusion.50
  123.6 0.9 dynamic-slice_bitcast_fusion
  124.5 7.1 broadcast_multiply_fusion
  131.6 10.7 mul.80
  143.2 2.2 fusion.59
  145.3 0.7 fusion.10
  146.0 2.6 fusion.9
  148.7 180.8 %all-reduce.5.cloned.1.call-done = f32[32,8,16,3,128]{4,1,3,0,2:T(8,128)} async-done(((f32[32,8,16,3,128]{4,1,3,0,2:T(8,128)}), f32[32,8,16,3,128]{4,1,3,0,2:T(8,128)}) %all-reduce.5.cloned.1.call-update) | async-done | bytes 6291472
  329.5 1.6 constant_dynamic-slice_fusion
  331.1 0.7 copy.84
  331.8 5.2 all-to-all-start.1
  337.0 66.1 %all-gather.19.cloned.1.call-done = bf16[1,4096,128]{2,1,0:T(8,128)(2,1)} async-done(((bf16[1,128,128]{2,1,0:T(8,128)(2,1)}), bf16[1,4096,128]{2,1,0:T(8,128)(2,1)}) %all-gather.19.cloned.1.call-update) | async-done | bytes 1048592 | tf_op jit(solution)/shard_map/all_gather | solution.py:77
  403.1 3.3 fusion.39
  407.0 3.4 fusion.2
  410.4 2.1 convolution_multiply_fusion.1
  412.6 4.3 fusion.45
  416.9 2.8 convolution_convert_fusion.4
  419.7 0.9 reshape.93
  420.7 14.1 %all_to_all.30 = bf16[1,8,16,3,128]{4,2,3,0,1:T(8,128)(2,1)S(1)} all-to-all(bf16[1,8,16,3,128]{4,2,3,0,1:T(8,128)(2,1)S(1)} %copy.86), channel_id=1, replica_groups=mesh['seq'=32,'node'=4,'dev'=2] {'node','dev'}, dimensions={1} | all-to-all | bytes 196608 | tf_op jit(solution)/shard_map/all_to_all | solution.py:125
  434.8 0.7 copy.87
  435.9 9.0 all_to_all.31
  444.9 3.2 convolution_convert_fusion.1
  448.2 3.7 copy.92
  451.8 5.2 all-to-all-start.4
  457.1 168.8 %reduce-scatter.4.cloned.1.call-done = f32[128,128]{1,0:T(8,128)} async-done(((f32[4096,128]{1,0:T(8,128)}), f32[128,128]{1,0:T(8,128)}) %reduce-scatter.4.cloned.1.call-update) | async-done | bytes 65552 | tf_op jit(solution)/shard_map/reduce_scatter | solution.py:146
  625.9 1.5 convert_element_type.100
  627.4 216.8 %reduce-scatter.6.cloned.1.call-done = f32[128,128]{1,0:T(8,128)} async-done(((f32[4096,128]{1,0:T(8,128)}), f32[128,128]{1,0:T(8,128)}) %reduce-scatter.6.cloned.1.call-update) | async-done | bytes 65552 | tf_op jit(solution)/shard_map/reduce_scatter | solution.py:147
  844.2 1.5 convert_element_type.101
  845.7 81.4 %all-gather.9.cloned.1.call-done = bf16[32,8,16,3,128]{4,1,3,0,2:T(8,128)(2,1)} async-done(((bf16[1,8,16,3,128]{4,1,3,0,2:T(8,128)(2,1)}), bf16[32,8,16,3,128]{4,1,3,0,2:T(8,128)(2,1)}) %all-gather.9.cloned.1.call-update) | async-done | bytes 3145744 | tf_op jit(solution)/shard_map/all_gather | solution.py:129
  927.0 2.9 convert_bitcast_fusion
  929.9 3.7 copy.88
  933.6 7.4 all-to-all-start.3
  941.3 67.5 %all-gather.15.cloned.1.call-done = bf16[32,8,16,3,128]{4,2,3,1,0:T(8,128)(2,1)} async-done(((bf16[1,8,16,3,128]{4,2,3,1,0:T(8,128)(2,1)}), bf16[32,8,16,3,128]{4,2,3,1,0:T(8,128)(2,1)}) %all-gather.15.cloned.1.call-update) | async-done | bytes 3145744 | tf_op jit(solution)/shard_map/all_gather | solution.py:130
  1008.8 9.0 fusion.25
  1017.8 66.8 %all-gather.11.cloned.1.call-done = bf16[4096,128]{1,0:T(8,128)(2,1)} async-done(((bf16[128,128]{1,0:T(8,128)(2,1)}), bf16[4096,128]{1,0:T(8,128)(2,1)}) %all-gather.11.cloned.1.call-update) | async-done | bytes 1048592 | tf_op jit(solution)/shard_map/all_gather | solution.py:150
  1084.7 2.3 fusion.35
  1087.0 75.0 %all-gather.13.cloned.1.call-done = bf16[4096,128]{1,0:T(8,128)(2,1)} async-done(((bf16[128,128]{1,0:T(8,128)(2,1)}), bf16[4096,128]{1,0:T(8,128)(2,1)}) %all-gather.13.cloned.1.call-update) | async-done | bytes 1048592 | tf_op jit(solution)/shard_map/all_gather | solution.py:151
  1162.0 2.3 fusion.36
  1164.3 5.1 fusion.22
  1169.4 59.5 %all-reduce.7.cloned.1.call-done = (bf16[128,128]{0,1:T(8,128)(2,1)}, bf16[128,128]{0,1:T(8,128)(2,1)}) async-done(((bf16[128,128]{0,1:T(8,128)(2,1)}, bf16[128,128]{0,1:T(8,128)(2,1)}), (bf16[128,128]{0,1:T(8,128)(2,1)}, bf16[128,128]{0,1:T(8,128)(2,1)})) %all-reduce.7.cloned.1.call-update) | async-done | bytes 65552 | tf_op jit(solution)/shard_map/psum | solution.py:167
  1228.9 1.5 copy.98
  1230.4 1.5 copy.99
  1231.9 3.0 copy.89
  1235.0 1.0 fusion.32
  1236.7 0.6 copy-done.4
  1237.3 1.4 fusion.4
  (63 shorter events, 4.1 us)
Async XLA Ops:
  7.2 437.7 %copy-start = (bf16[1,4096,128]{2,1,0:T(8,128)(2,1)S(1)}, bf16[1,4096,128]{2,1,0:T(8,128)(2,1)}, u32[]{:S(2)}) copy-start(bf16[1,4096,128]{2,1,0:T(8,128)(2,1)} %param.11) | copy-start | bytes 3145732
  29.4 22.7 %copy-start.5 = (bf16[1,4096,128]{2,1,0:T(8,128)(2,1)S(1)}, bf16[1,4096,128]{2,1,0:T(8,128)(2,1)}, u32[]{:S(2)}) copy-start(bf16[1,4096,128]{2,1,0:T(8,128)(2,1)} %param.12) | copy-start | bytes 3145732
  52.1 2.0 copy-start.1
  56.4 45.3 %all-to-all-start = ((bf16[32,8,16,3,128]{4,2,3,0,1:T(8,128)(2,1)}), bf16[32,8,16,3,128]{4,2,3,0,1:T(8,128)(2,1)}, u32[]{:S(2)}, u32[]{:S(2)}) async-start(bf16[32,8,16,3,128]{4,2,3,0,1:T(8,128)(2,1)} %copy.82), calls=%async_computation | async-start | bytes 6291456 | tf_op jit(solution)/shard_map/all_to_all | solution.py:95
  64.0 79.2 %all-gather.17.cloned.1.call-start = ((), (), s32[]{:S(2)}) async-start(), calls=%async_computation.14 | async-start | bytes 1081344 | tf_op jit(solution)/shard_map/all_gather | solution.py:76
  64.7 264.8 %all-reduce.5.cloned.1.call-start = ((), (), s32[]{:S(2)}) async-start(), calls=%async_computation.16 | async-start | bytes 12582912
  108.2 294.9 %all-gather.19.cloned.1.call-start = ((), (), s32[]{:S(2)}) async-start(), calls=%async_computation.15 | async-start | bytes 1081344 | tf_op jit(solution)/shard_map/all_gather | solution.py:77
  131.6 10.7 copy-start.11
  131.6 11.0 copy-start.12
  131.6 11.6 copy-start.7
  331.8 74.6 %all-to-all-start.1 = ((f32[1,8,16,3,128]{4,2,3,0,1:T(8,128)}), f32[1,8,16,3,128]{4,2,3,0,1:T(8,128)S(1)}, u32[]{:S(2)}, u32[]{:S(2)}) async-start(f32[1,8,16,3,128]{4,2,3,0,1:T(8,128)} %copy.84), calls=%async_computation.1 | async-start | bytes 393216 | tf_op jit(solution)/shard_map/all_to_all | solution.py:103
  337.0 288.9 %reduce-scatter.4.cloned.1.call-start = ((), (), s32[]{:S(2)}) async-start(), calls=%async_computation.9 | async-start | bytes 2162688 | tf_op jit(solution)/shard_map/reduce_scatter | solution.py:146
  407.0 3.4 copy-start.8
  412.5 431.7 %reduce-scatter.6.cloned.1.call-start = ((), (), s32[]{:S(2)}) async-start(), calls=%async_computation.11 | async-start | bytes 2162688 | tf_op jit(solution)/shard_map/reduce_scatter | solution.py:147
  416.9 510.2 %all-gather.9.cloned.1.call-start = ((), (), s32[]{:S(2)}) async-start(), calls=%async_computation.8 | async-start | bytes 3244032 | tf_op jit(solution)/shard_map/all_gather | solution.py:129
  435.5 573.3 %all-gather.15.cloned.1.call-start = ((), (), s32[]{:S(2)}) async-start(), calls=%async_computation.13 | async-start | bytes 3244032 | tf_op jit(solution)/shard_map/all_gather | solution.py:130
  451.8 475.2 %copy-start.6 = (bf16[16,128,128]{2,1,0:T(8,128)(2,1)S(1)}, bf16[16,128,128]{2,1,0:T(8,128)(2,1)}, u32[]{:S(2)}) copy-start(bf16[16,128,128]{2,1,0:T(8,128)(2,1)} %param.18) | copy-start | bytes 1572868
  451.8 481.8 %all-to-all-start.4 = ((bf16[32,8,16,3,128]{4,0,3,2,1:T(8,128)(2,1)}), bf16[32,8,16,3,128]{4,0,3,2,1:T(8,128)(2,1)}, u32[]{:S(2)}, u32[]{:S(2)}) async-start(bf16[32,8,16,3,128]{4,0,3,2,1:T(8,128)(2,1)} %copy.92), calls=%async_computation.6 | async-start | bytes 6291456 | tf_op jit(solution)/shard_map/all_to_all | solution.py:94
  457.1 627.6 %all-gather.11.cloned.1.call-start = ((), (), s32[]{:S(2)}) async-start(), calls=%async_computation.10 | async-start | bytes 1081344 | tf_op jit(solution)/shard_map/all_gather | solution.py:150
  627.4 534.6 %all-gather.13.cloned.1.call-start = ((), (), s32[]{:S(2)}) async-start(), calls=%async_computation.12 | async-start | bytes 1081344 | tf_op jit(solution)/shard_map/all_gather | solution.py:151
  933.6 298.3 %all-to-all-start.3 = ((bf16[32,8,16,3,128]{4,2,3,0,1:T(8,128)(2,1)}), bf16[32,8,16,3,128]{4,2,3,0,1:T(8,128)(2,1)}, u32[]{:S(2)}, u32[]{:S(2)}) async-start(bf16[32,8,16,3,128]{4,2,3,0,1:T(8,128)(2,1)} %copy.88), calls=%async_computation.3 | async-start | bytes 6291456 | tf_op jit(solution)/shard_map/all_to_all | solution.py:139
  941.1 287.8 %all-reduce.7.cloned.1.call-start = ((), (), s32[]{:S(2)}) async-start(), calls=%async_computation.17 | async-start | bytes 131072 | tf_op jit(solution)/shard_map/psum | solution.py:167
  1231.9 3.1 copy-start.2
  1235.0 1.2 copy-start.3
  1235.0 1.2 copy-start.9
  1236.0 1.3 copy-start.4
  1236.0 1.3 copy-start.10
Sparse Core Ops, SparseCore 0:
  67.4 72.7 all-gather.16
  143.7 185.7 all-reduce.4
  332.4 70.6 all-gather.18
  412.6 213.2 reduce-scatter.3
  629.6 214.5 reduce-scatter.5
  847.5 79.5 all-gather.8
  929.9 78.8 all-gather.14
  1012.3 72.3 all-gather.10
  1088.2 73.7 all-gather.12
  1164.9 63.9 all-reduce.6
where the time goes:
time: 1260 us; the launch traced here: 1250 us
  waiting for transfers between devices  1020 us (81%)
  matrix products  76.6 us (6%)
  other arithmetic  43.1 us (3%)
  local copies, waits for them, and re-layouts  41.2 us (3%)
  starting transfers between devices  26.4 us (2%)
  blocking collectives  23.1 us (2%)
  between operations  14.7 us (1%)
    reduce_scatter x1, waiting for transfers between devices, per_device(): lax.psum_scatter(value_sum, 'seq', scatter_dimension=0, tiled=True)  217 us
    unnamed x11, waiting for transfers between devices  182 us
    reduce_scatter x1, waiting for transfers between devices, per_device(): lax.psum_scatter(key_sum, 'seq', scatter_dimension=0, tiled=True)  169 us
    all_gather x1, waiting for transfers between devices, per_device(): lax.all_gather(dq_mine, 'seq', axis=0, tiled=True)  81.4 us
    all_gather x1, waiting for transfers between devices, per_device(): lax.all_gather(value_own.astype(jnp.bfloat16), 'seq', axis=0, tiled=True)  75 us
    all_gather x1, waiting for transfers between devices, per_device(): lax.all_gather(gated_mine, 'seq', axis=0, tiled=True)  67.5 us
    all_gather x1, waiting for transfers between devices, per_device(): lax.all_gather(key_own.astype(jnp.bfloat16), 'seq', axis=0, tiled=True)  66.8 us
    all_gather x1, waiting for transfers between devices, per_device(): lax.all_gather(value_heads[0], 'seq', axis=0, tiled=True)  66.1 us
  transfers between devices with their start and end apart: 14, of which 10 were waited for; matrix products, arithmetic and copies ran while one was open for 8% of the time, Pallas kernels for 0%

commit v1 on v0

v1 whole, which is shorter than its diff:
```python
import math

import jax
import jax.numpy as jnp
import numpy as np
from jax import lax
from jax.experimental import pallas as pl
from jax.experimental.pallas import tpu as pltpu
from jax.sharding import Mesh
from jax.sharding import PartitionSpec as P

HD = 128
EXPERTS = 128
TOP = 2
CAP = 3
BLOCK = 128
EPD = 2
ROWS = EPD * CAP
PAD = 8
SEQ = ("x", "zh", "zl")
GRP = ("node", "dev")
SLAB = ("x", "zl")
WIDE = ("x", "zl", "node", "dev")
F32 = jnp.float32
BF16 = jnp.bfloat16
VMEM_LIMIT = 56 * 1024 * 1024


def swap_matrix():
    out = np.arange(8 * 8 * ROWS)
    a, b, q = out // (8 * ROWS), out // ROWS % 8, out % ROWS
    m = np.zeros((8 * 8 * ROWS, 8 * 8 * ROWS), np.float32)
    m[out, b * 8 * ROWS + a * ROWS + q] = 1
    return m


def pad_matrix():
    src = np.arange(8 * 8 * ROWS)
    a, b, q = src // (8 * ROWS), src // ROWS % 8, src % ROWS
    m = np.zeros((8 * 8 * PAD, 8 * 8 * ROWS), np.float32)
    m[b * 8 * PAD + a * PAD + q, src] = 1
    return m


def params(n):
    return pltpu.CompilerParams(dimension_semantics=("arbitrary",) * n, vmem_limit_bytes=VMEM_LIMIT)


def dot_nt(a, b):
    return lax.dot_general(a, b, (((1,), (1,)), ((), ())), preferred_element_type=F32)


def dot_tn(a, b):
    return lax.dot_general(a, b, (((0,), (0,)), ((), ())), preferred_element_type=F32)


def dot_nn(a, b):
    return jnp.dot(a, b, preferred_element_type=F32)


def pack_kernel(routes_ref, hid_ref, grad_ref, swap_ref, hid_out, grad_out, rho_out, stage):
    expert = lax.broadcasted_iota(jnp.int32, (EXPERTS, BLOCK), 0)
    before = (
        lax.broadcasted_iota(jnp.int32, (BLOCK, BLOCK), 0)
        < lax.broadcasted_iota(jnp.int32, (BLOCK, BLOCK), 1)
    ).astype(F32).astype(BF16)
    row_id = lax.broadcasted_iota(jnp.int32, (64 * ROWS, BLOCK), 0)
    for j in range(8):
        x, span = j // 2, pl.ds((j % 2) * BLOCK, BLOCK)
        first = routes_ref[x, 0, 0:1, span]
        second = routes_ref[x, 0, 1:2, span]
        hot_a = (expert == first).astype(F32)
        hot_b = (expert == second).astype(F32)
        earlier = dot_nn((hot_a + hot_b).astype(BF16), before)
        slot_a = jnp.sum(hot_a * earlier, axis=0, keepdims=True).astype(jnp.int32)
        slot_b = jnp.sum(hot_b * earlier, axis=0, keepdims=True).astype(jnp.int32)

        def row_of(e, slot):
            return (((e >> 1) & 7) * 8 + (e >> 4)) * ROWS + (e & 1) * CAP + slot

        rho_a, rho_b = row_of(first, slot_a), row_of(second, slot_b)
        rho_out[x, 0, 0:1, span] = rho_a
        rho_out[x, 0, 1:2, span] = rho_b
        pick = ((row_id == rho_a) | (row_id == rho_b)).astype(F32).astype(BF16)
        both = jnp.concatenate([hid_ref[x, 0, span, :], grad_ref[x, 0, span, :]], axis=1)
        picked = dot_nn(pick, both).astype(BF16)
        for d in range(8):
            stage[d, j * 8 * ROWS : (j + 1) * 8 * ROWS, :] = picked[d * 8 * ROWS : (d + 1) * 8 * ROWS]
    for d in range(8):
        turned = dot_nn(swap_ref[...], stage[d]).astype(BF16).reshape(8, 8 * ROWS, 2 * HD)
        hid_out[d * 8 : (d + 1) * 8, 0] = turned[:, :, :HD]
        grad_out[d * 8 : (d + 1) * 8, 0] = turned[:, :, HD:]


def pack(routes_t, hid, grad, swap):
    slab = pl.BlockSpec((4, 1, 2 * BLOCK, HD), lambda t: (0, t, 0, 0))
    rows = pl.BlockSpec((64, 1, 8 * ROWS, HD), lambda t: (0, t, 0, 0))
    ids = pl.BlockSpec((4, 1, TOP, 2 * BLOCK), lambda t: (0, t, 0, 0))
    return pl.pallas_call(
        pack_kernel,
        grid=(4,),
        in_specs=[ids, slab, slab, pl.BlockSpec(swap.shape, lambda t: (0, 0))],
        out_specs=[rows, rows, ids],
        out_shape=[
            jax.ShapeDtypeStruct((64, 4, 8 * ROWS, HD), BF16),
            jax.ShapeDtypeStruct((64, 4, 8 * ROWS, HD), BF16),
            jax.ShapeDtypeStruct((4, 4, TOP, 2 * BLOCK), jnp.int32),
        ],
        scratch_shapes=[pltpu.VMEM((8, 64 * ROWS, 2 * HD), BF16)],
        compiler_params=params(1),
        name="pack_rows",
    )(routes_t, hid, grad, swap)


def second_expert(shape):
    return lax.rem(lax.broadcasted_iota(jnp.int32, shape, 0), ROWS) >= CAP


def head_kernel(grad_ref, w_ref, out_ref):
    for g in range(2):
        total = dot_nt(grad_ref[0, g], w_ref[0])
        for r in range(1, 8):
            total += dot_nt(grad_ref[r, g], w_ref[r])
        own = jnp.where(second_expert((32 * ROWS, HD)), total[:, HD:], total[:, :HD])
        out_ref[:, g] = own.astype(BF16).reshape(4, 8 * ROWS, HD)


def head_sums(grad_rows, w_out_r):
    return pl.pallas_call(
        head_kernel,
        grid=(4,),
        in_specs=[
            pl.BlockSpec((8, 2, 32 * ROWS, HD), lambda i: (0, i, 0, 0)),
            pl.BlockSpec((8, 2 * HD, HD), lambda i: (0, 0, 0)),
        ],
        out_specs=pl.BlockSpec((4, 2, 8 * ROWS, HD), lambda i: (0, i, 0, 0)),
        out_shape=jax.ShapeDtypeStruct((4, 8, 8 * ROWS, HD), BF16),
        compiler_params=params(1),
        name="head_sums",
    )(grad_rows.reshape(8, 8, 32 * ROWS, HD), w_out_r)


def reduce_kernel(parts_ref, pad_ref, out_ref):
    total = parts_ref[0].astype(F32)
    for s in range(1, 4):
        total += parts_ref[s].astype(F32)
    out_ref[...] = dot_nn(pad_ref[...], total.astype(BF16)).astype(BF16)


def reduce_heads(parts, pad):
    return pl.pallas_call(
        reduce_kernel,
        out_shape=jax.ShapeDtypeStruct((64 * PAD, HD), BF16),
        compiler_params=params(0),
        name="reduce_heads",
    )(parts.reshape(4, 64 * ROWS, HD), pad)


def forward_kernel(start_ref, q_ref, kv_ref, gate_ref, prob_out, head_out, gated_out, score):
    n, length = q_ref.shape[0], kv_ref.shape[0]
    step = 512
    q = q_ref[...]
    pos = start_ref[0] + lax.rem(lax.broadcasted_iota(jnp.int32, (n, step), 0), BLOCK)
    lane = lax.broadcasted_iota(jnp.int32, (n, step), 1)
    top = jnp.full((n, 1), -jnp.inf, F32)
    for c in range(0, length, step):
        s = dot_nt(q, kv_ref[c : c + step, :HD]) * (1.0 / math.sqrt(HD))
        s = jnp.where(lane + c <= pos, s, -jnp.inf)
        score[:, c : c + step] = s
        top = jnp.maximum(top, jnp.max(s, axis=1, keepdims=True))
    total = jnp.zeros((n, 1), F32)
    for c in range(0, length, step):
        w = jnp.exp(score[:, c : c + step] - top)
        score[:, c : c + step] = w
        total += jnp.sum(w, axis=1, keepdims=True)
    inv = 1.0 / total
    out = jnp.zeros((n, HD), F32)
    for c in range(0, length, step):
        p = (score[:, c : c + step] * inv).astype(BF16)
        prob_out[:, c : c + step] = p
        out += dot_nn(p, kv_ref[c : c + step, HD:])
    head_out[...] = out
    gated_out[...] = (gate_ref[...] * out).astype(BF16)


def attend_forward(start, q, kv, gates):
    n, length = q.shape[0], kv.shape[0]
    vm = pl.BlockSpec(memory_space=pltpu.VMEM)
    return pl.pallas_call(
        forward_kernel,
        in_specs=[pl.BlockSpec(memory_space=pltpu.SMEM), vm, vm, vm],
        out_specs=[vm, vm, vm],
        out_shape=[
            jax.ShapeDtypeStruct((n, length), BF16),
            jax.ShapeDtypeStruct((n, HD), F32),
            jax.ShapeDtypeStruct((n, HD), BF16),
        ],
        scratch_shapes=[pltpu.VMEM((n, length), F32)],
        compiler_params=params(0),
        name="attend_forward",
    )(start, q, kv, gates)


def backward_kernel(
    head_ref, rho_row_ref, rho_col_ref, gate_ref, q_ref, kv_ref, prob_ref, out_ref, gated_ref, slots_out, dkv_out
):
    n, length = q_ref.shape[0], kv_ref.shape[0]
    step = 512
    scale = 1.0 / math.sqrt(HD)
    lanes = lax.broadcasted_iota(jnp.int32, (n, 64 * PAD), 1)
    pick = (lanes == rho_col_ref[...]).astype(F32).astype(BF16)
    head_grad = gate_ref[...] * dot_nn(pick, head_ref[...])
    delta = jnp.sum(head_grad * out_ref[...], axis=1, keepdims=True)
    grad = head_grad.astype(BF16)
    q = q_ref[...]
    dq = jnp.zeros((n, HD), F32)
    for c in range(0, length, step):
        keys, values = kv_ref[c : c + step, :HD], kv_ref[c : c + step, HD:]
        p = prob_ref[:, c : c + step]
        ds = (p.astype(F32) * (dot_nt(grad, values) - delta)).astype(BF16)
        dq += dot_nn(ds, keys)
        dkv_out[c : c + step, :HD] = (dot_tn(ds, q) * scale).astype(BF16)
        dkv_out[c : c + step, HD:] = dot_tn(p, grad).astype(BF16)
    both = jnp.concatenate([(dq * scale).astype(BF16), gated_ref[...]], axis=1)
    rows = lax.broadcasted_iota(jnp.int32, (64 * PAD, n), 0)
    place = (rows == rho_row_ref[...]).astype(F32).astype(BF16)
    slots_out[...] = dot_nn(place, both).astype(BF16)


def attend_backward(head, rho_row, rho_col, gates, q, kv, prob, out, gated):
    return pl.pallas_call(
        backward_kernel,
        out_shape=[
            jax.ShapeDtypeStruct((64 * PAD, 2 * HD), BF16),
            jax.ShapeDtypeStruct(kv.shape, BF16),
        ],
        compiler_params=params(0),
        name="attend_backward",
    )(head, rho_row, rho_col, gates, q, kv, prob, out, gated)


def unpad_kernel(rows_ref, unpad_ref, out_ref):
    out_ref[...] = dot_nn(unpad_ref[...], rows_ref[...]).astype(BF16)


def unpad_rows(rows, unpad):
    return pl.pallas_call(
        unpad_kernel,
        out_shape=jax.ShapeDtypeStruct((64 * ROWS, 2 * HD), BF16),
        compiler_params=params(0),
        name="unpad_rows",
    )(rows, unpad)


def by_expert(rows):
    later = second_expert(rows.shape)
    zero = jnp.zeros_like(rows)
    return jnp.concatenate([jnp.where(later, zero, rows), jnp.where(later, rows, zero)], axis=1)


def back_kernel(dqg_ref, w_ref, out_ref):
    for g in range(2):
        dq = by_expert(dqg_ref[:, g, :, :HD].reshape(32 * ROWS, HD))
        for r in range(8):
            out_ref[r, g] = dot_nn(dq, w_ref[r]).astype(BF16)


def route_back(dqg, w_query_r):
    return pl.pallas_call(
        back_kernel,
        grid=(4,),
        in_specs=[
            pl.BlockSpec((4, 2, 8 * ROWS, 2 * HD), lambda i: (0, i, 0, 0)),
            pl.BlockSpec((8, 2 * HD, HD), lambda i: (0, 0, 0)),
        ],
        out_specs=pl.BlockSpec((8, 2, 32 * ROWS, HD), lambda i: (0, i, 0, 0)),
        out_shape=jax.ShapeDtypeStruct((8, 8, 32 * ROWS, HD), BF16),
        compiler_params=params(1),
        name="route_back",
    )(dqg, w_query_r)


def weights_kernel(dqg_ref, hid_ref, grad_ref, wq_out, wo_out, wq_acc, wo_acc):
    @pl.when(pl.program_id(0) == 0)
    def _():
        wq_acc[...] = jnp.zeros_like(wq_acc)
        wo_acc[...] = jnp.zeros_like(wo_acc)

    for g in range(2):
        dq = by_expert(dqg_ref[:, g, :, :HD].reshape(32 * ROWS, HD))
        gated = by_expert(dqg_ref[:, g, :, HD:].reshape(32 * ROWS, HD))
        for r in range(8):
            wq_acc[r] += dot_tn(hid_ref[r, g], dq)
            wo_acc[r] += dot_tn(gated, grad_ref[r, g])

    @pl.when(pl.program_id(0) == 3)
    def _():
        for r in range(8):
            for k in range(EPD):
                wq_out[r, k] = wq_acc[r, :, k * HD : (k + 1) * HD].astype(BF16)
                wo_out[r, k] = wo_acc[r, k * HD : (k + 1) * HD, :].astype(BF16)


def weight_grads(dqg, hid_rows, grad_rows):
    rows = pl.BlockSpec((8, 2, 32 * ROWS, HD), lambda i: (0, i, 0, 0))
    whole = pl.BlockSpec((8, EPD, HD, HD), lambda i: (0, 0, 0, 0))
    return pl.pallas_call(
        weights_kernel,
        grid=(4,),
        in_specs=[pl.BlockSpec((4, 2, 8 * ROWS, 2 * HD), lambda i: (0, i, 0, 0)), rows, rows],
        out_specs=[whole, whole],
        out_shape=[jax.ShapeDtypeStruct((8, EPD, HD, HD), BF16)] * 2,
        scratch_shapes=[pltpu.VMEM((8, HD, EPD * HD), F32), pltpu.VMEM((8, EPD * HD, HD), F32)],
        compiler_params=params(1),
        name="weight_grads",
    )(dqg, hid_rows.reshape(8, 8, 32 * ROWS, HD), grad_rows.reshape(8, 8, 32 * ROWS, HD))


def combine_kernel(rho_ref, back_ref, swap_ref, dkv_ref, wkv_ref, out_ref, stage):
    for d in range(8):
        rows = back_ref[d * 8 : (d + 1) * 8, 0].reshape(64 * ROWS, HD)
        turned = dot_nn(swap_ref[...], rows).astype(BF16)
        for j in range(8):
            stage[j, d * 8 * ROWS : (d + 1) * 8 * ROWS, :] = turned[j * 8 * ROWS : (j + 1) * 8 * ROWS]
    row_id = lax.broadcasted_iota(jnp.int32, (64 * ROWS, BLOCK), 0)
    for j in range(8):
        x, span = j // 2, pl.ds((j % 2) * BLOCK, BLOCK)
        rho_a = rho_ref[x, 0, 0:1, span]
        rho_b = rho_ref[x, 0, 1:2, span]
        pick = ((row_id == rho_a) | (row_id == rho_b)).astype(F32).astype(BF16)
        total = dot_tn(pick, stage[j]) + dot_nt(dkv_ref[x, 0, span, :], wkv_ref[...])
        out_ref[x, 0, span, :] = total.astype(BF16)


def combine(rho, back, swap, dkv, wkv):
    return pl.pallas_call(
        combine_kernel,
        grid=(4,),
        in_specs=[
            pl.BlockSpec((4, 1, TOP, 2 * BLOCK), lambda t: (0, t, 0, 0)),
            pl.BlockSpec((64, 1, 8 * ROWS, HD), lambda t: (0, t, 0, 0)),
            pl.BlockSpec(swap.shape, lambda t: (0, 0)),
            pl.BlockSpec((4, 1, 2 * BLOCK, 2 * HD), lambda t: (0, t, 0, 0)),
            pl.BlockSpec(wkv.shape, lambda t: (0, 0)),
        ],
        out_specs=pl.BlockSpec((4, 1, 2 * BLOCK, HD), lambda t: (0, t, 0, 0)),
        out_shape=jax.ShapeDtypeStruct((4, 4, 2 * BLOCK, HD), BF16),
        scratch_shapes=[pltpu.VMEM((8, 64 * ROWS, HD), BF16)],
        compiler_params=params(1),
        name="combine_rows",
    )(rho, back, swap, dkv, wkv)


def exchange(rows, axes):
    return lax.all_to_all(rows, axes, split_axis=0, concat_axis=0, tiled=True)


def spread(rows, axes):
    n = lax.axis_size(axes)
    return exchange(jnp.broadcast_to(rows[None], (n,) + rows.shape), axes)


def per_device(
    hidden, out_grad, queries, key_heads, value_heads, routes, route_gates, w_query, w_out, w_key, w_value
):
    swap, pad = swap_matrix().astype(BF16), pad_matrix().astype(BF16)
    unpad = pad.T
    xi, zh, zl = lax.axis_index("x"), lax.axis_index("zh"), lax.axis_index("zl")
    kv_own = jnp.concatenate([key_heads[0], value_heads[0]], axis=1)
    kv = lax.all_gather(kv_own, SEQ, axis=0, tiled=True)
    routes_t = routes[0].reshape(4, 4, 2 * BLOCK, TOP).transpose(0, 1, 3, 2)
    hid_packed, grad_packed, rho = pack(
        routes_t,
        hidden[0].reshape(4, 4, 2 * BLOCK, HD),
        out_grad[0].reshape(4, 4, 2 * BLOCK, HD),
        swap,
    )
    grad_rows = exchange(grad_packed, WIDE)
    w_out_r = exchange(w_out, SLAB).reshape(8, EPD * HD, HD)
    w_query_r = exchange(w_query, SLAB).reshape(8, EPD, HD, HD).transpose(0, 1, 3, 2).reshape(8, EPD * HD, HD)
    hid_rows = exchange(hid_packed, WIDE)
    q = queries[0].transpose(1, 0, 2).reshape(TOP * BLOCK, HD)
    gates = route_gates[0].T.reshape(TOP * BLOCK, 1)
    own = lax.dynamic_slice(rho, (xi, zh, 0, zl * BLOCK), (1, 1, TOP, BLOCK)).reshape(TOP * BLOCK)
    own = own // ROWS * PAD + own % ROWS
    start = ((xi * 8 + zh * 2 + zl) * BLOCK).reshape(1)
    prob, head_out, gated = attend_forward(start, q, kv, gates)

    parts = exchange(head_sums(grad_rows, w_out_r), "zh")
    head_home = exchange(reduce_heads(parts, pad).reshape(64, PAD, HD), WIDE)
    slots, dkv_part = attend_backward(
        head_home.reshape(64 * PAD, HD), own.reshape(1, -1), own.reshape(-1, 1), gates, q, kv, prob, head_out, gated
    )
    mine = exchange(slots.reshape(64, PAD, 2 * HD), WIDE).reshape(64 * PAD, 2 * HD)
    dqg = spread(unpad_rows(mine, unpad), "zh").reshape(4, 8, 8 * ROWS, 2 * HD)
    back = exchange(route_back(dqg, w_query_r).reshape(64, 4, 8 * ROWS, HD), WIDE)
    grad_wq, grad_wo = weight_grads(dqg, hid_rows, grad_rows)
    grad_wq = exchange(grad_wq.reshape(16, HD, HD), SLAB).astype(F32)
    grad_wo = exchange(grad_wo.reshape(16, HD, HD), SLAB).astype(F32)

    dkv_x = exchange(dkv_part.reshape(4, 8 * BLOCK, 2 * HD), "x").astype(F32).sum(axis=0).astype(BF16)
    dkv_own = exchange(dkv_x.reshape(8, BLOCK, 2 * HD), ("zh", "zl")).astype(F32).sum(axis=0).astype(BF16)
    dkv = spread(spread(dkv_own, ("zh", "zl")).reshape(8 * BLOCK, 2 * HD), "x")
    dkv = dkv.reshape(4, 4, 2 * BLOCK, 2 * HD)
    wkv = jnp.concatenate([w_key, w_value], axis=1)
    grad_hidden = combine(rho, back, swap, dkv, wkv).reshape(1, 4096, HD)
    proj = lax.dot_general(
        hidden[0], dkv.reshape(-1, 2 * HD), (((0,), (0,)), ((), ())), preferred_element_type=F32
    )
    proj = spread(proj.astype(BF16), GRP).astype(F32).sum(axis=0)
    return (grad_hidden, grad_wq, grad_wo, proj[:, :HD], proj[:, HD:])


def solution(mesh):
    fine = Mesh(mesh.devices.reshape(4, 4, 2, 4, 2), SEQ + GRP)
    in_specs = (
        P(GRP, None, SEQ),
        P(GRP, None, SEQ),
        P(GRP, SEQ, None, None),
        P(GRP, SEQ, None),
        P(GRP, SEQ, None),
        P(GRP, None, None),
        P(GRP, SEQ, None),
        P(GRP, SEQ, None),
        P(GRP, None, SEQ),
        P(SEQ, None),
        P(SEQ, None),
    )
    out_specs = (
        P(GRP, None, SEQ),
        P(GRP, SEQ, None),
        P(GRP, None, SEQ),
        P(SEQ, None),
        P(SEQ, None),
    )
    return jax.shard_map(per_device, mesh=fine, in_specs=in_specs, out_specs=out_specs, check_vma=False)
```

time: 1260 us -> 478 us (0.38); the launches traced: 1250 us -> 476 us
  waiting for transfers between devices: 1020 us -> 189 us
  blocking collectives: 23.1 us -> 150 us
  matrix products: 76.6 us -> 0.75 us
  Pallas kernels: 0 us -> 51.6 us
  other arithmetic: 43.1 us -> 10.4 us
  local copies, waits for them, and re-layouts: 41.2 us -> 9.07 us
  starting transfers between devices: 26.4 us -> 51.4 us
    reduce_scatter x2 -> x0, waiting for transfers between devices: 386 us -> none  [the longest x1 217 us: per_device(): lax.psum_scatter(value_sum, 'seq', scatter_dimension=0, tiled=True)]
    all_gather x6 -> x1, waiting for transfers between devices: 357 us -> 76.7 us  [per_device(): kv = lax.all_gather(kv_own, SEQ, axis=0, tiled=True)]
    unnamed x11 -> x1, waiting for transfers between devices: 182 us -> 0.02 us
    all_to_all x2 -> x6, blocking collectives: 23.1 us -> 150 us  [exchange(): return lax.all_to_all(rows, axes, split_axis=0, concat_axis=0, tiled=True)]
    dot_general x20 -> x1, matrix products: 76.6 us -> 0.75 us  [per_device(): lax.dot_general(hidden[0], dkv.reshape(-1, 2 * HD), (((0,), (0,)), ((), (...]
    all_to_all x4 -> x10, waiting for transfers between devices: 36.9 us -> 113 us  [exchange(): return lax.all_to_all(rows, axes, split_axis=0, concat_axis=0, tiled=True)]
    psum x1 -> x0, waiting for transfers between devices: 59.5 us -> none  [per_device(): lax.psum(key_part.astype(jnp.bfloat16), ('node', 'dev')).astype(jnp.float32)]
    pallas_call x0 -> x9, Pallas kernels: none -> 51.6 us  [the longest x1 10.7 us: pack(): pl.pallas_call(pack_kernel, grid=(4,), in_specs=[ids, slab, slab, pl.Bloc...]
  transfers between devices with their start and end apart: 14 -> 11, of which waited for: 10 -> 9; matrix products, arithmetic and copies ran while one was open for 8% -> 3% of each run, Pallas kernels for 0% -> 8%
where the time goes in v1:
time: 478 us; the launch traced here: 476 us
  waiting for transfers between devices  189 us (40%)
  blocking collectives  150 us (31%)
  Pallas kernels  51.6 us (11%)
  starting transfers between devices  51.4 us (11%)
  between operations  14.3 us (3%)
  other arithmetic  10.4 us (2%)
  local copies, waits for them, and re-layouts  9.07 us (2%)
    all_to_all x6, blocking collectives, exchange(): return lax.all_to_all(rows, axes, split_axis=0, concat_axis=0, tiled=True)  150 us
    all_to_all x10, waiting for transfers between devices, exchange(): return lax.all_to_all(rows, axes, split_axis=0, concat_axis=0, tiled=True)  113 us
    all_gather x1, waiting for transfers between devices, per_device(): kv = lax.all_gather(kv_own, SEQ, axis=0, tiled=True)  76.7 us
    all_to_all x10, starting transfers between devices, exchange(): return lax.all_to_all(rows, axes, split_axis=0, concat_axis=0, tiled=True)  51.1 us
    pallas_call x1, Pallas kernels, pack(): pl.pallas_call(pack_kernel, grid=(4,), in_specs=[ids, slab, slab, pl.Bloc...  10.7 us
  transfers between devices with their start and end apart: 11, of which 9 were waited for; matrix products, arithmetic and copies ran while one was open for 3% of the time, Pallas kernels for 8%

profile of v1, /device:TPU:1, one launch (start us, length us, event | category | flops | bytes accessed | tf_op | source)
XLA Modules:
  0.0 476.4 jit_solution(17900154687301293309)
XLA Ops:
  7.2 6.2 %all-to-all-start.1 = ((bf16[16,128,128]{2,1,0:T(8,128)(2,1)}), bf16[16,128,128]{2,1,0:T(8,128)(2,1)S(1)}, u32[]{:S(2)}, u32[]{:S(2)}) async-start(bf16[16,128,128]{2,1,0:T(8,128)(2,1)} %param.22), calls=%async_computation.1 | async-start | bytes 1048576 | tf_op jit(solution)/shard_map/all_to_all | solution.py:355
  13.4 10.7 %pack_rows.1 = (bf16[64,4,48,128]{3,2,1,0:T(8,128)(2,1)}, bf16[64,4,48,128]{3,2,1,0:T(8,128)(2,1)}, s32[4,4,2,256]{3,2,1,0:T(2,128)}) custom-call(s32[4,4,2,256]{3,2,1,0:T(2,128)} %bitcast.90, bf16[4,4,256,128]{3,2,1,0:T(8,128)(2,1)} %bitcast.72, bf16[4,4,256,128]{3,2,1,0:T(8,128)(2,1)} %bitcast.80, bf16[384,384]{1,0:T(8,128)(2,1)} %constant.58.clone.swap_ref), custom_call_target="tpu_custom_call" | custom-call | tf_op jit(solution)/shard_map/pack_rows/pallas_call | solution.py:99
  24.1 0.0 all-to-all-done.1
  24.1 0.0 copy-start.10
  24.1 50.6 %all_to_all.80 = bf16[64,4,48,128]{3,2,1,0:T(8,128)(2,1)} all-to-all(bf16[64,4,48,128]{3,2,1,0:T(8,128)(2,1)} %get-tuple-element.16), channel_id=1, replica_groups=mesh['x'=4,'zh'=4,'zl'=2,'node'=4,'dev'=2] {'x','zl','node','dev'}, dimensions={0} | all-to-all | bytes 6291456 | tf_op jit(solution)/shard_map/all_to_all | solution.py:355
  74.8 4.9 %head_sums.1 = bf16[4,8,48,128]{3,2,1,0:T(8,128)(2,1)} custom-call(bf16[8,8,192,128]{3,2,1,0:T(8,128)(2,1)} %bitcast.64, bf16[8,256,128]{2,1,0:T(8,128)(2,1)} %bitcast.77), custom_call_target="tpu_custom_call" | custom-call | tf_op jit(solution)/shard_map/head_sums/pallas_call | solution.py:129
  79.7 20.0 %all_to_all.81 = bf16[4,8,48,128]{3,2,1,0:T(8,128)(2,1)} all-to-all(bf16[4,8,48,128]{3,2,1,0:T(8,128)(2,1)} %head_sums.1), channel_id=1, replica_groups=mesh['x'=4,'zh'=4,'zl'=2,'node'=4,'dev'=2] {'zh'}, dimensions={0} | all-to-all | bytes 786432 | tf_op jit(solution)/shard_map/all_to_all | solution.py:355
  99.7 3.5 all-to-all-start.6
  103.2 2.0 reduce_heads.1
  105.2 6.1 %all-to-all-done.6 = bf16[16,128,128]{2,1,0:T(8,128)(2,1)S(1)} async-done(((bf16[16,128,128]{2,1,0:T(8,128)(2,1)}), bf16[16,128,128]{2,1,0:T(8,128)(2,1)S(1)}, u32[]{:S(2)}, u32[]{:S(2)}) %all-to-all-start.6) | async-done | bytes 524320 | tf_op jit(solution)/shard_map/all_to_all | solution.py:355
  111.4 16.2 %all_to_all.82 = bf16[64,8,128]{2,1,0:T(8,128)(2,1)} all-to-all(bf16[64,8,128]{2,1,0:T(8,128)(2,1)} %bitcast.84), channel_id=1, replica_groups=mesh['x'=4,'zh'=4,'zl'=2,'node'=4,'dev'=2] {'x','zl','node','dev'}, dimensions={0} | all-to-all | bytes 262144 | tf_op jit(solution)/shard_map/all_to_all | solution.py:355
  127.6 4.7 all-to-all-start.12
  132.4 0.2 all-gather.2.cloned.1.call-start
  132.6 0.6 pad_maximum_fusion
  133.2 0.0 all-gather.2.cloned.1.call-update
  133.3 0.6 compare_bitcast_fusion
  133.9 0.1 copy.34
  134.1 0.1 copy.36
  134.2 0.2 copy.48
  134.4 0.8 copy.43.gate_ref
  135.2 0.6 copy.41
  135.9 0.5 fusion.4.rho_row_ref
  136.4 0.7 fusion.3.rho_col_ref
  137.1 76.7 %all-gather.2.cloned.1.call-done.kv_ref = bf16[4096,256]{1,0:T(8,128)(2,1)} async-done(((bf16[128,256]{1,0:T(8,128)(2,1)}), bf16[4096,256]{1,0:T(8,128)(2,1)}) %all-gather.2.cloned.1.call-update) | async-done | bytes 2097168 | tf_op jit(solution)/shard_map/all_gather | solution.py:370
  213.8 5.0 %attend_forward.1 = (bf16[256,4096]{1,0:T(8,128)(2,1)}, f32[256,128]{1,0:T(8,128)}, bf16[256,128]{1,0:T(8,128)(2,1)}) custom-call(s32[1]{0:T(128)} %bitcast.21.start_ref, bf16[256,128]{1,0:T(8,128)(2,1)} %bitcast.82, bf16[4096,256]{1,0:T(8,128)(2,1)} %all-gather.2.cloned.1.call-done.kv_ref, f32[256,1]{1,0:T(8,128)} %copy.43.gate_ref), custom_call_target="tpu_custom_call" | custom-call | tf_op jit(solution)/shard_map/attend_forward/pallas_call | solution.py:189
  218.8 7.2 %attend_backward.1 = (bf16[512,256]{1,0:T(8,128)(2,1)}, bf16[4096,256]{1,0:T(8,128)(2,1)}) custom-call(bf16[512,128]{1,0:T(8,128)(2,1)} %bitcast.87, s32[1,256]{1,0:T(1,128)} %fusion.4.rho_row_ref, s32[256,1]{1,0:T(8,128)} %fusion.3.rho_col_ref, f32[256,1]{1,0:T(8,128)} %copy.43.gate_ref, bf16[256,128]{1,0:T(8,128)(2,1)} %bitcast.83, ...), custom_call_target="tpu_custom_call" | custom-call | tf_op jit(solution)/shard_map/attend_backward/pallas_call | solution.py:231
  226.0 21.0 %all_to_all.83 = bf16[64,8,256]{2,1,0:T(8,128)(2,1)} all-to-all(bf16[64,8,256]{2,1,0:T(8,128)(2,1)} %bitcast.88), channel_id=1, replica_groups=mesh['x'=4,'zh'=4,'zl'=2,'node'=4,'dev'=2] {'x','zl','node','dev'}, dimensions={0} | all-to-all | bytes 524288 | tf_op jit(solution)/shard_map/all_to_all | solution.py:355
  247.0 4.5 all-to-all-start.8
  251.5 2.0 unpad_rows.1
  253.5 24.1 %all-to-all-done.8 = bf16[4,1024,256]{2,1,0:T(8,128)(2,1)} async-done(((bf16[4,1024,256]{2,1,0:T(8,128)(2,1)}), bf16[4,1024,256]{2,1,0:T(8,128)(2,1)}, u32[]{:S(2)}, u32[]{:S(2)}) %all-to-all-start.8) | async-done | bytes 2097184 | tf_op jit(solution)/shard_map/all_to_all | solution.py:355
  277.6 1.9 broadcast_in_dim.10
  279.4 4.2 all-to-all-start.5
  283.7 2.8 reduce_sum.33
  286.5 17.5 %all-to-all-done.5 = bf16[4,384,256]{2,1,0:T(8,128)(2,1)S(1)} async-done(((bf16[4,384,256]{2,1,0:T(8,128)(2,1)}), bf16[4,384,256]{2,1,0:T(8,128)(2,1)S(1)}, u32[]{:S(2)}, u32[]{:S(2)}) %all-to-all-start.5) | async-done | bytes 786464 | tf_op jit(solution)/shard_map/all_to_all | solution.py:355
  304.0 4.3 all-to-all-start.9
  308.3 7.5 %weight_grads.1 = (bf16[8,2,128,128]{3,2,1,0:T(8,128)(2,1)}, bf16[8,2,128,128]{3,2,1,0:T(8,128)(2,1)}) custom-call(bf16[4,8,48,256]{3,2,1,0:T(8,128)(2,1)} %bitcast.70, bf16[8,8,192,128]{3,2,1,0:T(8,128)(2,1)} %bitcast.68, bf16[8,8,192,128]{3,2,1,0:T(8,128)(2,1)} %bitcast.65), custom_call_target="tpu_custom_call" | custom-call | tf_op jit(solution)/shard_map/weight_grads/pallas_call | solution.py:307
  315.8 9.5 %all-to-all-done.9 = bf16[8,128,256]{2,1,0:T(8,128)(2,1)S(1)} async-done(((bf16[8,128,256]{2,1,0:T(8,128)(2,1)}), bf16[8,128,256]{2,1,0:T(8,128)(2,1)S(1)}, u32[]{:S(2)}, u32[]{:S(2)}) %all-to-all-start.9) | async-done | bytes 524320 | tf_op jit(solution)/shard_map/all_to_all | solution.py:355
  325.3 3.5 all-to-all-start.13
  328.8 0.1 reduce_sum.34
  328.9 8.5 %all-to-all-done.13 = bf16[16,128,128]{2,1,0:T(8,128)(2,1)S(1)} async-done(((bf16[16,128,128]{2,1,0:T(8,128)(2,1)}), bf16[16,128,128]{2,1,0:T(8,128)(2,1)S(1)}, u32[]{:S(2)}, u32[]{:S(2)}) %all-to-all-start.13) | async-done | bytes 524320 | tf_op jit(solution)/shard_map/all_to_all | solution.py:355
  337.5 16.9 %all_to_all.84 = bf16[8,128,256]{2,1,0:T(8,128)(2,1)S(1)} all-to-all(bf16[8,128,256]{2,1,0:T(8,128)(2,1)S(1)} %broadcast_in_dim.11), channel_id=1, replica_groups=mesh['x'=4,'zh'=4,'zl'=2,'node'=4,'dev'=2] {'zh','zl'}, dimensions={0} | all-to-all | bytes 1048576 | tf_op jit(solution)/shard_map/all_to_all | solution.py:355
  354.3 0.1 broadcast_in_dim.13
  354.5 0.0 copy-start.4
  354.5 25.0 %all_to_all.85 = bf16[4,1024,256]{2,1,0:T(8,128)(2,1)S(1)} all-to-all(bf16[4,1024,256]{2,1,0:T(8,128)(2,1)S(1)} %broadcast_in_dim.13), channel_id=1, replica_groups=mesh['x'=4,'zh'=4,'zl'=2,'node'=4,'dev'=2] {'x'}, dimensions={0} | all-to-all | bytes 4194304 | tf_op jit(solution)/shard_map/all_to_all | solution.py:355
  379.5 4.2 all-to-all-start.14
  383.7 0.8 fusion
  384.4 0.0 copy-start.9
  384.4 0.1 copy.45
  384.5 6.7 %all-to-all-done.14 = bf16[16,128,128]{2,1,0:T(8,128)(2,1)} async-done(((bf16[16,128,128]{2,1,0:T(8,128)(2,1)}), bf16[16,128,128]{2,1,0:T(8,128)(2,1)}, u32[]{:S(2)}, u32[]{:S(2)}) %all-to-all-start.14) | async-done | bytes 524320 | tf_op jit(solution)/shard_map/all_to_all | solution.py:355
  391.2 0.9 broadcast_in_dim.14
  392.0 11.0 %all-to-all-start.15 = ((bf16[8,128,256]{2,1,0:T(8,128)(2,1)}), bf16[8,128,256]{2,1,0:T(8,128)(2,1)S(1)}, u32[]{:S(2)}, u32[]{:S(2)}) async-start(bf16[8,128,256]{2,1,0:T(8,128)(2,1)} %broadcast_in_dim.14), calls=%async_computation.15 | async-start | bytes 1048576 | tf_op jit(solution)/shard_map/all_to_all | solution.py:355
  403.0 1.0 copy.44
  404.1 5.0 %route_back.1 = bf16[8,8,192,128]{3,2,1,0:T(8,128)(2,1)} custom-call(bf16[4,8,48,256]{3,2,1,0:T(8,128)(2,1)} %bitcast.71, bf16[8,256,128]{2,1,0:T(8,128)(2,1)} %bitcast.73), custom_call_target="tpu_custom_call" | custom-call | tf_op jit(solution)/shard_map/route_back/pallas_call | solution.py:269
  409.1 3.4 all-to-all-done.15
  412.5 0.8 copy-done.6
  413.3 5.0 %all-to-all-start.7 = ((bf16[64,4,48,128]{3,2,1,0:T(8,128)(2,1)}), bf16[64,4,48,128]{3,2,1,0:T(8,128)(2,1)S(1)}, u32[]{:S(2)}, u32[]{:S(2)}) async-start(bf16[64,4,48,128]{3,2,1,0:T(8,128)(2,1)} %bitcast.69), calls=%async_computation.7 | async-start | bytes 6291456 | tf_op jit(solution)/shard_map/all_to_all | solution.py:355
  418.4 0.6 pad_maximum_fusion.1.wkv_ref
  419.1 2.1 convert_element_type.19
  421.2 2.1 convert_element_type.20
  423.3 0.1 convert_reduce_fusion
  423.4 0.7 fusion.5
  424.0 36.7 %all-to-all-done.7.back_ref = bf16[64,4,48,128]{3,2,1,0:T(8,128)(2,1)S(1)} async-done(((bf16[64,4,48,128]{3,2,1,0:T(8,128)(2,1)}), bf16[64,4,48,128]{3,2,1,0:T(8,128)(2,1)S(1)}, u32[]{:S(2)}, u32[]{:S(2)}) %all-to-all-start.7) | async-done | bytes 3145760 | tf_op jit(solution)/shard_map/all_to_all | solution.py:355
  460.7 1.6 copy-done.2
  462.4 7.2 %combine_rows.1 = bf16[4,4,256,128]{3,2,1,0:T(8,128)(2,1)} custom-call(s32[4,4,2,256]{3,2,1,0:T(2,128)} %get-tuple-element.15.rho_ref, bf16[64,4,48,128]{3,2,1,0:T(8,128)(2,1)} %copy-done.2, bf16[384,384]{1,0:T(8,128)(2,1)} %constant.58.clone.swap_ref, bf16[4,4,256,256]{3,2,1,0:T(8,128)(2,1)} %bitcast.67, bf16[128,256]{1,0:T(8,128)(2,1)} %pad_maximum_fusion.1.wkv_ref), custom_call_target="tpu_custom_call" | custom-call | tf_op jit(solution)/shard_map/combine_rows/pallas_call | solution.py:336
  (33 shorter events, 0.1 us)
Async XLA Ops:
  7.2 16.9 %all-to-all-start.1 = ((bf16[16,128,128]{2,1,0:T(8,128)(2,1)}), bf16[16,128,128]{2,1,0:T(8,128)(2,1)S(1)}, u32[]{:S(2)}, u32[]{:S(2)}) async-start(bf16[16,128,128]{2,1,0:T(8,128)(2,1)} %param.22), calls=%async_computation.1 | async-start | bytes 1048576 | tf_op jit(solution)/shard_map/all_to_all | solution.py:355
  24.1 50.7 %copy-start.10 = (bf16[16,128,128]{2,1,0:T(8,128)(2,1)}, bf16[16,128,128]{2,1,0:T(8,128)(2,1)S(1)}, u32[]{:S(2)}) copy-start(bf16[16,128,128]{2,1,0:T(8,128)(2,1)S(1)} %all-to-all-done.1) | copy-start | bytes 1572868
  99.7 11.7 %all-to-all-start.6 = ((bf16[16,128,128]{2,1,0:T(8,128)(2,1)}), bf16[16,128,128]{2,1,0:T(8,128)(2,1)S(1)}, u32[]{:S(2)}, u32[]{:S(2)}) async-start(bf16[16,128,128]{2,1,0:T(8,128)(2,1)} %param.21), calls=%async_computation.6 | async-start | bytes 1048576 | tf_op jit(solution)/shard_map/all_to_all | solution.py:355
  111.4 16.3 %copy-start.8 = (bf16[16,128,128]{2,1,0:T(8,128)(2,1)}, bf16[16,128,128]{2,1,0:T(8,128)(2,1)S(1)}, u32[]{:S(2)}) copy-start(bf16[16,128,128]{2,1,0:T(8,128)(2,1)S(1)} %all-to-all-done.6) | copy-start | bytes 1572868
  127.6 5.0 %copy-start.12 = (bf16[1,128,128]{2,1,0:T(8,128)(2,1)S(1)}, bf16[1,128,128]{2,1,0:T(8,128)(2,1)}, u32[]{:S(2)}) copy-start(bf16[1,128,128]{2,1,0:T(8,128)(2,1)} %param.18) | copy-start | bytes 98308
  127.6 5.0 %copy-start.13 = (bf16[1,128,128]{2,1,0:T(8,128)(2,1)S(1)}, bf16[1,128,128]{2,1,0:T(8,128)(2,1)}, u32[]{:S(2)}) copy-start(bf16[1,128,128]{2,1,0:T(8,128)(2,1)} %param.17) | copy-start | bytes 98308
  127.6 6.8 %copy-start.16 = (f32[1,128,2]{1,2,0:T(2,128)S(1)}, f32[1,128,2]{1,2,0:T(2,128)}, u32[]{:S(2)}) copy-start(f32[1,128,2]{1,2,0:T(2,128)} %param.20) | copy-start | bytes 3076
  127.6 7.6 %copy-start.11 = (bf16[1,128,2,128]{3,2,1,0:T(2,128)(2,1)S(1)}, bf16[1,128,2,128]{3,2,1,0:T(2,128)(2,1)}, u32[]{:S(2)}) copy-start(bf16[1,128,2,128]{3,2,1,0:T(2,128)(2,1)} %param.16) | copy-start | bytes 196612
  127.6 98.4 %all-to-all-start.12 = ((bf16[64,4,48,128]{3,2,1,0:T(8,128)(2,1)}), bf16[64,4,48,128]{3,2,1,0:T(8,128)(2,1)S(1)}, u32[]{:S(2)}, u32[]{:S(2)}) async-start(bf16[64,4,48,128]{3,2,1,0:T(8,128)(2,1)} %get-tuple-element.22), calls=%async_computation.12 | async-start | bytes 6291456 | tf_op jit(solution)/shard_map/all_to_all | solution.py:355
  132.4 81.4 %all-gather.2.cloned.1.call-start = ((), (), s32[]{:S(2)}) async-start(), calls=%async_computation.16 | async-start | bytes 2162688 | tf_op jit(solution)/shard_map/all_gather | solution.py:370
  226.0 21.0 %copy-start.1 = (bf16[64,4,48,128]{3,2,1,0:T(8,128)(2,1)}, bf16[64,4,48,128]{3,2,1,0:T(8,128)(2,1)S(1)}, u32[]{:S(2)}) copy-start(bf16[64,4,48,128]{3,2,1,0:T(8,128)(2,1)S(1)} %all-to-all-done.12) | copy-start | bytes 9437188
  247.0 30.6 %all-to-all-start.8 = ((bf16[4,1024,256]{2,1,0:T(8,128)(2,1)}), bf16[4,1024,256]{2,1,0:T(8,128)(2,1)}, u32[]{:S(2)}, u32[]{:S(2)}) async-start(bf16[4,1024,256]{2,1,0:T(8,128)(2,1)} %bitcast.75), calls=%async_computation.8 | async-start | bytes 4194304 | tf_op jit(solution)/shard_map/all_to_all | solution.py:355
  279.4 24.5 %all-to-all-start.5 = ((bf16[4,384,256]{2,1,0:T(8,128)(2,1)}), bf16[4,384,256]{2,1,0:T(8,128)(2,1)S(1)}, u32[]{:S(2)}, u32[]{:S(2)}) async-start(bf16[4,384,256]{2,1,0:T(8,128)(2,1)} %broadcast_in_dim.10), calls=%async_computation.5 | async-start | bytes 1572864 | tf_op jit(solution)/shard_map/all_to_all | solution.py:355
  304.0 4.3 copy-start.3
  304.0 21.3 %all-to-all-start.9 = ((bf16[8,128,256]{2,1,0:T(8,128)(2,1)}), bf16[8,128,256]{2,1,0:T(8,128)(2,1)S(1)}, u32[]{:S(2)}, u32[]{:S(2)}) async-start(bf16[8,128,256]{2,1,0:T(8,128)(2,1)} %bitcast.32), calls=%async_computation.9 | async-start | bytes 1048576 | tf_op jit(solution)/shard_map/all_to_all | solution.py:355
  325.3 12.1 %all-to-all-start.13 = ((bf16[16,128,128]{2,1,0:T(8,128)(2,1)}), bf16[16,128,128]{2,1,0:T(8,128)(2,1)S(1)}, u32[]{:S(2)}, u32[]{:S(2)}) async-start(bf16[16,128,128]{2,1,0:T(8,128)(2,1)} %bitcast.86), calls=%async_computation.13 | async-start | bytes 1048576 | tf_op jit(solution)/shard_map/all_to_all | solution.py:355
  337.4 16.9 %copy-start.5 = (bf16[16,128,128]{2,1,0:T(8,128)(2,1)}, bf16[16,128,128]{2,1,0:T(8,128)(2,1)S(1)}, u32[]{:S(2)}) copy-start(bf16[16,128,128]{2,1,0:T(8,128)(2,1)S(1)} %all-to-all-done.13) | copy-start | bytes 1572868
  354.5 29.2 %copy-start.4 = (bf16[1,4096,128]{2,1,0:T(8,128)(2,1)S(1)}, bf16[1,4096,128]{2,1,0:T(8,128)(2,1)}, u32[]{:S(2)}) copy-start(bf16[1,4096,128]{2,1,0:T(8,128)(2,1)} %param.14) | copy-start | bytes 3145732
  379.5 4.9 %copy-start = (bf16[4,1024,256]{2,1,0:T(8,128)(2,1)}, bf16[4,1024,256]{2,1,0:T(8,128)(2,1)S(1)}, u32[]{:S(2)}) copy-start(bf16[4,1024,256]{2,1,0:T(8,128)(2,1)S(1)} %all_to_all.85) | copy-start | bytes 6291460
  379.5 11.7 %all-to-all-start.14 = ((bf16[16,128,128]{2,1,0:T(8,128)(2,1)}), bf16[16,128,128]{2,1,0:T(8,128)(2,1)}, u32[]{:S(2)}, u32[]{:S(2)}) async-start(bf16[16,128,128]{2,1,0:T(8,128)(2,1)} %bitcast.85), calls=%async_computation.14 | async-start | bytes 1048576 | tf_op jit(solution)/shard_map/all_to_all | solution.py:355
  384.4 18.6 %copy-start.9 = (bf16[16,128,128]{2,1,0:T(8,128)(2,1)S(1)}, bf16[16,128,128]{2,1,0:T(8,128)(2,1)}, u32[]{:S(2)}) copy-start(bf16[16,128,128]{2,1,0:T(8,128)(2,1)} %copy-done.8) | copy-start | bytes 1572868
  392.0 20.5 %all-to-all-start.15 = ((bf16[8,128,256]{2,1,0:T(8,128)(2,1)}), bf16[8,128,256]{2,1,0:T(8,128)(2,1)S(1)}, u32[]{:S(2)}, u32[]{:S(2)}) async-start(bf16[8,128,256]{2,1,0:T(8,128)(2,1)} %broadcast_in_dim.14), calls=%async_computation.15 | async-start | bytes 1048576 | tf_op jit(solution)/shard_map/all_to_all | solution.py:355
  412.5 0.8 copy-start.6
  412.5 5.9 %copy-start.14 = (bf16[128,128]{1,0:T(8,128)(2,1)S(1)}, bf16[128,128]{1,0:T(8,128)(2,1)}, u32[]{:S(2)}) copy-start(bf16[128,128]{1,0:T(8,128)(2,1)} %param.24) | copy-start | bytes 98308
  412.5 5.9 %copy-start.15 = (bf16[128,128]{1,0:T(8,128)(2,1)S(1)}, bf16[128,128]{1,0:T(8,128)(2,1)}, u32[]{:S(2)}) copy-start(bf16[128,128]{1,0:T(8,128)(2,1)} %param.23) | copy-start | bytes 98308
  413.3 47.4 %all-to-all-start.7 = ((bf16[64,4,48,128]{3,2,1,0:T(8,128)(2,1)}), bf16[64,4,48,128]{3,2,1,0:T(8,128)(2,1)S(1)}, u32[]{:S(2)}, u32[]{:S(2)}) async-start(bf16[64,4,48,128]{3,2,1,0:T(8,128)(2,1)} %bitcast.69), calls=%async_computation.7 | async-start | bytes 6291456 | tf_op jit(solution)/shard_map/all_to_all | solution.py:355
  418.4 4.9 %copy-start.7 = (bf16[8,128,256]{2,1,0:T(8,128)(2,1)S(1)}, bf16[8,128,256]{2,1,0:T(8,128)(2,1)}, u32[]{:S(2)}) copy-start(bf16[8,128,256]{2,1,0:T(8,128)(2,1)} %copy-done.6) | copy-start | bytes 1572868
  460.7 1.6 copy-start.2
Sparse Core Ops, SparseCore 0:
  136.4 77.3 all-gather.1

commit v2 on v1

--- a/solution.py
+++ b/solution.py
@@ -107,6 +107,7 @@
             jax.ShapeDtypeStruct((4, 4, TOP, 2 * BLOCK), jnp.int32),
         ],
         scratch_shapes=[pltpu.VMEM((8, 64 * ROWS, 2 * HD), BF16)],
+        cost_estimate=pl.CostEstimate(flops=1000, bytes_accessed=1000, transcendentals=0),
         compiler_params=params(1),
         name="pack_rows",
     )(routes_t, hid, grad, swap)
@@ -116,34 +117,37 @@
     return lax.rem(lax.broadcasted_iota(jnp.int32, shape, 0), ROWS) >= CAP
 
 
-def head_kernel(grad_ref, w_ref, out_ref):
+def head_kernel(at_ref, grad_ref, w_ref, out_ref):
+    zh = at_ref[1]
     for g in range(2):
-        total = dot_nt(grad_ref[0, g], w_ref[0])
-        for r in range(1, 8):
-            total += dot_nt(grad_ref[r, g], w_ref[r])
+        total = jnp.zeros((32 * ROWS, EPD * HD), F32)
+        for r in range(8):
+            total += dot_nt(grad_ref[r, g], jnp.concatenate([w_ref[r, 0, 0], w_ref[r, 1, 0]], axis=0))
         own = jnp.where(second_expert((32 * ROWS, HD)), total[:, HD:], total[:, :HD])
-        out_ref[:, g] = own.astype(BF16).reshape(4, 8 * ROWS, HD)
-
-
-def head_sums(grad_rows, w_out_r):
+        own = own.astype(BF16).reshape(4, 8 * ROWS, HD)
+        for t in range(4):
+            out_ref[(t + 4 - zh) % 4, g] = own[t]
+
+
+def head_sums(at, grad_rows, weights):
     return pl.pallas_call(
         head_kernel,
         grid=(4,),
         in_specs=[
+            pl.BlockSpec(memory_space=pltpu.SMEM),
             pl.BlockSpec((8, 2, 32 * ROWS, HD), lambda i: (0, i, 0, 0)),
-            pl.BlockSpec((8, 2 * HD, HD), lambda i: (0, 0, 0)),
+            pl.BlockSpec((8, EPD, 1, HD, HD), lambda i: (0, 0, 0, 0, 0)),
         ],
         out_specs=pl.BlockSpec((4, 2, 8 * ROWS, HD), lambda i: (0, i, 0, 0)),
         out_shape=jax.ShapeDtypeStruct((4, 8, 8 * ROWS, HD), BF16),
+        cost_estimate=pl.CostEstimate(flops=1000, bytes_accessed=1000, transcendentals=0),
         compiler_params=params(1),
         name="head_sums",
-    )(grad_rows.reshape(8, 8, 32 * ROWS, HD), w_out_r)
-
-
-def reduce_kernel(parts_ref, pad_ref, out_ref):
-    total = parts_ref[0].astype(F32)
-    for s in range(1, 4):
-        total += parts_ref[s].astype(F32)
+    )(at, grad_rows.reshape(8, 8, 32 * ROWS, HD), weights)
+
+
+def reduce_kernel(a_ref, b_ref, c_ref, d_ref, pad_ref, out_ref):
+    total = a_ref[...].astype(F32) + b_ref[...].astype(F32) + c_ref[...].astype(F32) + d_ref[...].astype(F32)
     out_ref[...] = dot_nn(pad_ref[...], total.astype(BF16)).astype(BF16)
 
 
@@ -151,16 +155,18 @@
     return pl.pallas_call(
         reduce_kernel,
         out_shape=jax.ShapeDtypeStruct((64 * PAD, HD), BF16),
+        cost_estimate=pl.CostEstimate(flops=1000, bytes_accessed=1000, transcendentals=0),
         compiler_params=params(0),
         name="reduce_heads",
-    )(parts.reshape(4, 64 * ROWS, HD), pad)
-
-
-def forward_kernel(start_ref, q_ref, kv_ref, gate_ref, prob_out, head_out, gated_out, score):
+    )(*[p.reshape(64 * ROWS, HD) for p in parts], pad)
+
+
+def forward_kernel(at_ref, q_ref, kv_ref, gate_ref, prob_out, head_out, gated_out, score):
     n, length = q_ref.shape[0], kv_ref.shape[0]
     step = 512
     q = q_ref[...]
-    pos = start_ref[0] + lax.rem(lax.broadcasted_iota(jnp.int32, (n, step), 0), BLOCK)
+    start = (at_ref[0] * 8 + at_ref[1] * 2 + at_ref[2]) * BLOCK
+    pos = start + lax.rem(lax.broadcasted_iota(jnp.int32, (n, step), 0), BLOCK)
     lane = lax.broadcasted_iota(jnp.int32, (n, step), 1)
     top = jnp.full((n, 1), -jnp.inf, F32)
     for c in range(0, length, step):
@@ -183,7 +189,7 @@
     gated_out[...] = (gate_ref[...] * out).astype(BF16)
 
 
-def attend_forward(start, q, kv, gates):
+def attend_forward(at, q, kv, gates):
     n, length = q.shape[0], kv.shape[0]
     vm = pl.BlockSpec(memory_space=pltpu.VMEM)
     return pl.pallas_call(
@@ -196,9 +202,10 @@
             jax.ShapeDtypeStruct((n, HD), BF16),
         ],
         scratch_shapes=[pltpu.VMEM((n, length), F32)],
+        cost_estimate=pl.CostEstimate(flops=1000, bytes_accessed=1000, transcendentals=0),
         compiler_params=params(0),
         name="attend_forward",
-    )(start, q, kv, gates)
+    )(at, q, kv, gates)
 
 
 def backward_kernel(
@@ -234,6 +241,7 @@
             jax.ShapeDtypeStruct((64 * PAD, 2 * HD), BF16),
             jax.ShapeDtypeStruct(kv.shape, BF16),
         ],
+        cost_estimate=pl.CostEstimate(flops=1000, bytes_accessed=1000, transcendentals=0),
         compiler_params=params(0),
         name="attend_backward",
     )(head, rho_row, rho_col, gates, q, kv, prob, out, gated)
@@ -247,6 +255,7 @@
     return pl.pallas_call(
         unpad_kernel,
         out_shape=jax.ShapeDtypeStruct((64 * ROWS, 2 * HD), BF16),
+        cost_estimate=pl.CostEstimate(flops=1000, bytes_accessed=1000, transcendentals=0),
         compiler_params=params(0),
         name="unpad_rows",
     )(rows, unpad)
@@ -258,29 +267,42 @@
     return jnp.concatenate([jnp.where(later, zero, rows), jnp.where(later, rows, zero)], axis=1)
 
 
-def back_kernel(dqg_ref, w_ref, out_ref):
+def in_order(at_ref, parts, stage):
+    zh = at_ref[1]
+    for s, part in enumerate(parts):
+        stage[(zh + 4 - s) % 4] = part[...]
+
+
+def back_kernel(at_ref, a_ref, b_ref, c_ref, d_ref, w_ref, out_ref, dqg_ref):
+    in_order(at_ref, (a_ref, b_ref, c_ref, d_ref), dqg_ref)
     for g in range(2):
         dq = by_expert(dqg_ref[:, g, :, :HD].reshape(32 * ROWS, HD))
         for r in range(8):
-            out_ref[r, g] = dot_nn(dq, w_ref[r]).astype(BF16)
-
-
-def route_back(dqg, w_query_r):
+            w = jnp.concatenate([w_ref[r, 0, 0], w_ref[r, 1, 0]], axis=1)
+            out_ref[r, g] = dot_nt(dq, w).astype(BF16)
+
+
+def route_back(at, dqg, weights):
     return pl.pallas_call(
         back_kernel,
         grid=(4,),
-        in_specs=[
-            pl.BlockSpec((4, 2, 8 * ROWS, 2 * HD), lambda i: (0, i, 0, 0)),
-            pl.BlockSpec((8, 2 * HD, HD), lambda i: (0, 0, 0)),
-        ],
+        in_specs=[pl.BlockSpec(memory_space=pltpu.SMEM)]
+        + [pl.BlockSpec((2, 8 * ROWS, 2 * HD), lambda i: (i, 0, 0))] * 4
+        + [pl.BlockSpec((8, EPD, 1, HD, HD), lambda i: (0, 0, 1, 0, 0))],
         out_specs=pl.BlockSpec((8, 2, 32 * ROWS, HD), lambda i: (0, i, 0, 0)),
         out_shape=jax.ShapeDtypeStruct((8, 8, 32 * ROWS, HD), BF16),
+        scratch_shapes=[pltpu.VMEM((4, 2, 8 * ROWS, 2 * HD), BF16)],
+        cost_estimate=pl.CostEstimate(flops=1000, bytes_accessed=1000, transcendentals=0),
         compiler_params=params(1),
         name="route_back",
-    )(dqg, w_query_r)
-
-
-def weights_kernel(dqg_ref, hid_ref, grad_ref, wq_out, wo_out, wq_acc, wo_acc):
+    )(at, *dqg, weights)
+
+
+def weights_kernel(
+    at_ref, a_ref, b_ref, c_ref, d_ref, hid_ref, grad_ref, out_ref, dqg_ref, wq_acc, wo_acc
+):
+    in_order(at_ref, (a_ref, b_ref, c_ref, d_ref), dqg_ref)
+
     @pl.when(pl.program_id(0) == 0)
     def _():
         wq_acc[...] = jnp.zeros_like(wq_acc)
@@ -297,23 +319,48 @@
     def _():
         for r in range(8):
             for k in range(EPD):
-                wq_out[r, k] = wq_acc[r, :, k * HD : (k + 1) * HD].astype(BF16)
-                wo_out[r, k] = wo_acc[r, k * HD : (k + 1) * HD, :].astype(BF16)
-
-
-def weight_grads(dqg, hid_rows, grad_rows):
+                out_ref[r, k, 0] = wq_acc[r, :, k * HD : (k + 1) * HD].astype(BF16)
+                out_ref[r, k, 1] = wo_acc[r, k * HD : (k + 1) * HD, :].astype(BF16)
+
+
+def weight_grads(at, dqg, hid_rows, grad_rows):
     rows = pl.BlockSpec((8, 2, 32 * ROWS, HD), lambda i: (0, i, 0, 0))
-    whole = pl.BlockSpec((8, EPD, HD, HD), lambda i: (0, 0, 0, 0))
     return pl.pallas_call(
         weights_kernel,
         grid=(4,),
-        in_specs=[pl.BlockSpec((4, 2, 8 * ROWS, 2 * HD), lambda i: (0, i, 0, 0)), rows, rows],
-        out_specs=[whole, whole],
-        out_shape=[jax.ShapeDtypeStruct((8, EPD, HD, HD), BF16)] * 2,
-        scratch_shapes=[pltpu.VMEM((8, HD, EPD * HD), F32), pltpu.VMEM((8, EPD * HD, HD), F32)],
+        in_specs=[pl.BlockSpec(memory_space=pltpu.SMEM)]
+        + [pl.BlockSpec((2, 8 * ROWS, 2 * HD), lambda i: (i, 0, 0))] * 4
+        + [rows, rows],
+        out_specs=pl.BlockSpec((8, EPD, 2, HD, HD), lambda i: (0, 0, 0, 0, 0)),
+        out_shape=jax.ShapeDtypeStruct((8, EPD, 2, HD, HD), BF16),
+        scratch_shapes=[
+            pltpu.VMEM((4, 2, 8 * ROWS, 2 * HD), BF16),
+            pltpu.VMEM((8, HD, EPD * HD), F32),
+            pltpu.VMEM((8, EPD * HD, HD), F32),
+        ],
+        cost_estimate=pl.CostEstimate(flops=1000, bytes_accessed=1000, transcendentals=0),
         compiler_params=params(1),
         name="weight_grads",
-    )(dqg, hid_rows.reshape(8, 8, 32 * ROWS, HD), grad_rows.reshape(8, 8, 32 * ROWS, HD))
+    )(
+        at,
+        *dqg,
+        hid_rows.reshape(8, 8, 32 * ROWS, HD),
+        grad_rows.reshape(8, 8, 32 * ROWS, HD),
+    )
+
+
+def projection_kernel(hid_ref, dkv_ref, out_ref):
+    out_ref[...] = dot_tn(hid_ref[...], dkv_ref[...]).astype(BF16)
+
+
+def projection(hid, dkv):
+    return pl.pallas_call(
+        projection_kernel,
+        out_shape=jax.ShapeDtypeStruct((HD, 2 * HD), BF16),
+        cost_estimate=pl.CostEstimate(flops=1000, bytes_accessed=1000, transcendentals=0),
+        compiler_params=params(0),
+        name="projection",
+    )(hid, dkv)
 
 
 def combine_kernel(rho_ref, back_ref, swap_ref, dkv_ref, wkv_ref, out_ref, stage):
@@ -346,6 +393,7 @@
         out_specs=pl.BlockSpec((4, 1, 2 * BLOCK, HD), lambda t: (0, t, 0, 0)),
         out_shape=jax.ShapeDtypeStruct((4, 4, 2 * BLOCK, HD), BF16),
         scratch_shapes=[pltpu.VMEM((8, 64 * ROWS, HD), BF16)],
+        cost_estimate=pl.CostEstimate(flops=1000, bytes_accessed=1000, transcendentals=0),
         compiler_params=params(1),
         name="combine_rows",
     )(rho, back, swap, dkv, wkv)
@@ -355,9 +403,17 @@
     return lax.all_to_all(rows, axes, split_axis=0, concat_axis=0, tiled=True)
 
 
-def spread(rows, axes):
-    n = lax.axis_size(axes)
-    return exchange(jnp.broadcast_to(rows[None], (n,) + rows.shape), axes)
+def shifted(rows, axis, s):
+    n = lax.axis_size(axis)
+    return lax.ppermute(rows, axis, [(i, (i + s) % n) for i in range(n)])
+
+
+def gather(rows, axis):
+    return [rows] + [shifted(rows, axis, s) for s in range(1, lax.axis_size(axis))]
+
+
+def after(rows, *others):
+    return lax.optimization_barrier((rows,) + others)[0]
 
 
 def per_device(
@@ -366,8 +422,9 @@
     swap, pad = swap_matrix().astype(BF16), pad_matrix().astype(BF16)
     unpad = pad.T
     xi, zh, zl = lax.axis_index("x"), lax.axis_index("zh"), lax.axis_index("zl")
-    kv_own = jnp.concatenate([key_heads[0], value_heads[0]], axis=1)
-    kv = lax.all_gather(kv_own, SEQ, axis=0, tiled=True)
+    at = jnp.stack([xi, zh, zl])
+    kv = lax.all_gather(jnp.concatenate([key_heads[0], value_heads[0]], axis=1), SEQ, axis=0, tiled=True)
+    weights = exchange(jnp.stack([w_out, w_query], axis=1), SLAB).reshape(8, EPD, 2, HD, HD)
     routes_t = routes[0].reshape(4, 4, 2 * BLOCK, TOP).transpose(0, 1, 3, 2)
     hid_packed, grad_packed, rho = pack(
         routes_t,
@@ -375,39 +432,38 @@
         out_grad[0].reshape(4, 4, 2 * BLOCK, HD),
         swap,
     )
-    grad_rows = exchange(grad_packed, WIDE)
-    w_out_r = exchange(w_out, SLAB).reshape(8, EPD * HD, HD)
-    w_query_r = exchange(w_query, SLAB).reshape(8, EPD, HD, HD).transpose(0, 1, 3, 2).reshape(8, EPD * HD, HD)
-    hid_rows = exchange(hid_packed, WIDE)
+    grad_rows = exchange(after(grad_packed, weights), WIDE)
     q = queries[0].transpose(1, 0, 2).reshape(TOP * BLOCK, HD)
     gates = route_gates[0].T.reshape(TOP * BLOCK, 1)
     own = lax.dynamic_slice(rho, (xi, zh, 0, zl * BLOCK), (1, 1, TOP, BLOCK)).reshape(TOP * BLOCK)
     own = own // ROWS * PAD + own % ROWS
-    start = ((xi * 8 + zh * 2 + zl) * BLOCK).reshape(1)
-    prob, head_out, gated = attend_forward(start, q, kv, gates)
-
-    parts = exchange(head_sums(grad_rows, w_out_r), "zh")
+    prob, head_out, gated = attend_forward(at, q, kv, gates)
+
+    parts = head_sums(at, after(grad_rows, own), weights)
+    parts = [parts[0]] + [shifted(parts[s], "zh", s) for s in range(1, 4)]
     head_home = exchange(reduce_heads(parts, pad).reshape(64, PAD, HD), WIDE)
     slots, dkv_part = attend_backward(
         head_home.reshape(64 * PAD, HD), own.reshape(1, -1), own.reshape(-1, 1), gates, q, kv, prob, head_out, gated
     )
     mine = exchange(slots.reshape(64, PAD, 2 * HD), WIDE).reshape(64 * PAD, 2 * HD)
-    dqg = spread(unpad_rows(mine, unpad), "zh").reshape(4, 8, 8 * ROWS, 2 * HD)
-    back = exchange(route_back(dqg, w_query_r).reshape(64, 4, 8 * ROWS, HD), WIDE)
-    grad_wq, grad_wo = weight_grads(dqg, hid_rows, grad_rows)
-    grad_wq = exchange(grad_wq.reshape(16, HD, HD), SLAB).astype(F32)
-    grad_wo = exchange(grad_wo.reshape(16, HD, HD), SLAB).astype(F32)
-
-    dkv_x = exchange(dkv_part.reshape(4, 8 * BLOCK, 2 * HD), "x").astype(F32).sum(axis=0).astype(BF16)
-    dkv_own = exchange(dkv_x.reshape(8, BLOCK, 2 * HD), ("zh", "zl")).astype(F32).sum(axis=0).astype(BF16)
-    dkv = spread(spread(dkv_own, ("zh", "zl")).reshape(8 * BLOCK, 2 * HD), "x")
-    dkv = dkv.reshape(4, 4, 2 * BLOCK, 2 * HD)
+    dkv_x = lax.psum_scatter(dkv_part, "x", scatter_dimension=0, tiled=True)
+    dqg = gather(unpad_rows(mine, unpad).reshape(8, 8 * ROWS, 2 * HD), "zh")
+    hid_rows = exchange(after(hid_packed, dkv_x, *dqg), WIDE)
+    back_rows = route_back(at, dqg, weights).reshape(64, 4, 8 * ROWS, HD)
+    dkv_own = lax.psum_scatter(dkv_x, ("zh", "zl"), scatter_dimension=0, tiled=True)
+    back = exchange(after(back_rows, hid_rows, dkv_own), WIDE)
+    dkv = lax.all_gather(dkv_own, SEQ, axis=0, tiled=True)
+    dqg[0] = after(dqg[0], back_rows)
+    grads = weight_grads(at, dqg, hid_rows, grad_rows).reshape(16, 2, HD, HD)
+    grads = exchange(after(grads, back), SLAB)
+    grad_wq, grad_wo = grads[:, 0].astype(F32), grads[:, 1].astype(F32)
+
     wkv = jnp.concatenate([w_key, w_value], axis=1)
-    grad_hidden = combine(rho, back, swap, dkv, wkv).reshape(1, 4096, HD)
-    proj = lax.dot_general(
-        hidden[0], dkv.reshape(-1, 2 * HD), (((0,), (0,)), ((), ())), preferred_element_type=F32
-    )
-    proj = spread(proj.astype(BF16), GRP).astype(F32).sum(axis=0)
+    grad_hidden = combine(rho, back, swap, dkv.reshape(4, 4, 2 * BLOCK, 2 * HD), wkv).reshape(1, 4096, HD)
+    proj = projection(hidden[0], dkv)
+    proj = sum(p.astype(F32) for p in gather(proj, "dev")).astype(BF16)
+    proj = [p.astype(F32) for p in gather(proj, "node")]
+    proj = (proj[0] + proj[2]) + (proj[1] + proj[3])
     return (grad_hidden, grad_wq, grad_wo, proj[:, :HD], proj[:, HD:])
 
 

time: 478 us -> 358 us (0.75)
  blocking collectives: 150 us -> 19.1 us
  starting transfers between devices: 51.4 us -> 58.7 us
    all_to_all x6 -> x1, blocking collectives: 150 us -> 19.1 us  [exchange(): return lax.all_to_all(rows, axes, split_axis=0, concat_axis=0, tiled=True)]
    all_gather x1 -> x2, waiting for transfers between devices: 76.7 us -> 40.1 us  [the longest x1 33.8 us: per_device(): dkv = lax.all_gather(dkv_own, SEQ, axis=0, tiled=True)]
    reduce_scatter x0 -> x2, waiting for transfers between devices: none -> 29.7 us  [the longest x1 29.7 us: per_device(): lax.psum_scatter(dkv_x, ('zh', 'zl'), scatter_dimension=0, tiled=True)]
    ppermute x0 -> x10, waiting for transfers between devices: none -> 28.6 us  [shifted(): return lax.ppermute(rows, axis, [(i, (i + s) % n) for i in range(n)])]
    all_to_all x10 -> x6, waiting for transfers between devices: 113 us -> 90.1 us  [exchange(): return lax.all_to_all(rows, axes, split_axis=0, concat_axis=0, tiled=True)]
    ppermute x0 -> x10, starting transfers between devices: none -> 19.1 us  [shifted(): return lax.ppermute(rows, axis, [(i, (i + s) % n) for i in range(n)])]
    all_to_all x10 -> x6, starting transfers between devices: 51.1 us -> 39 us  [exchange(): return lax.all_to_all(rows, axes, split_axis=0, concat_axis=0, tiled=True)]
    pallas_call x3 -> x4, Pallas kernels: 17.4 us -> 20.7 us  [the longest x1 7.57 us: weight_grads(): pl.pallas_call(weights_kernel, grid=(4,), in_specs=[pl.BlockSpec(memory_s...]
  transfers between devices with their start and end apart: 11 -> 20, of which waited for: 9 -> 16; matrix products, arithmetic and copies ran while one was open for 3% -> 3% of each run, Pallas kernels for 8% -> 13%
where the time goes in v2:
time: 358 us; the launch traced here: 356 us
  waiting for transfers between devices  189 us (53%)
  starting transfers between devices  58.7 us (16%)
  Pallas kernels  55.1 us (15%)
  blocking collectives  19.1 us (5%)
  between operations  13.9 us (4%)
  local copies, waits for them, and re-layouts  9.87 us (3%)
  other arithmetic  9.83 us (3%)
    all_to_all x6, waiting for transfers between devices, exchange(): return lax.all_to_all(rows, axes, split_axis=0, concat_axis=0, tiled=True)  90.1 us
    all_to_all x6, starting transfers between devices, exchange(): return lax.all_to_all(rows, axes, split_axis=0, concat_axis=0, tiled=True)  39 us
    all_gather x1, waiting for transfers between devices, per_device(): dkv = lax.all_gather(dkv_own, SEQ, axis=0, tiled=True)  33.8 us
    reduce_scatter x1, waiting for transfers between devices, per_device(): lax.psum_scatter(dkv_x, ('zh', 'zl'), scatter_dimension=0, tiled=True)  29.7 us
    ppermute x10, waiting for transfers between devices, shifted(): return lax.ppermute(rows, axis, [(i, (i + s) % n) for i in range(n)])  28.6 us
    ppermute x10, starting transfers between devices, shifted(): return lax.ppermute(rows, axis, [(i, (i + s) % n) for i in range(n)])  19.1 us
    all_to_all x1, blocking collectives, exchange(): return lax.all_to_all(rows, axes, split_axis=0, concat_axis=0, tiled=True)  19.1 us
    pallas_call x1, Pallas kernels, pack(): pl.pallas_call(pack_kernel, grid=(4,), in_specs=[ids, slab, slab, pl.Bloc...  10.8 us
  transfers between devices with their start and end apart: 20, of which 16 were waited for; matrix products, arithmetic and copies ran while one was open for 3% of the time, Pallas kernels for 13%

profile of v2, /device:TPU:1, one launch (start us, length us, event | category | flops | bytes accessed | tf_op | source)
XLA Modules:
  0.0 356.0 jit_solution(13165264138616380647)
XLA Ops:
  7.2 2.3 pad_maximum_fusion
  9.4 6.2 %all-to-all-start = ((bf16[16,2,128,128]{3,2,1,0:T(8,128)(2,1)}), bf16[16,2,128,128]{3,2,1,0:T(8,128)(2,1)S(1)}, u32[]{:S(2)}, u32[]{:S(2)}) async-start(bf16[16,2,128,128]{3,2,1,0:T(8,128)(2,1)} %pad_maximum_fusion), calls=%async_computation | async-start | bytes 2097152 | tf_op jit(solution)/shard_map/all_to_all | solution.py:403
  15.6 10.8 %pack_rows.1 = (bf16[64,4,48,128]{3,2,1,0:T(8,128)(2,1)}, bf16[64,4,48,128]{3,2,1,0:T(8,128)(2,1)}, s32[4,4,2,256]{3,2,1,0:T(2,128)}) custom-call(s32[4,4,2,256]{3,2,1,0:T(2,128)} %bitcast.104, bf16[4,4,256,128]{3,2,1,0:T(8,128)(2,1)} %bitcast.81, bf16[4,4,256,128]{3,2,1,0:T(8,128)(2,1)} %bitcast.90, bf16[384,384]{1,0:T(8,128)(2,1)} %constant.50.clone.swap_ref), custom_call_target="tpu_custom_call" | custom-call | flops 1000 | bytes 1000 | tf_op jit(solution)/shard_map/pack_rows/pallas_call | solution.py:99
  26.5 3.7 %all-to-all-done = bf16[16,2,128,128]{3,2,1,0:T(8,128)(2,1)S(1)} async-done(((bf16[16,2,128,128]{3,2,1,0:T(8,128)(2,1)}), bf16[16,2,128,128]{3,2,1,0:T(8,128)(2,1)S(1)}, u32[]{:S(2)}, u32[]{:S(2)}) %all-to-all-start) | async-done | bytes 1048608 | tf_op jit(solution)/shard_map/all_to_all | solution.py:403
  30.1 1.0 copy-done.3
  31.1 8.1 %all-to-all-start.1 = ((bf16[64,4,48,128]{3,2,1,0:T(8,128)(2,1)}), bf16[64,4,48,128]{3,2,1,0:T(8,128)(2,1)S(1)}, u32[]{:S(2)}, u32[]{:S(2)}) async-start(bf16[64,4,48,128]{3,2,1,0:T(8,128)(2,1)} %get-tuple-element.20), calls=%async_computation.1 | async-start | bytes 6291456 | tf_op jit(solution)/shard_map/all_to_all | solution.py:403
  39.3 0.6 pad_maximum_fusion.1
  39.9 0.6 pad_add_fusion.at_ref
  40.5 0.7 compare_bitcast_fusion
  41.2 40.9 %all-to-all-done.1 = bf16[64,4,48,128]{3,2,1,0:T(8,128)(2,1)S(1)} async-done(((bf16[64,4,48,128]{3,2,1,0:T(8,128)(2,1)}), bf16[64,4,48,128]{3,2,1,0:T(8,128)(2,1)S(1)}, u32[]{:S(2)}, u32[]{:S(2)}) %all-to-all-start.1) | async-done | bytes 3145760 | tf_op jit(solution)/shard_map/all_to_all | solution.py:403
  82.1 1.7 copy-done
  83.8 5.0 %head_sums.1 = bf16[4,8,48,128]{3,2,1,0:T(8,128)(2,1)} custom-call(s32[3]{0:T(128)} %pad_add_fusion.at_ref, bf16[8,8,192,128]{3,2,1,0:T(8,128)(2,1)} %bitcast.74, bf16[8,2,2,128,128]{4,3,2,1,0:T(8,128)(2,1)} %bitcast.78), custom_call_target="tpu_custom_call" | custom-call | flops 1000 | bytes 1000 | tf_op jit(solution)/shard_map/head_sums/pallas_call | solution.py:133
  88.8 1.7 slice_bitcast_fusion.2
  90.5 5.4 %collective-permute-start.2 = (bf16[8,48,128]{2,1,0:T(8,128)(2,1)S(1)}, bf16[8,48,128]{2,1,0:T(8,128)(2,1)S(1)}, u32[]{:S(2)}, u32[]{:S(2)}) collective-permute-start(bf16[8,48,128]{2,1,0:T(8,128)(2,1)S(1)} %get-tuple-element.35), channel_id=1, source_target_pairs={{0,48},{16,0},{32,16},{48,32},{1,49},{17,1},{33,17},{49,33},{2,50}... | collective-permute-start | bytes 294920 | tf_op jit(solution)/shard_map/ppermute | solution.py:408
  95.9 1.0 collective-permute-start.1
  96.9 2.3 collective-permute-start
  99.3 6.6 %collective-permute-done.2 = bf16[8,48,128]{2,1,0:T(8,128)(2,1)S(1)} collective-permute-done((bf16[8,48,128]{2,1,0:T(8,128)(2,1)S(1)}, bf16[8,48,128]{2,1,0:T(8,128)(2,1)S(1)}, u32[]{:S(2)}, u32[]{:S(2)}) %collective-permute-start.2) | collective-permute-done | bytes 98336 | tf_op jit(solution)/shard_map/ppermute | solution.py:408
  105.8 3.0 collective-permute-done.1
  108.8 0.6 copy-done.8
  109.5 2.1 reduce_heads.1
  111.6 4.7 %all-to-all-start.2 = ((bf16[64,8,128]{2,1,0:T(8,128)(2,1)}), bf16[64,8,128]{2,1,0:T(8,128)(2,1)S(1)}, u32[]{:S(2)}, u32[]{:S(2)}) async-start(bf16[64,8,128]{2,1,0:T(8,128)(2,1)} %bitcast.94), calls=%async_computation.2 | async-start | bytes 262144 | tf_op jit(solution)/shard_map/all_to_all | solution.py:403
  116.3 0.2 reduce-scatter.3.cloned.1.call-start
  116.6 0.6 fusion.4.rho_row_ref
  117.2 0.6 copy.41
  117.8 0.8 copy.43.gate_ref
  119.1 0.7 fusion.3.rho_col_ref
  119.8 6.3 %all-gather.3.cloned.1.call-done.kv_ref = bf16[4096,256]{1,0:T(8,128)(2,1)} async-done(((bf16[128,256]{1,0:T(8,128)(2,1)}), bf16[4096,256]{1,0:T(8,128)(2,1)}) %all-gather.3.cloned.1.call-update) | async-done | bytes 2097168 | tf_op jit(solution)/shard_map/all_gather | solution.py:426
  126.1 5.1 %attend_forward.1 = (bf16[256,4096]{1,0:T(8,128)(2,1)}, f32[256,128]{1,0:T(8,128)}, bf16[256,128]{1,0:T(8,128)(2,1)}) custom-call(s32[3]{0:T(128)} %pad_add_fusion.at_ref, bf16[256,128]{1,0:T(8,128)(2,1)} %bitcast.92, bf16[4096,256]{1,0:T(8,128)(2,1)} %all-gather.3.cloned.1.call-done.kv_ref, f32[256,1]{1,0:T(8,128)} %copy.43.gate_ref), custom_call_target="tpu_custom_call" | custom-call | flops 1000 | bytes 1000 | tf_op jit(solution)/shard_map/attend_forward/pallas_call | solution.py:195
  131.2 0.7 copy-done.6
  131.8 7.2 %attend_backward.1 = (bf16[512,256]{1,0:T(8,128)(2,1)}, bf16[4096,256]{1,0:T(8,128)(2,1)}) custom-call(bf16[512,128]{1,0:T(8,128)(2,1)} %bitcast.97, s32[1,256]{1,0:T(1,128)} %fusion.4.rho_row_ref, s32[256,1]{1,0:T(8,128)} %fusion.3.rho_col_ref, f32[256,1]{1,0:T(8,128)} %copy.43.gate_ref, bf16[256,128]{1,0:T(8,128)(2,1)} %bitcast.93, ...), custom_call_target="tpu_custom_call" | custom-call | flops 1000 | bytes 1000 | tf_op jit(solution)/shard_map/attend_backward/pallas_call | solution.py:238
  139.1 19.1 %all_to_all.35 = bf16[64,8,256]{2,1,0:T(8,128)(2,1)} all-to-all(bf16[64,8,256]{2,1,0:T(8,128)(2,1)} %bitcast.99), channel_id=1, replica_groups=mesh['x'=4,'zh'=4,'zl'=2,'node'=4,'dev'=2] {'x','zl','node','dev'}, dimensions={0} | all-to-all | bytes 524288 | tf_op jit(solution)/shard_map/all_to_all | solution.py:403
  158.2 2.0 unpad_rows.1
  160.2 2.2 collective-permute-start.5
  162.4 3.0 collective-permute-start.4
  165.4 10.7 %collective-permute-done.5.d_ref = bf16[8,48,256]{2,1,0:T(8,128)(2,1)S(1)} collective-permute-done((bf16[8,48,256]{2,1,0:T(8,128)(2,1)}, bf16[8,48,256]{2,1,0:T(8,128)(2,1)S(1)}, u32[]{:S(2)}, u32[]{:S(2)}) %collective-permute-start.5) | collective-permute-done | bytes 196640 | tf_op jit(solution)/shard_map/ppermute | solution.py:408
  176.1 1.1 collective-permute-done.4.c_ref
  177.2 2.3 collective-permute-done.3.b_ref
  179.5 10.2 %all-to-all-start.4 = ((bf16[64,4,48,128]{3,2,1,0:T(8,128)(2,1)}), bf16[64,4,48,128]{3,2,1,0:T(8,128)(2,1)S(1)}, u32[]{:S(2)}, u32[]{:S(2)}) async-start(bf16[64,4,48,128]{3,2,1,0:T(8,128)(2,1)} %get-tuple-element.27), calls=%async_computation.5 | async-start | bytes 6291456 | tf_op jit(solution)/shard_map/all_to_all | solution.py:403
  189.8 0.7 reduce-scatter.5.cloned.1.call-update
  190.5 5.1 %route_back.1 = bf16[8,8,192,128]{3,2,1,0:T(8,128)(2,1)} custom-call(s32[3]{0:T(128)} %pad_add_fusion.at_ref, bf16[8,48,256]{2,1,0:T(8,128)(2,1)} %bitcast.87, bf16[8,48,256]{2,1,0:T(8,128)(2,1)} %collective-permute-done.3.b_ref, bf16[8,48,256]{2,1,0:T(8,128)(2,1)} %copy-done.5, bf16[8,48,256]{2,1,0:T(8,128)(2,1)} %copy-done.4, ...), custom_call_target="tpu_custom_call" | custom-call | flops 1000 | bytes 1000 | tf_op jit(solution)/shard_map/route_back/pallas_call | solution.py:286
  195.5 29.7 %reduce-scatter.5.cloned.1.call-done = bf16[128,256]{1,0:T(8,128)(2,1)} async-done(((bf16[1024,256]{1,0:T(8,128)(2,1)}), bf16[128,256]{1,0:T(8,128)(2,1)}) %reduce-scatter.5.cloned.1.call-update) | async-done | bytes 65552 | tf_op jit(solution)/shard_map/reduce_scatter | solution.py:453
  225.2 10.1 %all-to-all-done.4 = bf16[64,4,48,128]{3,2,1,0:T(8,128)(2,1)S(1)} async-done(((bf16[64,4,48,128]{3,2,1,0:T(8,128)(2,1)}), bf16[64,4,48,128]{3,2,1,0:T(8,128)(2,1)S(1)}, u32[]{:S(2)}, u32[]{:S(2)}) %all-to-all-start.4) | async-done | bytes 3145760 | tf_op jit(solution)/shard_map/all_to_all | solution.py:403
  235.4 1.6 copy-done.2
  237.0 5.5 %all-to-all-start.5 = ((bf16[64,4,48,128]{3,2,1,0:T(8,128)(2,1)}), bf16[64,4,48,128]{3,2,1,0:T(8,128)(2,1)S(1)}, u32[]{:S(2)}, u32[]{:S(2)}) async-start(bf16[64,4,48,128]{3,2,1,0:T(8,128)(2,1)} %bitcast.76), calls=%async_computation.7 | async-start | bytes 6291456 | tf_op jit(solution)/shard_map/all_to_all | solution.py:403
  242.5 0.3 all-gather.5.cloned.1.call-start
  242.8 0.3 all-gather.5.cloned.1.call-update
  243.1 7.6 %weight_grads.1 = bf16[8,2,2,128,128]{4,3,2,1,0:T(8,128)(2,1)} custom-call(s32[3]{0:T(128)} %pad_add_fusion.at_ref, bf16[8,48,256]{2,1,0:T(8,128)(2,1)} %bitcast.88, bf16[8,48,256]{2,1,0:T(8,128)(2,1)} %collective-permute-done.3.b_ref, bf16[8,48,256]{2,1,0:T(8,128)(2,1)} %copy-done.5, bf16[8,48,256]{2,1,0:T(8,128)(2,1)} %copy-done.4, ...), custom_call_target="tpu_custom_call" | custom-call | flops 1000 | bytes 1000 | tf_op jit(solution)/shard_map/weight_grads/pallas_call | solution.py:328
  250.7 35.4 %all-to-all-done.5.back_ref = bf16[64,4,48,128]{3,2,1,0:T(8,128)(2,1)S(1)} async-done(((bf16[64,4,48,128]{3,2,1,0:T(8,128)(2,1)}), bf16[64,4,48,128]{3,2,1,0:T(8,128)(2,1)S(1)}, u32[]{:S(2)}, u32[]{:S(2)}) %all-to-all-start.5) | async-done | bytes 3145760 | tf_op jit(solution)/shard_map/all_to_all | solution.py:403
  286.0 4.3 %all-to-all-start.6 = ((bf16[16,2,128,128]{3,2,1,0:T(8,128)(2,1)}), bf16[16,2,128,128]{3,2,1,0:T(8,128)(2,1)}, u32[]{:S(2)}, u32[]{:S(2)}) async-start(bf16[16,2,128,128]{3,2,1,0:T(8,128)(2,1)} %bitcast.83), calls=%async_computation.8 | async-start | bytes 2097152 | tf_op jit(solution)/shard_map/all_to_all | solution.py:403
  290.3 33.8 %all-gather.5.cloned.1.call-done.dkv_ref = bf16[4096,256]{1,0:T(8,128)(2,1)} async-done(((bf16[128,256]{1,0:T(8,128)(2,1)}), bf16[4096,256]{1,0:T(8,128)(2,1)}) %all-gather.5.cloned.1.call-update) | async-done | bytes 2097168 | tf_op jit(solution)/shard_map/all_gather | solution.py:455
  324.1 3.0 projection.1
  327.1 3.4 collective-permute-start.6
  330.5 1.1 collective-permute-done.6
  331.6 0.9 add_convert_fusion
  332.5 0.6 collective-permute-start.9
  333.1 1.0 collective-permute-start.8
  334.0 0.3 collective-permute-start.7
  334.3 0.6 pad_maximum_fusion.2.wkv_ref
  335.0 0.7 collective-permute-done.9
  335.7 1.7 collective-permute-done.8
  337.4 1.4 collective-permute-done.7
  338.8 0.7 fusion.5
  339.5 7.2 %combine_rows.1 = bf16[4,4,256,128]{3,2,1,0:T(8,128)(2,1)} custom-call(s32[4,4,2,256]{3,2,1,0:T(2,128)} %get-tuple-element.18.rho_ref, bf16[64,4,48,128]{3,2,1,0:T(8,128)(2,1)} %copy-done.1, bf16[384,384]{1,0:T(8,128)(2,1)} %constant.50.clone.swap_ref, bf16[4,4,256,256]{3,2,1,0:T(8,128)(2,1)} %bitcast.80, bf16[128,256]{1,0:T(8,128)(2,1)} %pad_maximum_fusion.2.wkv_ref), custom_call_target="tpu_custom_call" | custom-call | flops 1000 | bytes 1000 | tf_op jit(solution)/shard_map/combine_rows/pallas_call | solution.py:383
  346.7 2.8 fusion
  (42 shorter events, 0.7 us)
Async XLA Ops:
  9.4 20.7 %all-to-all-start = ((bf16[16,2,128,128]{3,2,1,0:T(8,128)(2,1)}), bf16[16,2,128,128]{3,2,1,0:T(8,128)(2,1)S(1)}, u32[]{:S(2)}, u32[]{:S(2)}) async-start(bf16[16,2,128,128]{3,2,1,0:T(8,128)(2,1)} %pad_maximum_fusion), calls=%async_computation | async-start | bytes 2097152 | tf_op jit(solution)/shard_map/all_to_all | solution.py:403
  30.1 1.0 copy-start.3
  30.1 9.1 %copy-start.11 = (bf16[1,128,128]{2,1,0:T(8,128)(2,1)S(1)}, bf16[1,128,128]{2,1,0:T(8,128)(2,1)}, u32[]{:S(2)}) copy-start(bf16[1,128,128]{2,1,0:T(8,128)(2,1)} %param.18) | copy-start | bytes 98308
  30.1 9.1 %copy-start.12 = (bf16[1,128,128]{2,1,0:T(8,128)(2,1)S(1)}, bf16[1,128,128]{2,1,0:T(8,128)(2,1)}, u32[]{:S(2)}) copy-start(bf16[1,128,128]{2,1,0:T(8,128)(2,1)} %param.17) | copy-start | bytes 98308
  31.1 51.0 %all-to-all-start.1 = ((bf16[64,4,48,128]{3,2,1,0:T(8,128)(2,1)}), bf16[64,4,48,128]{3,2,1,0:T(8,128)(2,1)S(1)}, u32[]{:S(2)}, u32[]{:S(2)}) async-start(bf16[64,4,48,128]{3,2,1,0:T(8,128)(2,1)} %get-tuple-element.20), calls=%async_computation.1 | async-start | bytes 6291456 | tf_op jit(solution)/shard_map/all_to_all | solution.py:403
  39.2 86.9 %all-gather.3.cloned.1.call-start = ((), (), s32[]{:S(2)}) async-start(), calls=%async_computation.9 | async-start | bytes 2162688 | tf_op jit(solution)/shard_map/all_gather | solution.py:426
  82.1 1.7 copy-start
  83.8 33.4 %copy-start.10 = (bf16[1,128,2,128]{3,2,1,0:T(2,128)(2,1)S(1)}, bf16[1,128,2,128]{3,2,1,0:T(2,128)(2,1)}, u32[]{:S(2)}) copy-start(bf16[1,128,2,128]{3,2,1,0:T(2,128)(2,1)} %param.16) | copy-start | bytes 196612
  83.8 34.0 %copy-start.15 = (f32[1,128,2]{1,2,0:T(2,128)S(1)}, f32[1,128,2]{1,2,0:T(2,128)}, u32[]{:S(2)}) copy-start(f32[1,128,2]{1,2,0:T(2,128)} %param.20) | copy-start | bytes 3076
  90.5 15.3 %collective-permute-start.2 = (bf16[8,48,128]{2,1,0:T(8,128)(2,1)S(1)}, bf16[8,48,128]{2,1,0:T(8,128)(2,1)S(1)}, u32[]{:S(2)}, u32[]{:S(2)}) collective-permute-start(bf16[8,48,128]{2,1,0:T(8,128)(2,1)S(1)} %get-tuple-element.35), channel_id=1, source_target_pairs={{0,48},{16,0},{32,16},{48,32},{1,49},{17,1},{33,17},{49,33},{2,50}... | collective-permute-start | bytes 294920 | tf_op jit(solution)/shard_map/ppermute | solution.py:408
  95.9 12.9 %collective-permute-start.1 = (bf16[8,48,128]{2,1,0:T(8,128)(2,1)S(1)}, bf16[8,48,128]{2,1,0:T(8,128)(2,1)S(1)}, u32[]{:S(2)}, u32[]{:S(2)}) collective-permute-start(bf16[8,48,128]{2,1,0:T(8,128)(2,1)S(1)} %get-tuple-element.36), channel_id=1, source_target_pairs={{0,32},{16,48},{32,0},{48,16},{1,33},{17,49},{33,1},{49,17},{2,34}... | collective-permute-start | bytes 294920 | tf_op jit(solution)/shard_map/ppermute | solution.py:408
  96.9 11.9 %collective-permute-start = (bf16[8,48,128]{2,1,0:T(8,128)(2,1)S(1)}, bf16[8,48,128]{2,1,0:T(8,128)(2,1)S(1)}, u32[]{:S(2)}, u32[]{:S(2)}) collective-permute-start(bf16[8,48,128]{2,1,0:T(8,128)(2,1)S(1)} %get-tuple-element.37), channel_id=1, source_target_pairs={{0,16},{16,32},{32,48},{48,0},{1,17},{17,33},{33,49},{49,1},{2,18}... | collective-permute-start | bytes 294920 | tf_op jit(solution)/shard_map/ppermute | solution.py:408
  105.8 3.0 copy-start.7
  108.8 0.6 copy-start.8
  108.8 0.7 copy-start.9
  111.6 19.6 %all-to-all-start.2 = ((bf16[64,8,128]{2,1,0:T(8,128)(2,1)}), bf16[64,8,128]{2,1,0:T(8,128)(2,1)S(1)}, u32[]{:S(2)}, u32[]{:S(2)}) async-start(bf16[64,8,128]{2,1,0:T(8,128)(2,1)} %bitcast.94), calls=%async_computation.2 | async-start | bytes 262144 | tf_op jit(solution)/shard_map/all_to_all | solution.py:403
  116.3 63.2 %reduce-scatter.3.cloned.1.call-start = ((), (), s32[]{:S(2)}) async-start(), calls=%async_computation.10 | async-start | bytes 2621440 | tf_op jit(solution)/shard_map/reduce_scatter | solution.py:449
  131.2 0.7 copy-start.6
  160.2 15.9 %collective-permute-start.5 = (bf16[8,48,256]{2,1,0:T(8,128)(2,1)}, bf16[8,48,256]{2,1,0:T(8,128)(2,1)S(1)}, u32[]{:S(2)}, u32[]{:S(2)}) collective-permute-start(bf16[8,48,256]{2,1,0:T(8,128)(2,1)} %bitcast.84), channel_id=1, source_target_pairs={{0,48},{16,0},{32,16},{48,32},{1,49},{17,1},{33,17},{49,33},{2,50}... | collective-permute-start | bytes 589832 | tf_op jit(solution)/shard_map/ppermute | solution.py:408
  162.4 14.8 %collective-permute-start.4 = (bf16[8,48,256]{2,1,0:T(8,128)(2,1)}, bf16[8,48,256]{2,1,0:T(8,128)(2,1)S(1)}, u32[]{:S(2)}, u32[]{:S(2)}) collective-permute-start(bf16[8,48,256]{2,1,0:T(8,128)(2,1)} %bitcast.85), channel_id=1, source_target_pairs={{0,32},{16,48},{32,0},{48,16},{1,33},{17,49},{33,1},{49,17},{2,34}... | collective-permute-start | bytes 589832 | tf_op jit(solution)/shard_map/ppermute | solution.py:408
  165.4 14.1 %collective-permute-start.3 = (bf16[8,48,256]{2,1,0:T(8,128)(2,1)}, bf16[8,48,256]{2,1,0:T(8,128)(2,1)}, u32[]{:S(2)}, u32[]{:S(2)}) collective-permute-start(bf16[8,48,256]{2,1,0:T(8,128)(2,1)} %bitcast.86), channel_id=1, source_target_pairs={{0,16},{16,32},{32,48},{48,0},{1,17},{17,33},{33,49},{49,1},{2,18}... | collective-permute-start | bytes 589832 | tf_op jit(solution)/shard_map/ppermute | solution.py:408
  176.1 3.4 copy-start.4
  177.2 2.3 copy-start.5
  179.5 55.9 %all-to-all-start.4 = ((bf16[64,4,48,128]{3,2,1,0:T(8,128)(2,1)}), bf16[64,4,48,128]{3,2,1,0:T(8,128)(2,1)S(1)}, u32[]{:S(2)}, u32[]{:S(2)}) async-start(bf16[64,4,48,128]{3,2,1,0:T(8,128)(2,1)} %get-tuple-element.27), calls=%async_computation.5 | async-start | bytes 6291456 | tf_op jit(solution)/shard_map/all_to_all | solution.py:403
  189.7 35.5 %reduce-scatter.5.cloned.1.call-start = ((), (), s32[]{:S(2)}) async-start(), calls=%async_computation.11 | async-start | bytes 589824 | tf_op jit(solution)/shard_map/reduce_scatter | solution.py:453
  235.4 1.6 copy-start.2
  237.0 49.0 %all-to-all-start.5 = ((bf16[64,4,48,128]{3,2,1,0:T(8,128)(2,1)}), bf16[64,4,48,128]{3,2,1,0:T(8,128)(2,1)S(1)}, u32[]{:S(2)}, u32[]{:S(2)}) async-start(bf16[64,4,48,128]{3,2,1,0:T(8,128)(2,1)} %bitcast.76), calls=%async_computation.7 | async-start | bytes 6291456 | tf_op jit(solution)/shard_map/all_to_all | solution.py:403
  242.5 81.6 %all-gather.5.cloned.1.call-start = ((), (), s32[]{:S(2)}) async-start(), calls=%async_computation.12 | async-start | bytes 2162688 | tf_op jit(solution)/shard_map/all_gather | solution.py:455
  250.7 83.7 %copy-start.13 = (bf16[128,128]{1,0:T(8,128)(2,1)S(1)}, bf16[128,128]{1,0:T(8,128)(2,1)}, u32[]{:S(2)}) copy-start(bf16[128,128]{1,0:T(8,128)(2,1)} %param.24) | copy-start | bytes 98308
  250.7 83.7 %copy-start.14 = (bf16[128,128]{1,0:T(8,128)(2,1)S(1)}, bf16[128,128]{1,0:T(8,128)(2,1)}, u32[]{:S(2)}) copy-start(bf16[128,128]{1,0:T(8,128)(2,1)} %param.23) | copy-start | bytes 98308
  286.0 53.4 %copy-start.1 = (bf16[64,4,48,128]{3,2,1,0:T(8,128)(2,1)}, bf16[64,4,48,128]{3,2,1,0:T(8,128)(2,1)S(1)}, u32[]{:S(2)}) copy-start(bf16[64,4,48,128]{3,2,1,0:T(8,128)(2,1)S(1)} %all-to-all-done.5.back_ref) | copy-start | bytes 9437188
  286.0 60.6 %all-to-all-start.6 = ((bf16[16,2,128,128]{3,2,1,0:T(8,128)(2,1)}), bf16[16,2,128,128]{3,2,1,0:T(8,128)(2,1)}, u32[]{:S(2)}, u32[]{:S(2)}) async-start(bf16[16,2,128,128]{3,2,1,0:T(8,128)(2,1)} %bitcast.83), calls=%async_computation.8 | async-start | bytes 2097152 | tf_op jit(solution)/shard_map/all_to_all | solution.py:403
  327.1 4.5 %collective-permute-start.6 = (bf16[128,256]{1,0:T(8,128)(2,1)}, bf16[128,256]{1,0:T(8,128)(2,1)S(1)}, u32[]{:S(2)}, u32[]{:S(2)}) collective-permute-start(bf16[128,256]{1,0:T(8,128)(2,1)} %projection.1), channel_id=1, source_target_pairs={{0,1},{1,0},{2,3},{3,2},{4,5},{5,4},{6,7},{7,6},{8,9},{9,8},{10,11... | collective-permute-start | bytes 196616 | tf_op jit(solution)/shard_map/ppermute | solution.py:408
  332.5 3.2 collective-permute-start.9
  333.1 4.3 %collective-permute-start.8 = (bf16[128,256]{1,0:T(8,128)(2,1)S(1)}, bf16[128,256]{1,0:T(8,128)(2,1)S(1)}, u32[]{:S(2)}, u32[]{:S(2)}) collective-permute-start(bf16[128,256]{1,0:T(8,128)(2,1)S(1)} %add_convert_fusion), channel_id=1, source_target_pairs={{0,2},{2,4},{4,6},{6,0},{1,3},{3,5},{5,7},{7,1},{8,10},{10,12},{12... | collective-permute-start | bytes 196616 | tf_op jit(solution)/shard_map/ppermute | solution.py:408
  334.0 4.7 %collective-permute-start.7 = (bf16[128,256]{1,0:T(8,128)(2,1)S(1)}, bf16[128,256]{1,0:T(8,128)(2,1)S(1)}, u32[]{:S(2)}, u32[]{:S(2)}) collective-permute-start(bf16[128,256]{1,0:T(8,128)(2,1)S(1)} %add_convert_fusion), channel_id=1, source_target_pairs={{0,4},{2,6},{4,0},{6,2},{1,5},{3,7},{5,1},{7,3},{8,12},{10,14},{12... | collective-permute-start | bytes 196616 | tf_op jit(solution)/shard_map/ppermute | solution.py:408
Sparse Core Ops, SparseCore 0:
  43.2 82.8 all-gather.2
  139.2 33.7 reduce-scatter.2
  193.2 31.9 reduce-scatter.4
  245.6 78.3 all-gather.4

commit v3 on v2

--- a/solution.py
+++ b/solution.py
@@ -58,59 +58,71 @@
     return jnp.dot(a, b, preferred_element_type=F32)
 
 
-def pack_kernel(routes_ref, hid_ref, grad_ref, swap_ref, hid_out, grad_out, rho_out, stage):
+def pack_rows(refs, rho_of, swap_ref, out_ref, stage):
+    row_id = lax.broadcasted_iota(jnp.int32, (64 * ROWS, BLOCK), 0)
+    for j in range(8):
+        x, span = j // 2, pl.ds((j % 2) * BLOCK, BLOCK)
+        rho_a, rho_b = rho_of(x, span)
+        pick = ((row_id == rho_a) | (row_id == rho_b)).astype(F32).astype(BF16)
+        picked = dot_nn(pick, refs[x, 0, span, :]).astype(BF16)
+        for d in range(8):
+            stage[d, j * 8 * ROWS : (j + 1) * 8 * ROWS, :] = picked[d * 8 * ROWS : (d + 1) * 8 * ROWS]
+    for d in range(8):
+        turned = dot_nn(swap_ref[...], stage[d]).astype(BF16)
+        out_ref[d * 8 : (d + 1) * 8, 0] = turned.reshape(8, 8 * ROWS, HD)
+
+
+def pack_first_kernel(routes_ref, rows_ref, swap_ref, packed_out, rho_out, stage):
     expert = lax.broadcasted_iota(jnp.int32, (EXPERTS, BLOCK), 0)
     before = (
         lax.broadcasted_iota(jnp.int32, (BLOCK, BLOCK), 0)
         < lax.broadcasted_iota(jnp.int32, (BLOCK, BLOCK), 1)
     ).astype(F32).astype(BF16)
-    row_id = lax.broadcasted_iota(jnp.int32, (64 * ROWS, BLOCK), 0)
-    for j in range(8):
-        x, span = j // 2, pl.ds((j % 2) * BLOCK, BLOCK)
+
+    def row_of(e, slot):
+        return (((e >> 1) & 7) * 8 + (e >> 4)) * ROWS + (e & 1) * CAP + slot
+
+    def rho_of(x, span):
         first = routes_ref[x, 0, 0:1, span]
         second = routes_ref[x, 0, 1:2, span]
         hot_a = (expert == first).astype(F32)
         hot_b = (expert == second).astype(F32)
         earlier = dot_nn((hot_a + hot_b).astype(BF16), before)
-        slot_a = jnp.sum(hot_a * earlier, axis=0, keepdims=True).astype(jnp.int32)
-        slot_b = jnp.sum(hot_b * earlier, axis=0, keepdims=True).astype(jnp.int32)
-
-        def row_of(e, slot):
-            return (((e >> 1) & 7) * 8 + (e >> 4)) * ROWS + (e & 1) * CAP + slot
-
-        rho_a, rho_b = row_of(first, slot_a), row_of(second, slot_b)
+        rho_a = row_of(first, jnp.sum(hot_a * earlier, axis=0, keepdims=True).astype(jnp.int32))
+        rho_b = row_of(second, jnp.sum(hot_b * earlier, axis=0, keepdims=True).astype(jnp.int32))
         rho_out[x, 0, 0:1, span] = rho_a
         rho_out[x, 0, 1:2, span] = rho_b
-        pick = ((row_id == rho_a) | (row_id == rho_b)).astype(F32).astype(BF16)
-        both = jnp.concatenate([hid_ref[x, 0, span, :], grad_ref[x, 0, span, :]], axis=1)
-        picked = dot_nn(pick, both).astype(BF16)
-        for d in range(8):
-            stage[d, j * 8 * ROWS : (j + 1) * 8 * ROWS, :] = picked[d * 8 * ROWS : (d + 1) * 8 * ROWS]
-    for d in range(8):
-        turned = dot_nn(swap_ref[...], stage[d]).astype(BF16).reshape(8, 8 * ROWS, 2 * HD)
-        hid_out[d * 8 : (d + 1) * 8, 0] = turned[:, :, :HD]
-        grad_out[d * 8 : (d + 1) * 8, 0] = turned[:, :, HD:]
-
-
-def pack(routes_t, hid, grad, swap):
-    slab = pl.BlockSpec((4, 1, 2 * BLOCK, HD), lambda t: (0, t, 0, 0))
-    rows = pl.BlockSpec((64, 1, 8 * ROWS, HD), lambda t: (0, t, 0, 0))
-    ids = pl.BlockSpec((4, 1, TOP, 2 * BLOCK), lambda t: (0, t, 0, 0))
-    return pl.pallas_call(
-        pack_kernel,
-        grid=(4,),
-        in_specs=[ids, slab, slab, pl.BlockSpec(swap.shape, lambda t: (0, 0))],
-        out_specs=[rows, rows, ids],
-        out_shape=[
-            jax.ShapeDtypeStruct((64, 4, 8 * ROWS, HD), BF16),
-            jax.ShapeDtypeStruct((64, 4, 8 * ROWS, HD), BF16),
-            jax.ShapeDtypeStruct((4, 4, TOP, 2 * BLOCK), jnp.int32),
-        ],
-        scratch_shapes=[pltpu.VMEM((8, 64 * ROWS, 2 * HD), BF16)],
+        return rho_a, rho_b
+
+    pack_rows(rows_ref, rho_of, swap_ref, packed_out, stage)
+
+
+def pack_again_kernel(rho_ref, rows_ref, swap_ref, packed_out, stage):
+    def rho_of(x, span):
+        return rho_ref[x, 0, 0:1, span], rho_ref[x, 0, 1:2, span]
+
+    pack_rows(rows_ref, rho_of, swap_ref, packed_out, stage)
+
+
+def pack(kernel, ids, rows, swap, with_rho, first, steps):
+    slab = pl.BlockSpec((4, 1, 2 * BLOCK, HD), lambda t: (0, t + first, 0, 0))
+    packed = pl.BlockSpec((64, 1, 8 * ROWS, HD), lambda t: (0, t, 0, 0))
+    id_spec = pl.BlockSpec((4, 1, TOP, 2 * BLOCK), lambda t: (0, t + first, 0, 0))
+    shapes = [
+        jax.ShapeDtypeStruct((64, steps, 8 * ROWS, HD), BF16),
+        jax.ShapeDtypeStruct((4, 4, TOP, 2 * BLOCK), jnp.int32),
+    ]
+    return pl.pallas_call(
+        kernel,
+        grid=(steps,),
+        in_specs=[id_spec, slab, pl.BlockSpec(swap.shape, lambda t: (0, 0))],
+        out_specs=[packed, id_spec][: 1 + with_rho],
+        out_shape=shapes[: 1 + with_rho],
+        scratch_shapes=[pltpu.VMEM((8, 64 * ROWS, HD), BF16)],
         cost_estimate=pl.CostEstimate(flops=1000, bytes_accessed=1000, transcendentals=0),
         compiler_params=params(1),
         name="pack_rows",
-    )(routes_t, hid, grad, swap)
+    )(ids, rows, swap)
 
 
 def second_expert(shape):
@@ -122,7 +134,7 @@
     for g in range(2):
         total = jnp.zeros((32 * ROWS, EPD * HD), F32)
         for r in range(8):
-            total += dot_nt(grad_ref[r, g], jnp.concatenate([w_ref[r, 0, 0], w_ref[r, 1, 0]], axis=0))
+            total += dot_nt(grad_ref[r, g], w_ref[r])
         own = jnp.where(second_expert((32 * ROWS, HD)), total[:, HD:], total[:, :HD])
         own = own.astype(BF16).reshape(4, 8 * ROWS, HD)
         for t in range(4):
@@ -136,7 +148,7 @@
         in_specs=[
             pl.BlockSpec(memory_space=pltpu.SMEM),
             pl.BlockSpec((8, 2, 32 * ROWS, HD), lambda i: (0, i, 0, 0)),
-            pl.BlockSpec((8, EPD, 1, HD, HD), lambda i: (0, 0, 0, 0, 0)),
+            pl.BlockSpec((8, EPD * HD, HD), lambda i: (0, 0, 0)),
         ],
         out_specs=pl.BlockSpec((4, 2, 8 * ROWS, HD), lambda i: (0, i, 0, 0)),
         out_shape=jax.ShapeDtypeStruct((4, 8, 8 * ROWS, HD), BF16),
@@ -255,7 +267,7 @@
     return pl.pallas_call(
         unpad_kernel,
         out_shape=jax.ShapeDtypeStruct((64 * ROWS, 2 * HD), BF16),
-        cost_estimate=pl.CostEstimate(flops=1000, bytes_accessed=1000, transcendentals=0),
+        cost_estimate=pl.CostEstimate(flops=10000000000, bytes_accessed=4000000, transcendentals=0),
         compiler_params=params(0),
         name="unpad_rows",
     )(rows, unpad)
@@ -278,7 +290,7 @@
     for g in range(2):
         dq = by_expert(dqg_ref[:, g, :, :HD].reshape(32 * ROWS, HD))
         for r in range(8):
-            w = jnp.concatenate([w_ref[r, 0, 0], w_ref[r, 1, 0]], axis=1)
+            w = jnp.concatenate([w_ref[r, 0], w_ref[r, 1]], axis=1)
             out_ref[r, g] = dot_nt(dq, w).astype(BF16)
 
 
@@ -288,7 +300,7 @@
         grid=(4,),
         in_specs=[pl.BlockSpec(memory_space=pltpu.SMEM)]
         + [pl.BlockSpec((2, 8 * ROWS, 2 * HD), lambda i: (i, 0, 0))] * 4
-        + [pl.BlockSpec((8, EPD, 1, HD, HD), lambda i: (0, 0, 1, 0, 0))],
+        + [pl.BlockSpec((8, EPD, HD, HD), lambda i: (0, 0, 0, 0))],
         out_specs=pl.BlockSpec((8, 2, 32 * ROWS, HD), lambda i: (0, i, 0, 0)),
         out_shape=jax.ShapeDtypeStruct((8, 8, 32 * ROWS, HD), BF16),
         scratch_shapes=[pltpu.VMEM((4, 2, 8 * ROWS, 2 * HD), BF16)],
@@ -298,9 +310,7 @@
     )(at, *dqg, weights)
 
 
-def weights_kernel(
-    at_ref, a_ref, b_ref, c_ref, d_ref, hid_ref, grad_ref, out_ref, dqg_ref, wq_acc, wo_acc
-):
+def early_weights_kernel(at_ref, a_ref, b_ref, c_ref, d_ref, hid_ref, grad_ref, wq_acc, wo_acc, dqg_ref):
     in_order(at_ref, (a_ref, b_ref, c_ref, d_ref), dqg_ref)
 
     @pl.when(pl.program_id(0) == 0)
@@ -309,44 +319,82 @@
         wo_acc[...] = jnp.zeros_like(wo_acc)
 
     for g in range(2):
-        dq = by_expert(dqg_ref[:, g, :, :HD].reshape(32 * ROWS, HD))
+        dq = by_expert(dqg_ref[:2, g, :, :HD].reshape(16 * ROWS, HD))
         gated = by_expert(dqg_ref[:, g, :, HD:].reshape(32 * ROWS, HD))
         for r in range(8):
             wq_acc[r] += dot_tn(hid_ref[r, g], dq)
             wo_acc[r] += dot_tn(gated, grad_ref[r, g])
+
+
+def late_weights_kernel(at_ref, a_ref, b_ref, c_ref, d_ref, hid_ref, wq_ref, wo_ref, out_ref, dqg_ref, wq_acc):
+    in_order(at_ref, (a_ref, b_ref, c_ref, d_ref), dqg_ref)
+
+    @pl.when(pl.program_id(0) == 0)
+    def _():
+        wq_acc[...] = wq_ref[...]
+        for r in range(8):
+            for k in range(EPD):
+                out_ref[r, k, 1] = wo_ref[r, k * HD : (k + 1) * HD, :].astype(BF16)
+
+    for g in range(2):
+        dq = by_expert(dqg_ref[2:, g, :, :HD].reshape(16 * ROWS, HD))
+        for r in range(8):
+            wq_acc[r] += dot_tn(hid_ref[r, g], dq)
 
     @pl.when(pl.program_id(0) == 3)
     def _():
         for r in range(8):
             for k in range(EPD):
                 out_ref[r, k, 0] = wq_acc[r, :, k * HD : (k + 1) * HD].astype(BF16)
-                out_ref[r, k, 1] = wo_acc[r, k * HD : (k + 1) * HD, :].astype(BF16)
-
-
-def weight_grads(at, dqg, hid_rows, grad_rows):
-    rows = pl.BlockSpec((8, 2, 32 * ROWS, HD), lambda i: (0, i, 0, 0))
-    return pl.pallas_call(
-        weights_kernel,
+
+
+def weights_call(kernel, name, operands, in_specs, out_shapes, scratch):
+    def whole(shape):
+        return pl.BlockSpec(shape, lambda i: (0,) * len(shape))
+
+    return pl.pallas_call(
+        kernel,
         grid=(4,),
         in_specs=[pl.BlockSpec(memory_space=pltpu.SMEM)]
         + [pl.BlockSpec((2, 8 * ROWS, 2 * HD), lambda i: (i, 0, 0))] * 4
-        + [rows, rows],
-        out_specs=pl.BlockSpec((8, EPD, 2, HD, HD), lambda i: (0, 0, 0, 0, 0)),
-        out_shape=jax.ShapeDtypeStruct((8, EPD, 2, HD, HD), BF16),
-        scratch_shapes=[
-            pltpu.VMEM((4, 2, 8 * ROWS, 2 * HD), BF16),
-            pltpu.VMEM((8, HD, EPD * HD), F32),
-            pltpu.VMEM((8, EPD * HD, HD), F32),
-        ],
+        + in_specs
+        + [whole(o.shape) for o in operands[5 + len(in_specs) :]],
+        out_specs=[whole(o.shape) for o in out_shapes],
+        out_shape=out_shapes,
+        scratch_shapes=[pltpu.VMEM((4, 2, 8 * ROWS, 2 * HD), BF16)] + scratch,
         cost_estimate=pl.CostEstimate(flops=1000, bytes_accessed=1000, transcendentals=0),
         compiler_params=params(1),
-        name="weight_grads",
-    )(
-        at,
-        *dqg,
-        hid_rows.reshape(8, 8, 32 * ROWS, HD),
-        grad_rows.reshape(8, 8, 32 * ROWS, HD),
+        name=name,
+    )(*operands)
+
+
+def early_weights(at, dqg, hid_a, grad_rows):
+    return weights_call(
+        early_weights_kernel,
+        "early_weights",
+        [at, *dqg, hid_a.reshape(8, 8, 16 * ROWS, HD), grad_rows.reshape(8, 8, 32 * ROWS, HD)],
+        [
+            pl.BlockSpec((8, 2, 16 * ROWS, HD), lambda i: (0, i, 0, 0)),
+            pl.BlockSpec((8, 2, 32 * ROWS, HD), lambda i: (0, i, 0, 0)),
+        ],
+        [
+            jax.ShapeDtypeStruct((8, HD, EPD * HD), F32),
+            jax.ShapeDtypeStruct((8, EPD * HD, HD), F32),
+        ],
+        [],
     )
+
+
+def late_weights(at, dqg, hid_b, wq, wo):
+    (out,) = weights_call(
+        late_weights_kernel,
+        "late_weights",
+        [at, *dqg, hid_b.reshape(8, 8, 16 * ROWS, HD), wq, wo],
+        [pl.BlockSpec((8, 2, 16 * ROWS, HD), lambda i: (0, i, 0, 0))],
+        [jax.ShapeDtypeStruct((8, EPD, 2, HD, HD), BF16)],
+        [pltpu.VMEM((8, HD, EPD * HD), F32)],
+    )
+    return out
 
 
 def projection_kernel(hid_ref, dkv_ref, out_ref):
@@ -363,7 +411,7 @@
     )(hid, dkv)
 
 
-def combine_kernel(rho_ref, back_ref, swap_ref, dkv_ref, wkv_ref, out_ref, stage):
+def unpack_kernel(rho_ref, back_ref, swap_ref, out_ref, stage):
     for d in range(8):
         rows = back_ref[d * 8 : (d + 1) * 8, 0].reshape(64 * ROWS, HD)
         turned = dot_nn(swap_ref[...], rows).astype(BF16)
@@ -375,28 +423,48 @@
         rho_a = rho_ref[x, 0, 0:1, span]
         rho_b = rho_ref[x, 0, 1:2, span]
         pick = ((row_id == rho_a) | (row_id == rho_b)).astype(F32).astype(BF16)
-        total = dot_tn(pick, stage[j]) + dot_nt(dkv_ref[x, 0, span, :], wkv_ref[...])
-        out_ref[x, 0, span, :] = total.astype(BF16)
-
-
-def combine(rho, back, swap, dkv, wkv):
-    return pl.pallas_call(
-        combine_kernel,
+        out_ref[x, 0, span, :] = dot_tn(pick, stage[j])
+
+
+def unpack(rho, back, swap):
+    return pl.pallas_call(
+        unpack_kernel,
         grid=(4,),
         in_specs=[
             pl.BlockSpec((4, 1, TOP, 2 * BLOCK), lambda t: (0, t, 0, 0)),
             pl.BlockSpec((64, 1, 8 * ROWS, HD), lambda t: (0, t, 0, 0)),
             pl.BlockSpec(swap.shape, lambda t: (0, 0)),
+        ],
+        out_specs=pl.BlockSpec((4, 1, 2 * BLOCK, HD), lambda t: (0, t, 0, 0)),
+        out_shape=jax.ShapeDtypeStruct((4, 4, 2 * BLOCK, HD), F32),
+        scratch_shapes=[pltpu.VMEM((8, 64 * ROWS, HD), BF16)],
+        cost_estimate=pl.CostEstimate(flops=1000, bytes_accessed=1000, transcendentals=0),
+        compiler_params=params(1),
+        name="unpack_rows",
+    )(rho, back, swap)
+
+
+def finish_kernel(rows_ref, dkv_ref, wkv_ref, out_ref):
+    for x in range(4):
+        total = rows_ref[x, 0] + dot_nt(dkv_ref[x, 0], wkv_ref[...])
+        out_ref[x, 0] = total.astype(BF16)
+
+
+def finish(rows, dkv, wkv):
+    return pl.pallas_call(
+        finish_kernel,
+        grid=(4,),
+        in_specs=[
+            pl.BlockSpec((4, 1, 2 * BLOCK, HD), lambda t: (0, t, 0, 0)),
             pl.BlockSpec((4, 1, 2 * BLOCK, 2 * HD), lambda t: (0, t, 0, 0)),
             pl.BlockSpec(wkv.shape, lambda t: (0, 0)),
         ],
         out_specs=pl.BlockSpec((4, 1, 2 * BLOCK, HD), lambda t: (0, t, 0, 0)),
         out_shape=jax.ShapeDtypeStruct((4, 4, 2 * BLOCK, HD), BF16),
-        scratch_shapes=[pltpu.VMEM((8, 64 * ROWS, HD), BF16)],
-        cost_estimate=pl.CostEstimate(flops=1000, bytes_accessed=1000, transcendentals=0),
+        cost_estimate=pl.CostEstimate(flops=5000000000, bytes_accessed=10000000, transcendentals=0),
         compiler_params=params(1),
-        name="combine_rows",
-    )(rho, back, swap, dkv, wkv)
+        name="finish_rows",
+    )(rows, dkv, wkv)
 
 
 def exchange(rows, axes):
@@ -424,45 +492,54 @@
     xi, zh, zl = lax.axis_index("x"), lax.axis_index("zh"), lax.axis_index("zl")
     at = jnp.stack([xi, zh, zl])
     kv = lax.all_gather(jnp.concatenate([key_heads[0], value_heads[0]], axis=1), SEQ, axis=0, tiled=True)
-    weights = exchange(jnp.stack([w_out, w_query], axis=1), SLAB).reshape(8, EPD, 2, HD, HD)
     routes_t = routes[0].reshape(4, 4, 2 * BLOCK, TOP).transpose(0, 1, 3, 2)
-    hid_packed, grad_packed, rho = pack(
-        routes_t,
-        hidden[0].reshape(4, 4, 2 * BLOCK, HD),
-        out_grad[0].reshape(4, 4, 2 * BLOCK, HD),
-        swap,
-    )
-    grad_rows = exchange(after(grad_packed, weights), WIDE)
+    slab = (4, 4, 2 * BLOCK, HD)
+    grad_packed, rho = pack(pack_first_kernel, routes_t, out_grad[0].reshape(slab), swap, 1, 0, 4)
+    w_out_r = exchange(w_out, SLAB).reshape(8, EPD * HD, HD)
+    grad_rows = exchange(after(grad_packed, w_out_r), WIDE)
+    (hid_a,) = pack(pack_again_kernel, rho, hidden[0].reshape(slab), swap, 0, 0, 2)
+    (hid_b,) = pack(pack_again_kernel, rho, hidden[0].reshape(slab), swap, 0, 2, 2)
     q = queries[0].transpose(1, 0, 2).reshape(TOP * BLOCK, HD)
     gates = route_gates[0].T.reshape(TOP * BLOCK, 1)
     own = lax.dynamic_slice(rho, (xi, zh, 0, zl * BLOCK), (1, 1, TOP, BLOCK)).reshape(TOP * BLOCK)
     own = own // ROWS * PAD + own % ROWS
-    prob, head_out, gated = attend_forward(at, q, kv, gates)
-
-    parts = head_sums(at, after(grad_rows, own), weights)
+    own_row, own_col = own.reshape(1, -1), own.reshape(-1, 1)
+
+    parts = head_sums(at, after(grad_rows, own_row, own_col, q, gates, hid_a, hid_b), w_out_r)
+    w_query_r = exchange(after(w_query, grad_rows, own_row, own_col, q, gates, hid_a, hid_b), SLAB).reshape(8, EPD, HD, HD)
+    parts = list(lax.optimization_barrier((*[parts[s] for s in range(4)], w_query_r)))[:4]
     parts = [parts[0]] + [shifted(parts[s], "zh", s) for s in range(1, 4)]
     head_home = exchange(reduce_heads(parts, pad).reshape(64, PAD, HD), WIDE)
+    hid_a = exchange(after(hid_a, head_home), WIDE)
+    prob, head_out, gated = attend_forward(at, after(q, head_home), kv, gates)
     slots, dkv_part = attend_backward(
-        head_home.reshape(64 * PAD, HD), own.reshape(1, -1), own.reshape(-1, 1), gates, q, kv, prob, head_out, gated
+        head_home.reshape(64 * PAD, HD), own_row, own_col, gates, q, kv,
+        prob, head_out, gated,
     )
-    mine = exchange(slots.reshape(64, PAD, 2 * HD), WIDE).reshape(64 * PAD, 2 * HD)
     dkv_x = lax.psum_scatter(dkv_part, "x", scatter_dimension=0, tiled=True)
-    dqg = gather(unpad_rows(mine, unpad).reshape(8, 8 * ROWS, 2 * HD), "zh")
-    hid_rows = exchange(after(hid_packed, dkv_x, *dqg), WIDE)
-    back_rows = route_back(at, dqg, weights).reshape(64, 4, 8 * ROWS, HD)
-    dkv_own = lax.psum_scatter(dkv_x, ("zh", "zl"), scatter_dimension=0, tiled=True)
-    back = exchange(after(back_rows, hid_rows, dkv_own), WIDE)
+    mine = exchange(after(slots, hid_a).reshape(64, PAD, 2 * HD), WIDE).reshape(64 * PAD, 2 * HD)
+    dqg = unpad_rows(mine, unpad).reshape(8, 8 * ROWS, 2 * HD)
+    dqg = gather(dqg, "zh")
+    dkv_z = exchange(after(dkv_x, *dqg).reshape(8, BLOCK, 2 * HD), ("zh", "zl"))
+    dkv_own = dkv_z.astype(F32).sum(axis=0).astype(BF16)
     dkv = lax.all_gather(dkv_own, SEQ, axis=0, tiled=True)
+    back_rows = route_back(at, dqg, w_query_r).reshape(64, 4, 8 * ROWS, HD)
+    back = exchange(after(back_rows, dkv_z), WIDE)
+    hid_b = exchange(after(hid_b, back), WIDE)
+    unpacked = unpack(rho, back, swap)
     dqg[0] = after(dqg[0], back_rows)
-    grads = weight_grads(at, dqg, hid_rows, grad_rows).reshape(16, 2, HD, HD)
-    grads = exchange(after(grads, back), SLAB)
+    wq, wo = early_weights(at, dqg, hid_a, grad_rows)
+    dqg[0] = after(dqg[0], unpacked, wq)
+    grads = late_weights(at, dqg, hid_b, wq, wo).reshape(16, 2, HD, HD)
+    grads = exchange(grads, SLAB)
     grad_wq, grad_wo = grads[:, 0].astype(F32), grads[:, 1].astype(F32)
 
     wkv = jnp.concatenate([w_key, w_value], axis=1)
-    grad_hidden = combine(rho, back, swap, dkv.reshape(4, 4, 2 * BLOCK, 2 * HD), wkv).reshape(1, 4096, HD)
     proj = projection(hidden[0], dkv)
+    grad_hidden = finish(unpacked, dkv.reshape(4, 4, 2 * BLOCK, 2 * HD), wkv).reshape(1, 4096, HD)
     proj = sum(p.astype(F32) for p in gather(proj, "dev")).astype(BF16)
     proj = [p.astype(F32) for p in gather(proj, "node")]
+    proj[0] = after(proj[0], grad_hidden)
     proj = (proj[0] + proj[2]) + (proj[1] + proj[3])
     return (grad_hidden, grad_wq, grad_wo, proj[:, :HD], proj[:, HD:])
 

time: 358 us -> 341 us (0.953)
  waiting for transfers between devices: 189 us -> 136 us
  Pallas kernels: 55.1 us -> 72 us
  starting transfers between devices: 58.7 us -> 73.3 us
  blocking collectives: 19.1 us -> 29.7 us
    all_gather x1, waiting for transfers between devices: 33.8 us -> 3.09 us  [per_device(): dkv = lax.all_gather(dkv_own, SEQ, axis=0, tiled=True)]
    reduce_scatter x1 -> x0, waiting for transfers between devices: 29.7 us -> none  [per_device(): lax.psum_scatter(dkv_x, ('zh', 'zl'), scatter_dimension=0, tiled=True)]
    all_to_all x6 -> x8, waiting for transfers between devices: 90.1 us -> 110 us  [exchange(): return lax.all_to_all(rows, axes, split_axis=0, concat_axis=0, tiled=True)]
    pallas_call x3 -> x7, Pallas kernels: 25.6 us -> 42.5 us  [the longest x3 18.1 us: pack(): pl.pallas_call(kernel, grid=(steps,), in_specs=[id_spec, slab, pl.BlockSp...]
    all_to_all x1 -> x2, blocking collectives: 19.1 us -> 29.7 us  [exchange(): return lax.all_to_all(rows, axes, split_axis=0, concat_axis=0, tiled=True)]
    all_to_all x6 -> x8, starting transfers between devices: 39 us -> 48.5 us  [exchange(): return lax.all_to_all(rows, axes, split_axis=0, concat_axis=0, tiled=True)]
    all_gather x1, waiting for transfers between devices: 6.29 us -> 0.01 us  [per_device(): lax.all_gather(jnp.concatenate([key_heads[0], value_heads[0]], axis=1), S...]
    ppermute x10, waiting for transfers between devices: 28.6 us -> 22.9 us  [shifted(): return lax.ppermute(rows, axis, [(i, (i + s) % n) for i in range(n)])]
  transfers between devices with their start and end apart: 20 -> 21, of which waited for: 16 -> 14; matrix products, arithmetic and copies ran while one was open for 3% -> 3% of each run, Pallas kernels for 13% -> 21%
where the time goes in v3:
time: 341 us; the launch traced here: 339 us
  waiting for transfers between devices  136 us (40%)
  starting transfers between devices  73.3 us (21%)
  Pallas kernels  72 us (21%)
  blocking collectives  29.7 us (9%)
  between operations  14 us (4%)
  other arithmetic  8.1 us (2%)
  local copies, waits for them, and re-layouts  6.52 us (2%)
    all_to_all x8, waiting for transfers between devices, exchange(): return lax.all_to_all(rows, axes, split_axis=0, concat_axis=0, tiled=True)  110 us
    all_to_all x8, starting transfers between devices, exchange(): return lax.all_to_all(rows, axes, split_axis=0, concat_axis=0, tiled=True)  48.5 us
    all_to_all x2, blocking collectives, exchange(): return lax.all_to_all(rows, axes, split_axis=0, concat_axis=0, tiled=True)  29.7 us
    ppermute x10, starting transfers between devices, shifted(): return lax.ppermute(rows, axis, [(i, (i + s) % n) for i in range(n)])  24.5 us
    ppermute x10, waiting for transfers between devices, shifted(): return lax.ppermute(rows, axis, [(i, (i + s) % n) for i in range(n)])  22.9 us
    pallas_call x3, Pallas kernels, pack(): pl.pallas_call(kernel, grid=(steps,), in_specs=[id_spec, slab, pl.BlockSp...  18.1 us
    pallas_call x2, Pallas kernels, weights_call(): pl.pallas_call(kernel, grid=(4,), in_specs=[pl.BlockSpec(memory_space=plt...  13.1 us
    pallas_call x1, Pallas kernels, attend_backward(): pl.pallas_call(backward_kernel, out_shape=[jax.ShapeDtypeStruct((64 * PAD...  7.24 us
  transfers between devices with their start and end apart: 21, of which 14 were waited for; matrix products, arithmetic and copies ran while one was open for 3% of the time, Pallas kernels for 21%

profile of v3, /device:TPU:1, one launch (start us, length us, event | category | flops | bytes accessed | tf_op | source)
XLA Modules:
  0.0 339.2 jit_solution(10618260940288546818)
XLA Ops:
  7.2 6.2 %all-to-all-start = ((bf16[16,128,128]{2,1,0:T(8,128)(2,1)}), bf16[16,128,128]{2,1,0:T(8,128)(2,1)S(1)}, u32[]{:S(2)}, u32[]{:S(2)}) async-start(bf16[16,128,128]{2,1,0:T(8,128)(2,1)} %param.22), calls=%async_computation | async-start | bytes 1048576 | tf_op jit(solution)/shard_map/all_to_all | solution.py:471
  13.4 9.4 %pack_rows.3 = (bf16[64,4,48,128]{3,2,1,0:T(8,128)(2,1)}, s32[4,4,2,256]{3,2,1,0:T(2,128)}) custom-call(s32[4,4,2,256]{3,2,1,0:T(2,128)} %bitcast.106, bf16[4,4,256,128]{3,2,1,0:T(8,128)(2,1)} %bitcast.93, bf16[384,384]{1,0:T(8,128)(2,1)} %constant.53.clone.swap_ref), custom_call_target="tpu_custom_call" | custom-call | flops 1000 | bytes 1000 | tf_op jit(solution)/shard_map/pack_rows/pallas_call | solution.py:115
  22.9 0.8 copy-done.3
  23.6 9.8 %all-to-all-start.1 = ((bf16[64,4,48,128]{3,2,1,0:T(8,128)(2,1)}), bf16[64,4,48,128]{3,2,1,0:T(8,128)(2,1)S(1)}, u32[]{:S(2)}, u32[]{:S(2)}) async-start(bf16[64,4,48,128]{3,2,1,0:T(8,128)(2,1)} %get-tuple-element.32), calls=%async_computation.1 | async-start | bytes 6291456 | tf_op jit(solution)/shard_map/all_to_all | solution.py:471
  33.5 0.6 pad_maximum_fusion
  34.2 4.3 %pack_rows.5 = bf16[64,2,48,128]{3,2,1,0:T(8,128)(2,1)} custom-call(s32[4,4,2,256]{3,2,1,0:T(2,128)} %get-tuple-element.30.rho_ref, bf16[4,4,256,128]{3,2,1,0:T(8,128)(2,1)} %bitcast.80, bf16[384,384]{1,0:T(8,128)(2,1)} %constant.53.clone.swap_ref), custom_call_target="tpu_custom_call" | custom-call | flops 1000 | bytes 1000 | tf_op jit(solution)/shard_map/pack_rows/pallas_call | solution.py:115
  38.5 4.3 %pack_rows.4 = bf16[64,2,48,128]{3,2,1,0:T(8,128)(2,1)} custom-call(s32[4,4,2,256]{3,2,1,0:T(2,128)} %get-tuple-element.30.rho_ref, bf16[4,4,256,128]{3,2,1,0:T(8,128)(2,1)} %bitcast.81, bf16[384,384]{1,0:T(8,128)(2,1)} %constant.53.clone.swap_ref), custom_call_target="tpu_custom_call" | custom-call | flops 1000 | bytes 1000 | tf_op jit(solution)/shard_map/pack_rows/pallas_call | solution.py:115
  42.9 0.6 copy.39
  43.5 0.6 compare_bitcast_fusion
  44.6 0.6 fusion.4.rho_row_ref
  45.2 0.7 fusion.3.rho_col_ref
  45.9 30.5 %all-to-all-done.1 = bf16[64,4,48,128]{3,2,1,0:T(8,128)(2,1)S(1)} async-done(((bf16[64,4,48,128]{3,2,1,0:T(8,128)(2,1)}), bf16[64,4,48,128]{3,2,1,0:T(8,128)(2,1)S(1)}, u32[]{:S(2)}, u32[]{:S(2)}) %all-to-all-start.1) | async-done | bytes 3145760 | tf_op jit(solution)/shard_map/all_to_all | solution.py:471
  76.4 4.1 %all-to-all-start.2 = ((bf16[16,128,128]{2,1,0:T(8,128)(2,1)}), bf16[16,128,128]{2,1,0:T(8,128)(2,1)}, u32[]{:S(2)}, u32[]{:S(2)}) async-start(bf16[16,128,128]{2,1,0:T(8,128)(2,1)} %param.21), calls=%async_computation.2 | async-start | bytes 1048576 | tf_op jit(solution)/shard_map/all_to_all | solution.py:471
  80.6 0.7 pad_add_fusion.at_ref
  81.2 4.9 %head_sums.1 = bf16[4,8,48,128]{3,2,1,0:T(8,128)(2,1)} custom-call(s32[3]{0:T(128)} %pad_add_fusion.at_ref, bf16[8,8,192,128]{3,2,1,0:T(8,128)(2,1)} %bitcast.77, bf16[8,256,128]{2,1,0:T(8,128)(2,1)} %bitcast.85), custom_call_target="tpu_custom_call" | custom-call | flops 1000 | bytes 1000 | tf_op jit(solution)/shard_map/head_sums/pallas_call | solution.py:145
  86.2 1.7 slice_bitcast_fusion.2
  87.9 2.4 all-to-all-done.2
  90.3 3.3 collective-permute-start
  93.6 4.4 %collective-permute-start.1 = (bf16[8,48,128]{2,1,0:T(8,128)(2,1)S(1)}, bf16[8,48,128]{2,1,0:T(8,128)(2,1)S(1)}, u32[]{:S(2)}, u32[]{:S(2)}) collective-permute-start(bf16[8,48,128]{2,1,0:T(8,128)(2,1)S(1)} %get-tuple-element.37), channel_id=1, source_target_pairs={{0,32},{16,48},{32,0},{48,16},{1,33},{17,49},{33,1},{49,17},{2,34}... | collective-permute-start | bytes 294920 | tf_op jit(solution)/shard_map/ppermute | solution.py:476
  98.0 2.4 collective-permute-start.2
  100.4 9.1 %collective-permute-done.1 = bf16[8,48,128]{2,1,0:T(8,128)(2,1)S(1)} collective-permute-done((bf16[8,48,128]{2,1,0:T(8,128)(2,1)S(1)}, bf16[8,48,128]{2,1,0:T(8,128)(2,1)S(1)}, u32[]{:S(2)}, u32[]{:S(2)}) %collective-permute-start.1) | collective-permute-done | bytes 98336 | tf_op jit(solution)/shard_map/ppermute | solution.py:476
  109.5 0.4 collective-permute-done.2
  110.1 0.5 copy-done.11
  110.6 2.2 reduce_heads.1
  112.8 15.3 %all_to_all.50 = bf16[64,8,128]{2,1,0:T(8,128)(2,1)} all-to-all(bf16[64,8,128]{2,1,0:T(8,128)(2,1)} %bitcast.96), channel_id=1, replica_groups=mesh['x'=4,'zh'=4,'zl'=2,'node'=4,'dev'=2] {'x','zl','node','dev'}, dimensions={0} | all-to-all | bytes 262144 | tf_op jit(solution)/shard_map/all_to_all | solution.py:471
  128.0 4.5 %all-to-all-start.4 = ((bf16[64,2,48,128]{3,2,1,0:T(8,128)(2,1)}), bf16[64,2,48,128]{3,2,1,0:T(8,128)(2,1)S(1)}, u32[]{:S(2)}, u32[]{:S(2)}) async-start(bf16[64,2,48,128]{3,2,1,0:T(8,128)(2,1)} %pack_rows.4), calls=%async_computation.4 | async-start | bytes 3145728 | tf_op jit(solution)/shard_map/all_to_all | solution.py:471
  132.5 0.2 reduce-scatter.2.cloned.1.call-start
  132.8 0.8 copy.41.gate_ref
  133.6 5.0 %attend_forward.1 = (bf16[256,4096]{1,0:T(8,128)(2,1)}, f32[256,128]{1,0:T(8,128)}, bf16[256,128]{1,0:T(8,128)(2,1)}) custom-call(s32[3]{0:T(128)} %pad_add_fusion.at_ref, bf16[256,128]{1,0:T(8,128)(2,1)} %bitcast.94, bf16[4096,256]{1,0:T(8,128)(2,1)} %all-gather.3.cloned.1.call-done.kv_ref, f32[256,1]{1,0:T(8,128)} %copy.41.gate_ref), custom_call_target="tpu_custom_call" | custom-call | flops 1000 | bytes 1000 | tf_op jit(solution)/shard_map/attend_forward/pallas_call | solution.py:207
  138.6 7.2 %attend_backward.1 = (bf16[512,256]{1,0:T(8,128)(2,1)}, bf16[4096,256]{1,0:T(8,128)(2,1)}) custom-call(bf16[512,128]{1,0:T(8,128)(2,1)} %bitcast.98, s32[1,256]{1,0:T(1,128)} %fusion.4.rho_row_ref, s32[256,1]{1,0:T(8,128)} %fusion.3.rho_col_ref, f32[256,1]{1,0:T(8,128)} %copy.41.gate_ref, bf16[256,128]{1,0:T(8,128)(2,1)} %bitcast.95, ...), custom_call_target="tpu_custom_call" | custom-call | flops 1000 | bytes 1000 | tf_op jit(solution)/shard_map/attend_backward/pallas_call | solution.py:250
  145.9 10.3 %all-to-all-done.4 = bf16[64,2,48,128]{3,2,1,0:T(8,128)(2,1)S(1)} async-done(((bf16[64,2,48,128]{3,2,1,0:T(8,128)(2,1)}), bf16[64,2,48,128]{3,2,1,0:T(8,128)(2,1)S(1)}, u32[]{:S(2)}, u32[]{:S(2)}) %all-to-all-start.4) | async-done | bytes 1572896 | tf_op jit(solution)/shard_map/all_to_all | solution.py:471
  156.1 14.4 %all_to_all.51 = bf16[64,8,256]{2,1,0:T(8,128)(2,1)} all-to-all(bf16[64,8,256]{2,1,0:T(8,128)(2,1)S(1)} %bitcast.100), channel_id=1, replica_groups=mesh['x'=4,'zh'=4,'zl'=2,'node'=4,'dev'=2] {'x','zl','node','dev'}, dimensions={0} | all-to-all | bytes 524288 | tf_op jit(solution)/shard_map/all_to_all | solution.py:471
  170.5 2.0 unpad_rows.1
  172.6 2.9 collective-permute-start.5
  175.4 1.1 collective-permute-start.4
  176.5 2.0 collective-permute-start.3
  178.5 5.3 %collective-permute-done.5.d_ref = bf16[8,48,256]{2,1,0:T(8,128)(2,1)S(1)} collective-permute-done((bf16[8,48,256]{2,1,0:T(8,128)(2,1)}, bf16[8,48,256]{2,1,0:T(8,128)(2,1)S(1)}, u32[]{:S(2)}, u32[]{:S(2)}) %collective-permute-start.5) | collective-permute-done | bytes 196640 | tf_op jit(solution)/shard_map/ppermute | solution.py:476
  183.8 4.8 %collective-permute-done.4.c_ref = bf16[8,48,256]{2,1,0:T(8,128)(2,1)S(1)} collective-permute-done((bf16[8,48,256]{2,1,0:T(8,128)(2,1)}, bf16[8,48,256]{2,1,0:T(8,128)(2,1)S(1)}, u32[]{:S(2)}, u32[]{:S(2)}) %collective-permute-start.4) | collective-permute-done | bytes 196640 | tf_op jit(solution)/shard_map/ppermute | solution.py:476
  188.6 2.7 collective-permute-done.3.b_ref
  191.3 10.0 %all-to-all-start.6 = ((bf16[8,128,256]{2,1,0:T(8,128)(2,1)}), bf16[8,128,256]{2,1,0:T(8,128)(2,1)S(1)}, u32[]{:S(2)}, u32[]{:S(2)}) async-start(bf16[8,128,256]{2,1,0:T(8,128)(2,1)} %bitcast.97), calls=%async_computation.7 | async-start | bytes 1048576 | tf_op jit(solution)/shard_map/all_to_all | solution.py:471
  201.3 5.1 %route_back.1 = bf16[8,8,192,128]{3,2,1,0:T(8,128)(2,1)} custom-call(s32[3]{0:T(128)} %pad_add_fusion.at_ref, bf16[8,48,256]{2,1,0:T(8,128)(2,1)} %bitcast.90, bf16[8,48,256]{2,1,0:T(8,128)(2,1)} %copy-done.7, bf16[8,48,256]{2,1,0:T(8,128)(2,1)} %copy-done.6, bf16[8,48,256]{2,1,0:T(8,128)(2,1)} %copy-done.5, bf16[8,2,128,128]{3,2,1,0:T(8,128)(2,1)} %bitcast.25.w_ref), custom_call_target="tpu_custom_call" | custom-call | flops 1000 | bytes 1000 | tf_op jit(solution)/shard_map/route_back/pallas_call | solution.py:298
  206.4 12.8 %all-to-all-done.6 = bf16[8,128,256]{2,1,0:T(8,128)(2,1)S(1)} async-done(((bf16[8,128,256]{2,1,0:T(8,128)(2,1)}), bf16[8,128,256]{2,1,0:T(8,128)(2,1)S(1)}, u32[]{:S(2)}, u32[]{:S(2)}) %all-to-all-start.6) | async-done | bytes 524320 | tf_op jit(solution)/shard_map/all_to_all | solution.py:471
  219.3 0.8 copy-done.4
  220.1 4.9 %all-to-all-start.7 = ((bf16[64,4,48,128]{3,2,1,0:T(8,128)(2,1)}), bf16[64,4,48,128]{3,2,1,0:T(8,128)(2,1)S(1)}, u32[]{:S(2)}, u32[]{:S(2)}) async-start(bf16[64,4,48,128]{3,2,1,0:T(8,128)(2,1)} %bitcast.79), calls=%async_computation.8 | async-start | bytes 6291456 | tf_op jit(solution)/shard_map/all_to_all | solution.py:471
  225.0 1.8 reduce_sum.12
  226.8 41.6 %all-to-all-done.7.back_ref = bf16[64,4,48,128]{3,2,1,0:T(8,128)(2,1)S(1)} async-done(((bf16[64,4,48,128]{3,2,1,0:T(8,128)(2,1)}), bf16[64,4,48,128]{3,2,1,0:T(8,128)(2,1)S(1)}, u32[]{:S(2)}, u32[]{:S(2)}) %all-to-all-start.7) | async-done | bytes 3145760 | tf_op jit(solution)/shard_map/all_to_all | solution.py:471
  268.4 5.3 %all-to-all-start.8 = ((bf16[64,2,48,128]{3,2,1,0:T(8,128)(2,1)}), bf16[64,2,48,128]{3,2,1,0:T(8,128)(2,1)}, u32[]{:S(2)}, u32[]{:S(2)}) async-start(bf16[64,2,48,128]{3,2,1,0:T(8,128)(2,1)} %pack_rows.5), calls=%async_computation.9 | async-start | bytes 3145728 | tf_op jit(solution)/shard_map/all_to_all | solution.py:471
  273.7 7.4 %early_weights.1 = (f32[8,128,256]{2,1,0:T(8,128)}, f32[8,256,128]{2,1,0:T(8,128)}) custom-call(s32[3]{0:T(128)} %pad_add_fusion.at_ref, bf16[8,48,256]{2,1,0:T(8,128)(2,1)} %bitcast.91, bf16[8,48,256]{2,1,0:T(8,128)(2,1)} %copy-done.7, bf16[8,48,256]{2,1,0:T(8,128)(2,1)} %copy-done.6, bf16[8,48,256]{2,1,0:T(8,128)(2,1)} %copy-done.5, ...), custom_call_target="tpu_custom_call" | custom-call | flops 1000 | bytes 1000 | tf_op jit(solution)/shard_map/early_weights/pallas_call | solution.py:355
  281.2 6.8 %unpack_rows.1.rows_ref = f32[4,4,256,128]{3,2,1,0:T(8,128)} custom-call(s32[4,4,2,256]{3,2,1,0:T(2,128)} %get-tuple-element.30.rho_ref, bf16[64,4,48,128]{3,2,1,0:T(8,128)(2,1)} %copy-done.1, bf16[384,384]{1,0:T(8,128)(2,1)} %constant.53.clone.swap_ref), custom_call_target="tpu_custom_call" | custom-call | flops 1000 | bytes 1000 | tf_op jit(solution)/shard_map/unpack_rows/pallas_call | solution.py:430
  288.0 12.0 %all-to-all-done.8 = bf16[64,2,48,128]{3,2,1,0:T(8,128)(2,1)} async-done(((bf16[64,2,48,128]{3,2,1,0:T(8,128)(2,1)}), bf16[64,2,48,128]{3,2,1,0:T(8,128)(2,1)}, u32[]{:S(2)}, u32[]{:S(2)}) %all-to-all-start.8) | async-done | bytes 1572896 | tf_op jit(solution)/shard_map/all_to_all | solution.py:471
  300.0 5.7 %late_weights.1 = bf16[8,2,2,128,128]{4,3,2,1,0:T(8,128)(2,1)} custom-call(s32[3]{0:T(128)} %pad_add_fusion.at_ref, bf16[8,48,256]{2,1,0:T(8,128)(2,1)} %bitcast.92, bf16[8,48,256]{2,1,0:T(8,128)(2,1)} %copy-done.7, bf16[8,48,256]{2,1,0:T(8,128)(2,1)} %copy-done.6, bf16[8,48,256]{2,1,0:T(8,128)(2,1)} %copy-done.5, bf16[8,8,96,128]{3,2,1,0:T(8,128)(2,1)} %bitcast.43.hid_ref, ...), custom_call_target="tpu_custom_call" | custom-call | flops 1000 | bytes 1000 | tf_op jit(solution)/shard_map/late_weights/pallas_call | solution.py:355
  305.7 3.6 %all-to-all-start.9 = ((bf16[16,2,128,128]{3,2,1,0:T(8,128)(2,1)}), bf16[16,2,128,128]{3,2,1,0:T(8,128)(2,1)S(1)}, u32[]{:S(2)}, u32[]{:S(2)}) async-start(bf16[16,2,128,128]{3,2,1,0:T(8,128)(2,1)} %bitcast.84), calls=%async_computation.10 | async-start | bytes 2097152 | tf_op jit(solution)/shard_map/all_to_all | solution.py:471
  309.3 3.1 all-gather.5.cloned.1.call-done.dkv_ref
  312.4 3.0 projection.1
  315.4 4.1 %collective-permute-start.6 = (bf16[128,256]{1,0:T(8,128)(2,1)}, bf16[128,256]{1,0:T(8,128)(2,1)S(1)}, u32[]{:S(2)}, u32[]{:S(2)}) collective-permute-start(bf16[128,256]{1,0:T(8,128)(2,1)} %projection.1), channel_id=1, source_target_pairs={{0,1},{1,0},{2,3},{3,2},{4,5},{5,4},{6,7},{7,6},{8,9},{9,8},{10,11... | collective-permute-start | bytes 196616 | tf_op jit(solution)/shard_map/ppermute | solution.py:476
  319.5 0.6 pad_maximum_fusion.1.wkv_ref
  320.1 0.5 collective-permute-done.6
  320.6 0.9 fusion.5
  321.4 1.0 collective-permute-start.8
  322.4 1.6 collective-permute-start.7
  324.0 2.0 collective-permute-start.9
  325.9 4.5 %finish_rows.1 = bf16[4,4,256,128]{3,2,1,0:T(8,128)(2,1)} custom-call(f32[4,4,256,128]{3,2,1,0:T(8,128)} %unpack_rows.1.rows_ref, bf16[4,4,256,256]{3,2,1,0:T(8,128)(2,1)} %bitcast.86, bf16[128,256]{1,0:T(8,128)(2,1)} %pad_maximum_fusion.1.wkv_ref), custom_call_target="tpu_custom_call" | custom-call | flops 5000000000 | bytes 10000000 | tf_op jit(solution)/shard_map/finish_rows/pallas_call | solution.py:454
  330.5 0.7 fusion.6
  331.1 1.6 fusion
  (52 shorter events, 1.0 us)
Async XLA Ops:
  7.2 15.7 %all-to-all-start = ((bf16[16,128,128]{2,1,0:T(8,128)(2,1)}), bf16[16,128,128]{2,1,0:T(8,128)(2,1)S(1)}, u32[]{:S(2)}, u32[]{:S(2)}) async-start(bf16[16,128,128]{2,1,0:T(8,128)(2,1)} %param.22), calls=%async_computation | async-start | bytes 1048576 | tf_op jit(solution)/shard_map/all_to_all | solution.py:471
  22.8 0.8 copy-start.3
  22.8 10.7 %copy-start.13 = (bf16[1,128,128]{2,1,0:T(8,128)(2,1)S(1)}, bf16[1,128,128]{2,1,0:T(8,128)(2,1)}, u32[]{:S(2)}) copy-start(bf16[1,128,128]{2,1,0:T(8,128)(2,1)} %param.18) | copy-start | bytes 98308
  22.8 10.7 %copy-start.14 = (bf16[1,128,128]{2,1,0:T(8,128)(2,1)S(1)}, bf16[1,128,128]{2,1,0:T(8,128)(2,1)}, u32[]{:S(2)}) copy-start(bf16[1,128,128]{2,1,0:T(8,128)(2,1)} %param.17) | copy-start | bytes 98308
  23.6 52.8 %all-to-all-start.1 = ((bf16[64,4,48,128]{3,2,1,0:T(8,128)(2,1)}), bf16[64,4,48,128]{3,2,1,0:T(8,128)(2,1)S(1)}, u32[]{:S(2)}, u32[]{:S(2)}) async-start(bf16[64,4,48,128]{3,2,1,0:T(8,128)(2,1)} %get-tuple-element.32), calls=%async_computation.1 | async-start | bytes 6291456 | tf_op jit(solution)/shard_map/all_to_all | solution.py:471
  33.5 100.1 %all-gather.3.cloned.1.call-start = ((), (), s32[]{:S(2)}) async-start(), calls=%async_computation.11 | async-start | bytes 2162688 | tf_op jit(solution)/shard_map/all_gather | solution.py:494
  38.5 4.3 %copy-start.12 = (bf16[1,128,2,128]{3,2,1,0:T(2,128)(2,1)S(1)}, bf16[1,128,2,128]{3,2,1,0:T(2,128)(2,1)}, u32[]{:S(2)}) copy-start(bf16[1,128,2,128]{3,2,1,0:T(2,128)(2,1)} %param.16) | copy-start | bytes 196612
  76.4 4.8 %copy-start = (bf16[64,4,48,128]{3,2,1,0:T(8,128)(2,1)}, bf16[64,4,48,128]{3,2,1,0:T(8,128)(2,1)S(1)}, u32[]{:S(2)}) copy-start(bf16[64,4,48,128]{3,2,1,0:T(8,128)(2,1)S(1)} %all-to-all-done.1) | copy-start | bytes 9437188
  76.4 13.9 %all-to-all-start.2 = ((bf16[16,128,128]{2,1,0:T(8,128)(2,1)}), bf16[16,128,128]{2,1,0:T(8,128)(2,1)}, u32[]{:S(2)}, u32[]{:S(2)}) async-start(bf16[16,128,128]{2,1,0:T(8,128)(2,1)} %param.21), calls=%async_computation.2 | async-start | bytes 1048576 | tf_op jit(solution)/shard_map/all_to_all | solution.py:471
  90.3 10.1 %collective-permute-start = (bf16[8,48,128]{2,1,0:T(8,128)(2,1)S(1)}, bf16[8,48,128]{2,1,0:T(8,128)(2,1)S(1)}, u32[]{:S(2)}, u32[]{:S(2)}) collective-permute-start(bf16[8,48,128]{2,1,0:T(8,128)(2,1)S(1)} %get-tuple-element.36), channel_id=1, source_target_pairs={{0,16},{16,32},{32,48},{48,0},{1,17},{17,33},{33,49},{49,1},{2,18}... | collective-permute-start | bytes 294920 | tf_op jit(solution)/shard_map/ppermute | solution.py:476
  93.6 15.9 %collective-permute-start.1 = (bf16[8,48,128]{2,1,0:T(8,128)(2,1)S(1)}, bf16[8,48,128]{2,1,0:T(8,128)(2,1)S(1)}, u32[]{:S(2)}, u32[]{:S(2)}) collective-permute-start(bf16[8,48,128]{2,1,0:T(8,128)(2,1)S(1)} %get-tuple-element.37), channel_id=1, source_target_pairs={{0,32},{16,48},{32,0},{48,16},{1,33},{17,49},{33,1},{49,17},{2,34}... | collective-permute-start | bytes 294920 | tf_op jit(solution)/shard_map/ppermute | solution.py:476
  98.0 12.0 %collective-permute-start.2 = (bf16[8,48,128]{2,1,0:T(8,128)(2,1)S(1)}, bf16[8,48,128]{2,1,0:T(8,128)(2,1)S(1)}, u32[]{:S(2)}, u32[]{:S(2)}) collective-permute-start(bf16[8,48,128]{2,1,0:T(8,128)(2,1)S(1)} %get-tuple-element.38), channel_id=1, source_target_pairs={{0,48},{16,0},{32,16},{48,32},{1,49},{17,1},{33,17},{49,33},{2,50}... | collective-permute-start | bytes 294920 | tf_op jit(solution)/shard_map/ppermute | solution.py:476
  100.4 9.5 %copy-start.9 = (bf16[8,48,128]{2,1,0:T(8,128)(2,1)}, bf16[8,48,128]{2,1,0:T(8,128)(2,1)S(1)}, u32[]{:S(2)}) copy-start(bf16[8,48,128]{2,1,0:T(8,128)(2,1)S(1)} %collective-permute-done) | copy-start | bytes 294916
  109.5 0.6 copy-start.10
  110.0 0.6 copy-start.11
  110.6 22.2 %copy-start.17 = (f32[1,128,2]{1,2,0:T(2,128)S(1)}, f32[1,128,2]{1,2,0:T(2,128)}, u32[]{:S(2)}) copy-start(f32[1,128,2]{1,2,0:T(2,128)} %param.20) | copy-start | bytes 3076
  128.0 28.1 %all-to-all-start.4 = ((bf16[64,2,48,128]{3,2,1,0:T(8,128)(2,1)}), bf16[64,2,48,128]{3,2,1,0:T(8,128)(2,1)S(1)}, u32[]{:S(2)}, u32[]{:S(2)}) async-start(bf16[64,2,48,128]{3,2,1,0:T(8,128)(2,1)} %pack_rows.4), calls=%async_computation.4 | async-start | bytes 3145728 | tf_op jit(solution)/shard_map/all_to_all | solution.py:471
  132.5 58.8 %reduce-scatter.2.cloned.1.call-start = ((), (), s32[]{:S(2)}) async-start(), calls=%async_computation.12 | async-start | bytes 2621440 | tf_op jit(solution)/shard_map/reduce_scatter | solution.py:519
  145.8 10.3 %copy-start.8 = (bf16[512,256]{1,0:T(8,128)(2,1)S(1)}, bf16[512,256]{1,0:T(8,128)(2,1)}, u32[]{:S(2)}) copy-start(bf16[512,256]{1,0:T(8,128)(2,1)} %get-tuple-element.45) | copy-start | bytes 786436
  156.1 16.4 %copy-start.2 = (bf16[64,2,48,128]{3,2,1,0:T(8,128)(2,1)}, bf16[64,2,48,128]{3,2,1,0:T(8,128)(2,1)S(1)}, u32[]{:S(2)}) copy-start(bf16[64,2,48,128]{3,2,1,0:T(8,128)(2,1)S(1)} %all-to-all-done.4) | copy-start | bytes 4718596
  172.6 11.2 %collective-permute-start.5 = (bf16[8,48,256]{2,1,0:T(8,128)(2,1)}, bf16[8,48,256]{2,1,0:T(8,128)(2,1)S(1)}, u32[]{:S(2)}, u32[]{:S(2)}) collective-permute-start(bf16[8,48,256]{2,1,0:T(8,128)(2,1)} %bitcast.87), channel_id=1, source_target_pairs={{0,48},{16,0},{32,16},{48,32},{1,49},{17,1},{33,17},{49,33},{2,50}... | collective-permute-start | bytes 589832 | tf_op jit(solution)/shard_map/ppermute | solution.py:476
  175.4 13.2 %collective-permute-start.4 = (bf16[8,48,256]{2,1,0:T(8,128)(2,1)}, bf16[8,48,256]{2,1,0:T(8,128)(2,1)S(1)}, u32[]{:S(2)}, u32[]{:S(2)}) collective-permute-start(bf16[8,48,256]{2,1,0:T(8,128)(2,1)} %bitcast.88), channel_id=1, source_target_pairs={{0,32},{16,48},{32,0},{48,16},{1,33},{17,49},{33,1},{49,17},{2,34}... | collective-permute-start | bytes 589832 | tf_op jit(solution)/shard_map/ppermute | solution.py:476
  176.5 14.8 %collective-permute-start.3 = (bf16[8,48,256]{2,1,0:T(8,128)(2,1)}, bf16[8,48,256]{2,1,0:T(8,128)(2,1)S(1)}, u32[]{:S(2)}, u32[]{:S(2)}) collective-permute-start(bf16[8,48,256]{2,1,0:T(8,128)(2,1)} %bitcast.89), channel_id=1, source_target_pairs={{0,16},{16,32},{32,48},{48,0},{1,17},{17,33},{33,49},{49,1},{2,18}... | collective-permute-start | bytes 589832 | tf_op jit(solution)/shard_map/ppermute | solution.py:476
  183.8 17.5 %copy-start.5 = (bf16[8,48,256]{2,1,0:T(8,128)(2,1)}, bf16[8,48,256]{2,1,0:T(8,128)(2,1)S(1)}, u32[]{:S(2)}) copy-start(bf16[8,48,256]{2,1,0:T(8,128)(2,1)S(1)} %collective-permute-done.5.d_ref) | copy-start | bytes 589828
  188.6 12.7 %copy-start.6 = (bf16[8,48,256]{2,1,0:T(8,128)(2,1)}, bf16[8,48,256]{2,1,0:T(8,128)(2,1)S(1)}, u32[]{:S(2)}) copy-start(bf16[8,48,256]{2,1,0:T(8,128)(2,1)S(1)} %collective-permute-done.4.c_ref) | copy-start | bytes 589828
  191.3 10.0 %copy-start.7 = (bf16[8,48,256]{2,1,0:T(8,128)(2,1)}, bf16[8,48,256]{2,1,0:T(8,128)(2,1)S(1)}, u32[]{:S(2)}) copy-start(bf16[8,48,256]{2,1,0:T(8,128)(2,1)S(1)} %collective-permute-done.3.b_ref) | copy-start | bytes 589828
  191.3 27.9 %all-to-all-start.6 = ((bf16[8,128,256]{2,1,0:T(8,128)(2,1)}), bf16[8,128,256]{2,1,0:T(8,128)(2,1)S(1)}, u32[]{:S(2)}, u32[]{:S(2)}) async-start(bf16[8,128,256]{2,1,0:T(8,128)(2,1)} %bitcast.97), calls=%async_computation.7 | async-start | bytes 1048576 | tf_op jit(solution)/shard_map/all_to_all | solution.py:471
  219.3 0.8 copy-start.4
  220.1 48.3 %all-to-all-start.7 = ((bf16[64,4,48,128]{3,2,1,0:T(8,128)(2,1)}), bf16[64,4,48,128]{3,2,1,0:T(8,128)(2,1)S(1)}, u32[]{:S(2)}, u32[]{:S(2)}) async-start(bf16[64,4,48,128]{3,2,1,0:T(8,128)(2,1)} %bitcast.79), calls=%async_computation.8 | async-start | bytes 6291456 | tf_op jit(solution)/shard_map/all_to_all | solution.py:471
  225.0 87.4 %all-gather.5.cloned.1.call-start = ((), (), s32[]{:S(2)}) async-start(), calls=%async_computation.13 | async-start | bytes 2162688 | tf_op jit(solution)/shard_map/all_gather | solution.py:525
  268.4 12.8 %copy-start.1 = (bf16[64,4,48,128]{3,2,1,0:T(8,128)(2,1)}, bf16[64,4,48,128]{3,2,1,0:T(8,128)(2,1)S(1)}, u32[]{:S(2)}) copy-start(bf16[64,4,48,128]{3,2,1,0:T(8,128)(2,1)S(1)} %all-to-all-done.7.back_ref) | copy-start | bytes 9437188
  268.4 31.6 %all-to-all-start.8 = ((bf16[64,2,48,128]{3,2,1,0:T(8,128)(2,1)}), bf16[64,2,48,128]{3,2,1,0:T(8,128)(2,1)}, u32[]{:S(2)}, u32[]{:S(2)}) async-start(bf16[64,2,48,128]{3,2,1,0:T(8,128)(2,1)} %pack_rows.5), calls=%async_computation.9 | async-start | bytes 3145728 | tf_op jit(solution)/shard_map/all_to_all | solution.py:471
  305.7 25.5 %all-to-all-start.9 = ((bf16[16,2,128,128]{3,2,1,0:T(8,128)(2,1)}), bf16[16,2,128,128]{3,2,1,0:T(8,128)(2,1)S(1)}, u32[]{:S(2)}, u32[]{:S(2)}) async-start(bf16[16,2,128,128]{3,2,1,0:T(8,128)(2,1)} %bitcast.84), calls=%async_computation.10 | async-start | bytes 2097152 | tf_op jit(solution)/shard_map/all_to_all | solution.py:471
  309.2 10.2 %copy-start.15 = (bf16[128,128]{1,0:T(8,128)(2,1)S(1)}, bf16[128,128]{1,0:T(8,128)(2,1)}, u32[]{:S(2)}) copy-start(bf16[128,128]{1,0:T(8,128)(2,1)} %param.24) | copy-start | bytes 98308
  309.3 10.2 %copy-start.16 = (bf16[128,128]{1,0:T(8,128)(2,1)S(1)}, bf16[128,128]{1,0:T(8,128)(2,1)}, u32[]{:S(2)}) copy-start(bf16[128,128]{1,0:T(8,128)(2,1)} %param.23) | copy-start | bytes 98308
  315.4 5.2 %collective-permute-start.6 = (bf16[128,256]{1,0:T(8,128)(2,1)}, bf16[128,256]{1,0:T(8,128)(2,1)S(1)}, u32[]{:S(2)}, u32[]{:S(2)}) collective-permute-start(bf16[128,256]{1,0:T(8,128)(2,1)} %projection.1), channel_id=1, source_target_pairs={{0,1},{1,0},{2,3},{3,2},{4,5},{5,4},{6,7},{7,6},{8,9},{9,8},{10,11... | collective-permute-start | bytes 196616 | tf_op jit(solution)/shard_map/ppermute | solution.py:476
  321.4 9.0 %collective-permute-start.8 = (bf16[128,256]{1,0:T(8,128)(2,1)S(1)}, bf16[128,256]{1,0:T(8,128)(2,1)S(1)}, u32[]{:S(2)}, u32[]{:S(2)}) collective-permute-start(bf16[128,256]{1,0:T(8,128)(2,1)S(1)} %get-tuple-element.56), channel_id=1, source_target_pairs={{0,2},{2,4},{4,6},{6,0},{1,3},{3,5},{5,7},{7,1},{8,10},{10,12},{12... | collective-permute-start | bytes 196616 | tf_op jit(solution)/shard_map/ppermute | solution.py:476
  322.4 8.0 %collective-permute-start.7 = (bf16[128,256]{1,0:T(8,128)(2,1)S(1)}, bf16[128,256]{1,0:T(8,128)(2,1)S(1)}, u32[]{:S(2)}, u32[]{:S(2)}) collective-permute-start(bf16[128,256]{1,0:T(8,128)(2,1)S(1)} %get-tuple-element.56), channel_id=1, source_target_pairs={{0,4},{2,6},{4,0},{6,2},{1,5},{3,7},{5,1},{7,3},{8,12},{10,14},{12... | collective-permute-start | bytes 196616 | tf_op jit(solution)/shard_map/ppermute | solution.py:476
  324.0 6.5 %collective-permute-start.9 = (bf16[128,256]{1,0:T(8,128)(2,1)S(1)}, bf16[128,256]{1,0:T(8,128)(2,1)S(1)}, u32[]{:S(2)}, u32[]{:S(2)}) collective-permute-start(bf16[128,256]{1,0:T(8,128)(2,1)S(1)} %get-tuple-element.56), channel_id=1, source_target_pairs={{0,6},{2,0},{4,2},{6,4},{1,7},{3,1},{5,3},{7,5},{8,14},{10,8},{12,... | collective-permute-start | bytes 196616 | tf_op jit(solution)/shard_map/ppermute | solution.py:476
Sparse Core Ops, SparseCore 0:
  37.5 85.2 all-gather.2
  146.0 34.5 reduce-scatter.1
  229.3 83.0 all-gather.4

commit v4 on v3

--- a/solution.py
+++ b/solution.py
@@ -129,47 +129,47 @@
     return lax.rem(lax.broadcasted_iota(jnp.int32, shape, 0), ROWS) >= CAP
 
 
-def head_kernel(at_ref, grad_ref, w_ref, out_ref):
-    zh = at_ref[1]
+def head_kernel(grad_ref, w_ref, o0, o1, o2, o3):
     for g in range(2):
         total = jnp.zeros((32 * ROWS, EPD * HD), F32)
         for r in range(8):
             total += dot_nt(grad_ref[r, g], w_ref[r])
         own = jnp.where(second_expert((32 * ROWS, HD)), total[:, HD:], total[:, :HD])
         own = own.astype(BF16).reshape(4, 8 * ROWS, HD)
-        for t in range(4):
-            out_ref[(t + 4 - zh) % 4, g] = own[t]
-
-
-def head_sums(at, grad_rows, weights):
+        for t, out in enumerate((o0, o1, o2, o3)):
+            out[g] = own[t]
+
+
+def head_sums(grad_rows, weights):
     return pl.pallas_call(
         head_kernel,
         grid=(4,),
         in_specs=[
-            pl.BlockSpec(memory_space=pltpu.SMEM),
             pl.BlockSpec((8, 2, 32 * ROWS, HD), lambda i: (0, i, 0, 0)),
             pl.BlockSpec((8, EPD * HD, HD), lambda i: (0, 0, 0)),
         ],
-        out_specs=pl.BlockSpec((4, 2, 8 * ROWS, HD), lambda i: (0, i, 0, 0)),
-        out_shape=jax.ShapeDtypeStruct((4, 8, 8 * ROWS, HD), BF16),
+        out_specs=[pl.BlockSpec((2, 8 * ROWS, HD), lambda i: (i, 0, 0))] * 4,
+        out_shape=[jax.ShapeDtypeStruct((8, 8 * ROWS, HD), BF16)] * 4,
         cost_estimate=pl.CostEstimate(flops=1000, bytes_accessed=1000, transcendentals=0),
         compiler_params=params(1),
         name="head_sums",
-    )(at, grad_rows.reshape(8, 8, 32 * ROWS, HD), weights)
-
-
-def reduce_kernel(a_ref, b_ref, c_ref, d_ref, pad_ref, out_ref):
-    total = a_ref[...].astype(F32) + b_ref[...].astype(F32) + c_ref[...].astype(F32) + d_ref[...].astype(F32)
-    out_ref[...] = dot_nn(pad_ref[...], total.astype(BF16)).astype(BF16)
-
-
-def reduce_heads(parts, pad):
-    return pl.pallas_call(
-        reduce_kernel,
-        out_shape=jax.ShapeDtypeStruct((64 * PAD, HD), BF16),
+    )(grad_rows.reshape(8, 8, 32 * ROWS, HD), weights)
+
+
+def address_kernel(t0, t1, t2, t3, pad_ref, out_ref):
+    for t, part in enumerate((t0, t1, t2, t3)):
+        rows = dot_nn(pad_ref[...], part[...]).astype(BF16)
+        for x in range(4):
+            out_ref[x, t] = rows[x * 16 * PAD : (x + 1) * 16 * PAD]
+
+
+def address_heads(parts, pad):
+    return pl.pallas_call(
+        address_kernel,
+        out_shape=jax.ShapeDtypeStruct((4, 4, 16 * PAD, HD), BF16),
         cost_estimate=pl.CostEstimate(flops=1000, bytes_accessed=1000, transcendentals=0),
         compiler_params=params(0),
-        name="reduce_heads",
+        name="address_heads",
     )(*[p.reshape(64 * ROWS, HD) for p in parts], pad)
 
 
@@ -226,7 +226,8 @@
     n, length = q_ref.shape[0], kv_ref.shape[0]
     step = 512
     scale = 1.0 / math.sqrt(HD)
-    lanes = lax.broadcasted_iota(jnp.int32, (n, 64 * PAD), 1)
+    lanes = lax.broadcasted_iota(jnp.int32, (n, 256 * PAD), 1)
+    lanes = (lanes >> 9) * (16 * PAD) + (lanes & (16 * PAD - 1))
     pick = (lanes == rho_col_ref[...]).astype(F32).astype(BF16)
     head_grad = gate_ref[...] * dot_nn(pick, head_ref[...])
     delta = jnp.sum(head_grad * out_ref[...], axis=1, keepdims=True)
@@ -505,22 +506,21 @@
     own = own // ROWS * PAD + own % ROWS
     own_row, own_col = own.reshape(1, -1), own.reshape(-1, 1)
 
-    parts = head_sums(at, after(grad_rows, own_row, own_col, q, gates, hid_a, hid_b), w_out_r)
-    w_query_r = exchange(after(w_query, grad_rows, own_row, own_col, q, gates, hid_a, hid_b), SLAB).reshape(8, EPD, HD, HD)
-    parts = list(lax.optimization_barrier((*[parts[s] for s in range(4)], w_query_r)))[:4]
-    parts = [parts[0]] + [shifted(parts[s], "zh", s) for s in range(1, 4)]
-    head_home = exchange(reduce_heads(parts, pad).reshape(64, PAD, HD), WIDE)
+    parts = head_sums(after(grad_rows, own_row, own_col, q, gates, hid_a, hid_b), w_out_r)
+    head_home = exchange(address_heads(parts, pad).reshape(256, PAD, HD), SEQ + GRP)
     hid_a = exchange(after(hid_a, head_home), WIDE)
     prob, head_out, gated = attend_forward(at, after(q, head_home), kv, gates)
     slots, dkv_part = attend_backward(
-        head_home.reshape(64 * PAD, HD), own_row, own_col, gates, q, kv,
+        head_home.reshape(256 * PAD, HD), own_row, own_col, gates, q, kv,
         prob, head_out, gated,
     )
     dkv_x = lax.psum_scatter(dkv_part, "x", scatter_dimension=0, tiled=True)
     mine = exchange(after(slots, hid_a).reshape(64, PAD, 2 * HD), WIDE).reshape(64 * PAD, 2 * HD)
     dqg = unpad_rows(mine, unpad).reshape(8, 8 * ROWS, 2 * HD)
+    first = dqg
     dqg = gather(dqg, "zh")
-    dkv_z = exchange(after(dkv_x, *dqg).reshape(8, BLOCK, 2 * HD), ("zh", "zl"))
+    w_query_r = exchange(after(w_query, mine), SLAB).reshape(8, EPD, HD, HD)
+    dkv_z = exchange(after(dkv_x, w_query_r, *dqg).reshape(8, BLOCK, 2 * HD), ("zh", "zl"))
     dkv_own = dkv_z.astype(F32).sum(axis=0).astype(BF16)
     dkv = lax.all_gather(dkv_own, SEQ, axis=0, tiled=True)
     back_rows = route_back(at, dqg, w_query_r).reshape(64, 4, 8 * ROWS, HD)

time: 341 us -> 340 us (level)
  blocking collectives: 29.7 us -> 50.2 us
  waiting for transfers between devices: 136 us -> 122 us
  starting transfers between devices: 73.3 us -> 65.9 us
    all_to_all x2, blocking collectives: 29.7 us -> 50.2 us  [exchange(): return lax.all_to_all(rows, axes, split_axis=0, concat_axis=0, tiled=True)]
    ppermute x10 -> x7, starting transfers between devices: 24.5 us -> 12.6 us  [shifted(): return lax.ppermute(rows, axis, [(i, (i + s) % n) for i in range(n)])]
    ppermute x10 -> x7, waiting for transfers between devices: 22.9 us -> 15.6 us  [shifted(): return lax.ppermute(rows, axis, [(i, (i + s) % n) for i in range(n)])]
    all_to_all x8, waiting for transfers between devices: 110 us -> 103 us  [exchange(): return lax.all_to_all(rows, axes, split_axis=0, concat_axis=0, tiled=True)]
    all_to_all x8, starting transfers between devices: 48.5 us -> 53 us  [exchange(): return lax.all_to_all(rows, axes, split_axis=0, concat_axis=0, tiled=True)]
  transfers between devices with their start and end apart: 21 -> 18, of which waited for: 14 -> 10; matrix products, arithmetic and copies ran while one was open for 3% -> 3% of each run, Pallas kernels for 21% -> 22%
where the time goes in v4:
time: 340 us; the launch traced here: 339 us
  waiting for transfers between devices  122 us (36%)
  Pallas kernels  72.8 us (21%)
  starting transfers between devices  65.9 us (19%)
  blocking collectives  50.2 us (15%)
  between operations  14 us (4%)
  other arithmetic  8.07 us (2%)
  local copies, waits for them, and re-layouts  5.79 us (2%)
    all_to_all x8, waiting for transfers between devices, exchange(): return lax.all_to_all(rows, axes, split_axis=0, concat_axis=0, tiled=True)  103 us
    all_to_all x8, starting transfers between devices, exchange(): return lax.all_to_all(rows, axes, split_axis=0, concat_axis=0, tiled=True)  53 us
    all_to_all x2, blocking collectives, exchange(): return lax.all_to_all(rows, axes, split_axis=0, concat_axis=0, tiled=True)  50.2 us
    pallas_call x3, Pallas kernels, pack(): pl.pallas_call(kernel, grid=(steps,), in_specs=[id_spec, slab, pl.BlockSp...  18.1 us
    ppermute x7, waiting for transfers between devices, shifted(): return lax.ppermute(rows, axis, [(i, (i + s) % n) for i in range(n)])  15.6 us
    pallas_call x2, Pallas kernels, weights_call(): pl.pallas_call(kernel, grid=(4,), in_specs=[pl.BlockSpec(memory_space=plt...  13.1 us
    ppermute x7, starting transfers between devices, shifted(): return lax.ppermute(rows, axis, [(i, (i + s) % n) for i in range(n)])  12.6 us
    pallas_call x1, Pallas kernels, attend_backward(): pl.pallas_call(backward_kernel, out_shape=[jax.ShapeDtypeStruct((64 * PAD...  7.7 us
  transfers between devices with their start and end apart: 18, of which 10 were waited for; matrix products, arithmetic and copies ran while one was open for 3% of the time, Pallas kernels for 22%

profile of v4, /device:TPU:1, one launch (start us, length us, event | category | flops | bytes accessed | tf_op | source)
XLA Modules:
  0.0 338.5 jit_solution(8455352788900361746)
XLA Ops:
  7.2 6.2 %all-to-all-start = ((bf16[16,128,128]{2,1,0:T(8,128)(2,1)}), bf16[16,128,128]{2,1,0:T(8,128)(2,1)S(1)}, u32[]{:S(2)}, u32[]{:S(2)}) async-start(bf16[16,128,128]{2,1,0:T(8,128)(2,1)} %param.22), calls=%async_computation | async-start | bytes 1048576 | tf_op jit(solution)/shard_map/all_to_all | solution.py:472
  13.4 9.5 %pack_rows.3 = (bf16[64,4,48,128]{3,2,1,0:T(8,128)(2,1)}, s32[4,4,2,256]{3,2,1,0:T(2,128)}) custom-call(s32[4,4,2,256]{3,2,1,0:T(2,128)} %bitcast.99, bf16[4,4,256,128]{3,2,1,0:T(8,128)(2,1)} %bitcast.88, bf16[384,384]{1,0:T(8,128)(2,1)} %constant.53.clone.swap_ref), custom_call_target="tpu_custom_call" | custom-call | flops 1000 | bytes 1000 | tf_op jit(solution)/shard_map/pack_rows/pallas_call | solution.py:115
  22.9 0.8 copy-done.3
  23.6 9.8 %all-to-all-start.1 = ((bf16[64,4,48,128]{3,2,1,0:T(8,128)(2,1)}), bf16[64,4,48,128]{3,2,1,0:T(8,128)(2,1)S(1)}, u32[]{:S(2)}, u32[]{:S(2)}) async-start(bf16[64,4,48,128]{3,2,1,0:T(8,128)(2,1)} %get-tuple-element.32), calls=%async_computation.1 | async-start | bytes 6291456 | tf_op jit(solution)/shard_map/all_to_all | solution.py:472
  33.5 0.0 all-gather.3.cloned.1.call-start
  33.6 0.6 pad_maximum_fusion
  34.2 0.0 all-gather.3.cloned.1.call-update
  34.2 4.3 %pack_rows.5 = bf16[64,2,48,128]{3,2,1,0:T(8,128)(2,1)} custom-call(s32[4,4,2,256]{3,2,1,0:T(2,128)} %get-tuple-element.30.rho_ref, bf16[4,4,256,128]{3,2,1,0:T(8,128)(2,1)} %bitcast.72, bf16[384,384]{1,0:T(8,128)(2,1)} %constant.53.clone.swap_ref), custom_call_target="tpu_custom_call" | custom-call | flops 1000 | bytes 1000 | tf_op jit(solution)/shard_map/pack_rows/pallas_call | solution.py:115
  38.6 4.3 %pack_rows.4 = bf16[64,2,48,128]{3,2,1,0:T(8,128)(2,1)} custom-call(s32[4,4,2,256]{3,2,1,0:T(2,128)} %get-tuple-element.30.rho_ref, bf16[4,4,256,128]{3,2,1,0:T(8,128)(2,1)} %bitcast.73, bf16[384,384]{1,0:T(8,128)(2,1)} %constant.53.clone.swap_ref), custom_call_target="tpu_custom_call" | custom-call | flops 1000 | bytes 1000 | tf_op jit(solution)/shard_map/pack_rows/pallas_call | solution.py:115
  42.9 0.6 copy.39
  43.5 0.7 compare_bitcast_fusion
  44.2 0.2 copy.44
  44.4 0.1 copy.32
  44.6 0.1 copy.34
  44.7 0.6 fusion.4.rho_row_ref
  45.3 0.7 fusion.3.rho_col_ref
  46.0 30.4 %all-to-all-done.1 = bf16[64,4,48,128]{3,2,1,0:T(8,128)(2,1)S(1)} async-done(((bf16[64,4,48,128]{3,2,1,0:T(8,128)(2,1)}), bf16[64,4,48,128]{3,2,1,0:T(8,128)(2,1)S(1)}, u32[]{:S(2)}, u32[]{:S(2)}) %all-to-all-start.1) | async-done | bytes 3145760 | tf_op jit(solution)/shard_map/all_to_all | solution.py:472
  76.4 1.6 copy-done
  78.0 4.8 %head_sums.1 = (bf16[8,48,128]{2,1,0:T(8,128)(2,1)}, bf16[8,48,128]{2,1,0:T(8,128)(2,1)}, bf16[8,48,128]{2,1,0:T(8,128)(2,1)}, bf16[8,48,128]{2,1,0:T(8,128)(2,1)}) custom-call(bf16[8,8,192,128]{3,2,1,0:T(8,128)(2,1)} %bitcast.69, bf16[8,256,128]{2,1,0:T(8,128)(2,1)} %bitcast.77), custom_call_target="tpu_custom_call" | custom-call | flops 1000 | bytes 1000 | tf_op jit(solution)/shard_map/head_sums/pallas_call | solution.py:144
  82.9 2.6 address_heads.1
  85.4 35.8 %all_to_all.50 = bf16[256,8,128]{2,1,0:T(8,128)(2,1)} all-to-all(bf16[256,8,128]{2,1,0:T(8,128)(2,1)} %bitcast.80), channel_id=1, replica_groups=mesh['x'=4,'zh'=4,'zl'=2,'node'=4,'dev'=2] {'x','zh','zl','node','dev'}, dimensions={0} | all-to-all | bytes 1048576 | tf_op jit(solution)/shard_map/all_to_all | solution.py:472
  121.2 6.1 %all-to-all-start.3 = ((bf16[64,2,48,128]{3,2,1,0:T(8,128)(2,1)}), bf16[64,2,48,128]{3,2,1,0:T(8,128)(2,1)S(1)}, u32[]{:S(2)}, u32[]{:S(2)}) async-start(bf16[64,2,48,128]{3,2,1,0:T(8,128)(2,1)} %pack_rows.4), calls=%async_computation.3 | async-start | bytes 3145728 | tf_op jit(solution)/shard_map/all_to_all | solution.py:472
  127.3 0.2 reduce-scatter.2.cloned.1.call-start
  127.5 0.8 copy.41.gate_ref
  128.3 0.6 pad_add_fusion.at_ref
  128.9 5.0 %attend_forward.1 = (bf16[256,4096]{1,0:T(8,128)(2,1)}, f32[256,128]{1,0:T(8,128)}, bf16[256,128]{1,0:T(8,128)(2,1)}) custom-call(s32[3]{0:T(128)} %pad_add_fusion.at_ref, bf16[256,128]{1,0:T(8,128)(2,1)} %bitcast.89, bf16[4096,256]{1,0:T(8,128)(2,1)} %all-gather.3.cloned.1.call-done.kv_ref, f32[256,1]{1,0:T(8,128)} %copy.41.gate_ref), custom_call_target="tpu_custom_call" | custom-call | flops 1000 | bytes 1000 | tf_op jit(solution)/shard_map/attend_forward/pallas_call | solution.py:207
  133.9 7.7 %attend_backward.1 = (bf16[512,256]{1,0:T(8,128)(2,1)}, bf16[4096,256]{1,0:T(8,128)(2,1)}) custom-call(bf16[2048,128]{1,0:T(8,128)(2,1)} %bitcast.81, s32[1,256]{1,0:T(1,128)} %fusion.4.rho_row_ref, s32[256,1]{1,0:T(8,128)} %fusion.3.rho_col_ref, f32[256,1]{1,0:T(8,128)} %copy.41.gate_ref, bf16[256,128]{1,0:T(8,128)(2,1)} %bitcast.90, ...), custom_call_target="tpu_custom_call" | custom-call | flops 1000 | bytes 1000 | tf_op jit(solution)/shard_map/attend_backward/pallas_call | solution.py:251
  141.6 0.0 reduce-scatter.2.cloned.1.call-update
  141.7 9.1 %all-to-all-done.3 = bf16[64,2,48,128]{3,2,1,0:T(8,128)(2,1)S(1)} async-done(((bf16[64,2,48,128]{3,2,1,0:T(8,128)(2,1)}), bf16[64,2,48,128]{3,2,1,0:T(8,128)(2,1)S(1)}, u32[]{:S(2)}, u32[]{:S(2)}) %all-to-all-start.3) | async-done | bytes 1572896 | tf_op jit(solution)/shard_map/all_to_all | solution.py:472
  150.7 14.4 %all_to_all.51 = bf16[64,8,256]{2,1,0:T(8,128)(2,1)} all-to-all(bf16[64,8,256]{2,1,0:T(8,128)(2,1)S(1)} %bitcast.92), channel_id=1, replica_groups=mesh['x'=4,'zh'=4,'zl'=2,'node'=4,'dev'=2] {'x','zl','node','dev'}, dimensions={0} | all-to-all | bytes 524288 | tf_op jit(solution)/shard_map/all_to_all | solution.py:472
  165.1 3.5 %all-to-all-start.5 = ((bf16[16,128,128]{2,1,0:T(8,128)(2,1)}), bf16[16,128,128]{2,1,0:T(8,128)(2,1)S(1)}, u32[]{:S(2)}, u32[]{:S(2)}) async-start(bf16[16,128,128]{2,1,0:T(8,128)(2,1)} %param.21), calls=%async_computation.5 | async-start | bytes 1048576 | tf_op jit(solution)/shard_map/all_to_all | solution.py:472
  168.6 2.0 unpad_rows.1
  170.7 0.1 collective-permute-start.2
  170.8 3.9 %collective-permute-start.1 = (bf16[8,48,256]{2,1,0:T(8,128)(2,1)}, bf16[8,48,256]{2,1,0:T(8,128)(2,1)S(1)}, u32[]{:S(2)}, u32[]{:S(2)}) collective-permute-start(bf16[8,48,256]{2,1,0:T(8,128)(2,1)} %bitcast.83), channel_id=1, source_target_pairs={{0,32},{16,48},{32,0},{48,16},{1,33},{17,49},{33,1},{49,17},{2,34}... | collective-permute-start | bytes 589832 | tf_op jit(solution)/shard_map/ppermute | solution.py:477
  174.7 2.7 collective-permute-done.2.d_ref
  177.5 4.6 %collective-permute-done.1.c_ref = bf16[8,48,256]{2,1,0:T(8,128)(2,1)S(1)} collective-permute-done((bf16[8,48,256]{2,1,0:T(8,128)(2,1)}, bf16[8,48,256]{2,1,0:T(8,128)(2,1)S(1)}, u32[]{:S(2)}, u32[]{:S(2)}) %collective-permute-start.1) | collective-permute-done | bytes 196640 | tf_op jit(solution)/shard_map/ppermute | solution.py:477
  182.1 7.8 %collective-permute-done.b_ref = bf16[8,48,256]{2,1,0:T(8,128)(2,1)S(1)} collective-permute-done((bf16[8,48,256]{2,1,0:T(8,128)(2,1)}, bf16[8,48,256]{2,1,0:T(8,128)(2,1)S(1)}, u32[]{:S(2)}, u32[]{:S(2)}) %collective-permute-start) | collective-permute-done | bytes 196640 | tf_op jit(solution)/shard_map/ppermute | solution.py:477
  189.8 8.0 %all-to-all-start.6 = ((bf16[8,128,256]{2,1,0:T(8,128)(2,1)}), bf16[8,128,256]{2,1,0:T(8,128)(2,1)S(1)}, u32[]{:S(2)}, u32[]{:S(2)}) async-start(bf16[8,128,256]{2,1,0:T(8,128)(2,1)} %bitcast.91), calls=%async_computation.7 | async-start | bytes 1048576 | tf_op jit(solution)/shard_map/all_to_all | solution.py:472
  197.8 5.1 %route_back.1 = bf16[8,8,192,128]{3,2,1,0:T(8,128)(2,1)} custom-call(s32[3]{0:T(128)} %pad_add_fusion.at_ref, bf16[8,48,256]{2,1,0:T(8,128)(2,1)} %bitcast.85, bf16[8,48,256]{2,1,0:T(8,128)(2,1)} %copy-done.8, bf16[8,48,256]{2,1,0:T(8,128)(2,1)} %copy-done.7, bf16[8,48,256]{2,1,0:T(8,128)(2,1)} %copy-done.6, bf16[8,2,128,128]{3,2,1,0:T(8,128)(2,1)} %bitcast.78), custom_call_target="tpu_custom_call" | custom-call | flops 1000 | bytes 1000 | tf_op jit(solution)/shard_map/route_back/pallas_call | solution.py:299
  202.9 10.0 %all-to-all-done.6 = bf16[8,128,256]{2,1,0:T(8,128)(2,1)S(1)} async-done(((bf16[8,128,256]{2,1,0:T(8,128)(2,1)}), bf16[8,128,256]{2,1,0:T(8,128)(2,1)S(1)}, u32[]{:S(2)}, u32[]{:S(2)}) %all-to-all-start.6) | async-done | bytes 524320 | tf_op jit(solution)/shard_map/all_to_all | solution.py:472
  212.9 0.8 copy-done.5
  213.7 10.6 %all-to-all-start.7 = ((bf16[64,4,48,128]{3,2,1,0:T(8,128)(2,1)}), bf16[64,4,48,128]{3,2,1,0:T(8,128)(2,1)S(1)}, u32[]{:S(2)}, u32[]{:S(2)}) async-start(bf16[64,4,48,128]{3,2,1,0:T(8,128)(2,1)} %bitcast.71), calls=%async_computation.8 | async-start | bytes 6291456 | tf_op jit(solution)/shard_map/all_to_all | solution.py:472
  224.3 0.0 all-gather.5.cloned.1.call-start
  224.3 1.8 reduce_sum.12
  226.1 0.0 all-gather.5.cloned.1.call-update
  226.1 41.6 %all-to-all-done.7.back_ref = bf16[64,4,48,128]{3,2,1,0:T(8,128)(2,1)S(1)} async-done(((bf16[64,4,48,128]{3,2,1,0:T(8,128)(2,1)}), bf16[64,4,48,128]{3,2,1,0:T(8,128)(2,1)S(1)}, u32[]{:S(2)}, u32[]{:S(2)}) %all-to-all-start.7) | async-done | bytes 3145760 | tf_op jit(solution)/shard_map/all_to_all | solution.py:472
  267.7 5.3 %all-to-all-start.8 = ((bf16[64,2,48,128]{3,2,1,0:T(8,128)(2,1)}), bf16[64,2,48,128]{3,2,1,0:T(8,128)(2,1)}, u32[]{:S(2)}, u32[]{:S(2)}) async-start(bf16[64,2,48,128]{3,2,1,0:T(8,128)(2,1)} %pack_rows.5), calls=%async_computation.9 | async-start | bytes 3145728 | tf_op jit(solution)/shard_map/all_to_all | solution.py:472
  273.0 7.4 %early_weights.1 = (f32[8,128,256]{2,1,0:T(8,128)}, f32[8,256,128]{2,1,0:T(8,128)}) custom-call(s32[3]{0:T(128)} %pad_add_fusion.at_ref, bf16[8,48,256]{2,1,0:T(8,128)(2,1)} %bitcast.86, bf16[8,48,256]{2,1,0:T(8,128)(2,1)} %copy-done.8, bf16[8,48,256]{2,1,0:T(8,128)(2,1)} %copy-done.7, bf16[8,48,256]{2,1,0:T(8,128)(2,1)} %copy-done.6, ...), custom_call_target="tpu_custom_call" | custom-call | flops 1000 | bytes 1000 | tf_op jit(solution)/shard_map/early_weights/pallas_call | solution.py:356
  280.5 6.8 %unpack_rows.1.rows_ref = f32[4,4,256,128]{3,2,1,0:T(8,128)} custom-call(s32[4,4,2,256]{3,2,1,0:T(2,128)} %get-tuple-element.30.rho_ref, bf16[64,4,48,128]{3,2,1,0:T(8,128)(2,1)} %copy-done.1, bf16[384,384]{1,0:T(8,128)(2,1)} %constant.53.clone.swap_ref), custom_call_target="tpu_custom_call" | custom-call | flops 1000 | bytes 1000 | tf_op jit(solution)/shard_map/unpack_rows/pallas_call | solution.py:431
  287.3 12.0 %all-to-all-done.8 = bf16[64,2,48,128]{3,2,1,0:T(8,128)(2,1)} async-done(((bf16[64,2,48,128]{3,2,1,0:T(8,128)(2,1)}), bf16[64,2,48,128]{3,2,1,0:T(8,128)(2,1)}, u32[]{:S(2)}, u32[]{:S(2)}) %all-to-all-start.8) | async-done | bytes 1572896 | tf_op jit(solution)/shard_map/all_to_all | solution.py:472
  299.3 5.7 %late_weights.1 = bf16[8,2,2,128,128]{4,3,2,1,0:T(8,128)(2,1)} custom-call(s32[3]{0:T(128)} %pad_add_fusion.at_ref, bf16[8,48,256]{2,1,0:T(8,128)(2,1)} %bitcast.87, bf16[8,48,256]{2,1,0:T(8,128)(2,1)} %copy-done.8, bf16[8,48,256]{2,1,0:T(8,128)(2,1)} %copy-done.7, bf16[8,48,256]{2,1,0:T(8,128)(2,1)} %copy-done.6, bf16[8,8,96,128]{3,2,1,0:T(8,128)(2,1)} %bitcast.39.hid_ref, ...), custom_call_target="tpu_custom_call" | custom-call | flops 1000 | bytes 1000 | tf_op jit(solution)/shard_map/late_weights/pallas_call | solution.py:356
  305.0 3.6 %all-to-all-start.9 = ((bf16[16,2,128,128]{3,2,1,0:T(8,128)(2,1)}), bf16[16,2,128,128]{3,2,1,0:T(8,128)(2,1)S(1)}, u32[]{:S(2)}, u32[]{:S(2)}) async-start(bf16[16,2,128,128]{3,2,1,0:T(8,128)(2,1)} %bitcast.76), calls=%async_computation.10 | async-start | bytes 2097152 | tf_op jit(solution)/shard_map/all_to_all | solution.py:472
  308.6 3.1 all-gather.5.cloned.1.call-done.dkv_ref
  311.7 3.0 projection.1
  314.7 4.1 %collective-permute-start.3 = (bf16[128,256]{1,0:T(8,128)(2,1)}, bf16[128,256]{1,0:T(8,128)(2,1)S(1)}, u32[]{:S(2)}, u32[]{:S(2)}) collective-permute-start(bf16[128,256]{1,0:T(8,128)(2,1)} %projection.1), channel_id=1, source_target_pairs={{0,1},{1,0},{2,3},{3,2},{4,5},{5,4},{6,7},{7,6},{8,9},{9,8},{10,11... | collective-permute-start | bytes 196616 | tf_op jit(solution)/shard_map/ppermute | solution.py:477
  318.8 0.6 pad_maximum_fusion.1.wkv_ref
  319.4 0.5 collective-permute-done.3
  319.9 0.9 fusion.5
  320.8 1.1 collective-permute-start.5
  321.8 1.4 collective-permute-start.4
  323.2 2.0 collective-permute-start.6
  325.2 4.5 %finish_rows.1 = bf16[4,4,256,128]{3,2,1,0:T(8,128)(2,1)} custom-call(f32[4,4,256,128]{3,2,1,0:T(8,128)} %unpack_rows.1.rows_ref, bf16[4,4,256,256]{3,2,1,0:T(8,128)(2,1)} %bitcast.79, bf16[128,256]{1,0:T(8,128)(2,1)} %pad_maximum_fusion.1.wkv_ref), custom_call_target="tpu_custom_call" | custom-call | flops 5000000000 | bytes 10000000 | tf_op jit(solution)/shard_map/finish_rows/pallas_call | solution.py:455
  329.8 0.7 fusion.6
  330.4 1.6 fusion
  (41 shorter events, 0.1 us)
Async XLA Ops:
  7.2 15.7 %all-to-all-start = ((bf16[16,128,128]{2,1,0:T(8,128)(2,1)}), bf16[16,128,128]{2,1,0:T(8,128)(2,1)S(1)}, u32[]{:S(2)}, u32[]{:S(2)}) async-start(bf16[16,128,128]{2,1,0:T(8,128)(2,1)} %param.22), calls=%async_computation | async-start | bytes 1048576 | tf_op jit(solution)/shard_map/all_to_all | solution.py:472
  22.8 0.8 copy-start.3
  22.8 10.7 %copy-start.11 = (bf16[1,128,128]{2,1,0:T(8,128)(2,1)S(1)}, bf16[1,128,128]{2,1,0:T(8,128)(2,1)}, u32[]{:S(2)}) copy-start(bf16[1,128,128]{2,1,0:T(8,128)(2,1)} %param.18) | copy-start | bytes 98308
  22.9 10.7 %copy-start.12 = (bf16[1,128,128]{2,1,0:T(8,128)(2,1)S(1)}, bf16[1,128,128]{2,1,0:T(8,128)(2,1)}, u32[]{:S(2)}) copy-start(bf16[1,128,128]{2,1,0:T(8,128)(2,1)} %param.17) | copy-start | bytes 98308
  23.6 52.8 %all-to-all-start.1 = ((bf16[64,4,48,128]{3,2,1,0:T(8,128)(2,1)}), bf16[64,4,48,128]{3,2,1,0:T(8,128)(2,1)S(1)}, u32[]{:S(2)}, u32[]{:S(2)}) async-start(bf16[64,4,48,128]{3,2,1,0:T(8,128)(2,1)} %get-tuple-element.32), calls=%async_computation.1 | async-start | bytes 6291456 | tf_op jit(solution)/shard_map/all_to_all | solution.py:472
  33.5 95.4 %all-gather.3.cloned.1.call-start = ((), (), s32[]{:S(2)}) async-start(), calls=%async_computation.11 | async-start | bytes 2162688 | tf_op jit(solution)/shard_map/all_gather | solution.py:495
  38.6 4.3 %copy-start.10 = (bf16[1,128,2,128]{3,2,1,0:T(2,128)(2,1)S(1)}, bf16[1,128,2,128]{3,2,1,0:T(2,128)(2,1)}, u32[]{:S(2)}) copy-start(bf16[1,128,2,128]{3,2,1,0:T(2,128)(2,1)} %param.16) | copy-start | bytes 196612
  76.4 1.6 copy-start
  85.4 42.1 %copy-start.15 = (f32[1,128,2]{1,2,0:T(2,128)S(1)}, f32[1,128,2]{1,2,0:T(2,128)}, u32[]{:S(2)}) copy-start(f32[1,128,2]{1,2,0:T(2,128)} %param.20) | copy-start | bytes 3076
  121.2 29.5 %all-to-all-start.3 = ((bf16[64,2,48,128]{3,2,1,0:T(8,128)(2,1)}), bf16[64,2,48,128]{3,2,1,0:T(8,128)(2,1)S(1)}, u32[]{:S(2)}, u32[]{:S(2)}) async-start(bf16[64,2,48,128]{3,2,1,0:T(8,128)(2,1)} %pack_rows.4), calls=%async_computation.3 | async-start | bytes 3145728 | tf_op jit(solution)/shard_map/all_to_all | solution.py:472
  127.3 62.6 %reduce-scatter.2.cloned.1.call-start = ((), (), s32[]{:S(2)}) async-start(), calls=%async_computation.12 | async-start | bytes 2621440 | tf_op jit(solution)/shard_map/reduce_scatter | solution.py:517
  141.6 9.1 %copy-start.9 = (bf16[512,256]{1,0:T(8,128)(2,1)S(1)}, bf16[512,256]{1,0:T(8,128)(2,1)}, u32[]{:S(2)}) copy-start(bf16[512,256]{1,0:T(8,128)(2,1)} %get-tuple-element.44) | copy-start | bytes 786436
  150.7 19.9 %copy-start.2 = (bf16[64,2,48,128]{3,2,1,0:T(8,128)(2,1)}, bf16[64,2,48,128]{3,2,1,0:T(8,128)(2,1)S(1)}, u32[]{:S(2)}) copy-start(bf16[64,2,48,128]{3,2,1,0:T(8,128)(2,1)S(1)} %all-to-all-done.3) | copy-start | bytes 4718596
  165.1 24.7 %all-to-all-start.5 = ((bf16[16,128,128]{2,1,0:T(8,128)(2,1)}), bf16[16,128,128]{2,1,0:T(8,128)(2,1)S(1)}, u32[]{:S(2)}, u32[]{:S(2)}) async-start(bf16[16,128,128]{2,1,0:T(8,128)(2,1)} %param.21), calls=%async_computation.5 | async-start | bytes 1048576 | tf_op jit(solution)/shard_map/all_to_all | solution.py:472
  170.7 6.8 %collective-permute-start.2 = (bf16[8,48,256]{2,1,0:T(8,128)(2,1)}, bf16[8,48,256]{2,1,0:T(8,128)(2,1)S(1)}, u32[]{:S(2)}, u32[]{:S(2)}) collective-permute-start(bf16[8,48,256]{2,1,0:T(8,128)(2,1)} %bitcast.82), channel_id=1, source_target_pairs={{0,48},{16,0},{32,16},{48,32},{1,49},{17,1},{33,17},{49,33},{2,50}... | collective-permute-start | bytes 589832 | tf_op jit(solution)/shard_map/ppermute | solution.py:477
  170.8 11.3 %collective-permute-start.1 = (bf16[8,48,256]{2,1,0:T(8,128)(2,1)}, bf16[8,48,256]{2,1,0:T(8,128)(2,1)S(1)}, u32[]{:S(2)}, u32[]{:S(2)}) collective-permute-start(bf16[8,48,256]{2,1,0:T(8,128)(2,1)} %bitcast.83), channel_id=1, source_target_pairs={{0,32},{16,48},{32,0},{48,16},{1,33},{17,49},{33,1},{49,17},{2,34}... | collective-permute-start | bytes 589832 | tf_op jit(solution)/shard_map/ppermute | solution.py:477
  174.7 15.1 %collective-permute-start = (bf16[8,48,256]{2,1,0:T(8,128)(2,1)}, bf16[8,48,256]{2,1,0:T(8,128)(2,1)S(1)}, u32[]{:S(2)}, u32[]{:S(2)}) collective-permute-start(bf16[8,48,256]{2,1,0:T(8,128)(2,1)} %bitcast.84), channel_id=1, source_target_pairs={{0,16},{16,32},{32,48},{48,0},{1,17},{17,33},{33,49},{49,1},{2,18}... | collective-permute-start | bytes 589832 | tf_op jit(solution)/shard_map/ppermute | solution.py:477
  177.5 20.3 %copy-start.6 = (bf16[8,48,256]{2,1,0:T(8,128)(2,1)}, bf16[8,48,256]{2,1,0:T(8,128)(2,1)S(1)}, u32[]{:S(2)}) copy-start(bf16[8,48,256]{2,1,0:T(8,128)(2,1)S(1)} %collective-permute-done.2.d_ref) | copy-start | bytes 589828
  182.1 15.7 %copy-start.7 = (bf16[8,48,256]{2,1,0:T(8,128)(2,1)}, bf16[8,48,256]{2,1,0:T(8,128)(2,1)S(1)}, u32[]{:S(2)}) copy-start(bf16[8,48,256]{2,1,0:T(8,128)(2,1)S(1)} %collective-permute-done.1.c_ref) | copy-start | bytes 589828
  189.8 8.0 %copy-start.8 = (bf16[8,48,256]{2,1,0:T(8,128)(2,1)}, bf16[8,48,256]{2,1,0:T(8,128)(2,1)S(1)}, u32[]{:S(2)}) copy-start(bf16[8,48,256]{2,1,0:T(8,128)(2,1)S(1)} %collective-permute-done.b_ref) | copy-start | bytes 589828
  189.8 8.0 %copy-start.4 = (bf16[16,128,128]{2,1,0:T(8,128)(2,1)}, bf16[16,128,128]{2,1,0:T(8,128)(2,1)S(1)}, u32[]{:S(2)}) copy-start(bf16[16,128,128]{2,1,0:T(8,128)(2,1)S(1)} %all-to-all-done.5) | copy-start | bytes 1572868
  189.8 23.0 %all-to-all-start.6 = ((bf16[8,128,256]{2,1,0:T(8,128)(2,1)}), bf16[8,128,256]{2,1,0:T(8,128)(2,1)S(1)}, u32[]{:S(2)}, u32[]{:S(2)}) async-start(bf16[8,128,256]{2,1,0:T(8,128)(2,1)} %bitcast.91), calls=%async_computation.7 | async-start | bytes 1048576 | tf_op jit(solution)/shard_map/all_to_all | solution.py:472
  212.9 0.8 copy-start.5
  213.7 54.0 %all-to-all-start.7 = ((bf16[64,4,48,128]{3,2,1,0:T(8,128)(2,1)}), bf16[64,4,48,128]{3,2,1,0:T(8,128)(2,1)S(1)}, u32[]{:S(2)}, u32[]{:S(2)}) async-start(bf16[64,4,48,128]{3,2,1,0:T(8,128)(2,1)} %bitcast.71), calls=%async_computation.8 | async-start | bytes 6291456 | tf_op jit(solution)/shard_map/all_to_all | solution.py:472
  224.3 87.4 %all-gather.5.cloned.1.call-start = ((), (), s32[]{:S(2)}) async-start(), calls=%async_computation.13 | async-start | bytes 2162688 | tf_op jit(solution)/shard_map/all_gather | solution.py:525
  267.7 12.8 %copy-start.1 = (bf16[64,4,48,128]{3,2,1,0:T(8,128)(2,1)}, bf16[64,4,48,128]{3,2,1,0:T(8,128)(2,1)S(1)}, u32[]{:S(2)}) copy-start(bf16[64,4,48,128]{3,2,1,0:T(8,128)(2,1)S(1)} %all-to-all-done.7.back_ref) | copy-start | bytes 9437188
  267.7 31.6 %all-to-all-start.8 = ((bf16[64,2,48,128]{3,2,1,0:T(8,128)(2,1)}), bf16[64,2,48,128]{3,2,1,0:T(8,128)(2,1)}, u32[]{:S(2)}, u32[]{:S(2)}) async-start(bf16[64,2,48,128]{3,2,1,0:T(8,128)(2,1)} %pack_rows.5), calls=%async_computation.9 | async-start | bytes 3145728 | tf_op jit(solution)/shard_map/all_to_all | solution.py:472
  305.0 25.5 %all-to-all-start.9 = ((bf16[16,2,128,128]{3,2,1,0:T(8,128)(2,1)}), bf16[16,2,128,128]{3,2,1,0:T(8,128)(2,1)S(1)}, u32[]{:S(2)}, u32[]{:S(2)}) async-start(bf16[16,2,128,128]{3,2,1,0:T(8,128)(2,1)} %bitcast.76), calls=%async_computation.10 | async-start | bytes 2097152 | tf_op jit(solution)/shard_map/all_to_all | solution.py:472
  308.5 10.3 %copy-start.13 = (bf16[128,128]{1,0:T(8,128)(2,1)S(1)}, bf16[128,128]{1,0:T(8,128)(2,1)}, u32[]{:S(2)}) copy-start(bf16[128,128]{1,0:T(8,128)(2,1)} %param.24) | copy-start | bytes 98308
  308.5 10.2 %copy-start.14 = (bf16[128,128]{1,0:T(8,128)(2,1)S(1)}, bf16[128,128]{1,0:T(8,128)(2,1)}, u32[]{:S(2)}) copy-start(bf16[128,128]{1,0:T(8,128)(2,1)} %param.23) | copy-start | bytes 98308
  314.7 5.2 %collective-permute-start.3 = (bf16[128,256]{1,0:T(8,128)(2,1)}, bf16[128,256]{1,0:T(8,128)(2,1)S(1)}, u32[]{:S(2)}, u32[]{:S(2)}) collective-permute-start(bf16[128,256]{1,0:T(8,128)(2,1)} %projection.1), channel_id=1, source_target_pairs={{0,1},{1,0},{2,3},{3,2},{4,5},{5,4},{6,7},{7,6},{8,9},{9,8},{10,11... | collective-permute-start | bytes 196616 | tf_op jit(solution)/shard_map/ppermute | solution.py:477
  320.8 9.0 %collective-permute-start.5 = (bf16[128,256]{1,0:T(8,128)(2,1)S(1)}, bf16[128,256]{1,0:T(8,128)(2,1)S(1)}, u32[]{:S(2)}, u32[]{:S(2)}) collective-permute-start(bf16[128,256]{1,0:T(8,128)(2,1)S(1)} %get-tuple-element.56), channel_id=1, source_target_pairs={{0,2},{2,4},{4,6},{6,0},{1,3},{3,5},{5,7},{7,1},{8,10},{10,12},{12... | collective-permute-start | bytes 196616 | tf_op jit(solution)/shard_map/ppermute | solution.py:477
  321.8 7.9 %collective-permute-start.4 = (bf16[128,256]{1,0:T(8,128)(2,1)S(1)}, bf16[128,256]{1,0:T(8,128)(2,1)S(1)}, u32[]{:S(2)}, u32[]{:S(2)}) collective-permute-start(bf16[128,256]{1,0:T(8,128)(2,1)S(1)} %get-tuple-element.56), channel_id=1, source_target_pairs={{0,4},{2,6},{4,0},{6,2},{1,5},{3,7},{5,1},{7,3},{8,12},{10,14},{12... | collective-permute-start | bytes 196616 | tf_op jit(solution)/shard_map/ppermute | solution.py:477
  323.2 6.5 %collective-permute-start.6 = (bf16[128,256]{1,0:T(8,128)(2,1)S(1)}, bf16[128,256]{1,0:T(8,128)(2,1)S(1)}, u32[]{:S(2)}, u32[]{:S(2)}) collective-permute-start(bf16[128,256]{1,0:T(8,128)(2,1)S(1)} %get-tuple-element.56), channel_id=1, source_target_pairs={{0,6},{2,0},{4,2},{6,4},{1,7},{3,1},{5,3},{7,5},{8,14},{10,8},{12,... | collective-permute-start | bytes 196616 | tf_op jit(solution)/shard_map/ppermute | solution.py:477
Sparse Core Ops, SparseCore 0:
  37.5 86.2 all-gather.2
  141.8 32.7 reduce-scatter.1
  228.6 83.0 all-gather.4

commit v5 on v4

--- a/solution.py
+++ b/solution.py
@@ -406,7 +406,7 @@
     return pl.pallas_call(
         projection_kernel,
         out_shape=jax.ShapeDtypeStruct((HD, 2 * HD), BF16),
-        cost_estimate=pl.CostEstimate(flops=1000, bytes_accessed=1000, transcendentals=0),
+        cost_estimate=pl.CostEstimate(flops=80000000000, bytes_accessed=1000, transcendentals=0),
         compiler_params=params(0),
         name="projection",
     )(hid, dkv)
@@ -517,25 +517,23 @@
     dkv_x = lax.psum_scatter(dkv_part, "x", scatter_dimension=0, tiled=True)
     mine = exchange(after(slots, hid_a).reshape(64, PAD, 2 * HD), WIDE).reshape(64 * PAD, 2 * HD)
     dqg = unpad_rows(mine, unpad).reshape(8, 8 * ROWS, 2 * HD)
-    first = dqg
     dqg = gather(dqg, "zh")
-    w_query_r = exchange(after(w_query, mine), SLAB).reshape(8, EPD, HD, HD)
-    dkv_z = exchange(after(dkv_x, w_query_r, *dqg).reshape(8, BLOCK, 2 * HD), ("zh", "zl"))
+    dkv_z = exchange(after(dkv_x, *dqg).reshape(8, BLOCK, 2 * HD), ("zh", "zl"))
     dkv_own = dkv_z.astype(F32).sum(axis=0).astype(BF16)
     dkv = lax.all_gather(dkv_own, SEQ, axis=0, tiled=True)
+    proj = projection(hidden[0], dkv)
+    hid_b = exchange(after(hid_b, dkv_own), WIDE)
+    wq, wo = early_weights(at, dqg, hid_a, grad_rows)
+    w_query_r = exchange(after(w_query, hid_b, wq), SLAB).reshape(8, EPD, HD, HD)
     back_rows = route_back(at, dqg, w_query_r).reshape(64, 4, 8 * ROWS, HD)
-    back = exchange(after(back_rows, dkv_z), WIDE)
-    hid_b = exchange(after(hid_b, back), WIDE)
-    unpacked = unpack(rho, back, swap)
+    back = exchange(back_rows, WIDE)
     dqg[0] = after(dqg[0], back_rows)
-    wq, wo = early_weights(at, dqg, hid_a, grad_rows)
-    dqg[0] = after(dqg[0], unpacked, wq)
     grads = late_weights(at, dqg, hid_b, wq, wo).reshape(16, 2, HD, HD)
-    grads = exchange(grads, SLAB)
+    grads = exchange(after(grads, back, proj), SLAB)
     grad_wq, grad_wo = grads[:, 0].astype(F32), grads[:, 1].astype(F32)
 
     wkv = jnp.concatenate([w_key, w_value], axis=1)
-    proj = projection(hidden[0], dkv)
+    unpacked = unpack(rho, after(back, proj), swap)
     grad_hidden = finish(unpacked, dkv.reshape(4, 4, 2 * BLOCK, 2 * HD), wkv).reshape(1, 4096, HD)
     proj = sum(p.astype(F32) for p in gather(proj, "dev")).astype(BF16)
     proj = [p.astype(F32) for p in gather(proj, "node")]

time: 340 us -> 344 us (1.012)
  blocking collectives: 50.2 us -> 85.7 us
  starting transfers between devices: 65.9 us -> 46.7 us
  waiting for transfers between devices: 122 us -> 111 us
    all_to_all x2 -> x4, blocking collectives: 50.2 us -> 85.7 us  [exchange(): return lax.all_to_all(rows, axes, split_axis=0, concat_axis=0, tiled=True)]
    all_to_all x8 -> x6, waiting for transfers between devices: 103 us -> 82.9 us  [exchange(): return lax.all_to_all(rows, axes, split_axis=0, concat_axis=0, tiled=True)]
    all_to_all x8 -> x6, starting transfers between devices: 53 us -> 38.6 us  [exchange(): return lax.all_to_all(rows, axes, split_axis=0, concat_axis=0, tiled=True)]
    all_gather x1, waiting for transfers between devices: 3.11 us -> 11.7 us  [per_device(): dkv = lax.all_gather(dkv_own, SEQ, axis=0, tiled=True)]
    ppermute x7, starting transfers between devices: 12.6 us -> 7.72 us  [shifted(): return lax.ppermute(rows, axis, [(i, (i + s) % n) for i in range(n)])]
  transfers between devices with their start and end apart: 18 -> 16, of which waited for: 10 -> 9; matrix products, arithmetic and copies ran while one was open for 3% -> 2% of each run, Pallas kernels for 22% -> 21%
where the time goes in v5:
time: 344 us; the launch traced here: 343 us
  waiting for transfers between devices  111 us (32%)
  blocking collectives  85.7 us (25%)
  Pallas kernels  72.8 us (21%)
  starting transfers between devices  46.7 us (14%)
  between operations  14 us (4%)
  other arithmetic  7.34 us (2%)
  local copies, waits for them, and re-layouts  5.02 us (1%)
    all_to_all x4, blocking collectives, exchange(): return lax.all_to_all(rows, axes, split_axis=0, concat_axis=0, tiled=True)  85.7 us
    all_to_all x6, waiting for transfers between devices, exchange(): return lax.all_to_all(rows, axes, split_axis=0, concat_axis=0, tiled=True)  82.9 us
    all_to_all x6, starting transfers between devices, exchange(): return lax.all_to_all(rows, axes, split_axis=0, concat_axis=0, tiled=True)  38.6 us
    pallas_call x3, Pallas kernels, pack(): pl.pallas_call(kernel, grid=(steps,), in_specs=[id_spec, slab, pl.BlockSp...  18.1 us
    ppermute x7, waiting for transfers between devices, shifted(): return lax.ppermute(rows, axis, [(i, (i + s) % n) for i in range(n)])  16.6 us
    pallas_call x2, Pallas kernels, weights_call(): pl.pallas_call(kernel, grid=(4,), in_specs=[pl.BlockSpec(memory_space=plt...  13.2 us
    all_gather x1, waiting for transfers between devices, per_device(): dkv = lax.all_gather(dkv_own, SEQ, axis=0, tiled=True)  11.7 us
    ppermute x7, starting transfers between devices, shifted(): return lax.ppermute(rows, axis, [(i, (i + s) % n) for i in range(n)])  7.72 us
  transfers between devices with their start and end apart: 16, of which 9 were waited for; matrix products, arithmetic and copies ran while one was open for 2% of the time, Pallas kernels for 21%

profile of v5, /device:TPU:1, one launch (start us, length us, event | category | flops | bytes accessed | tf_op | source)
XLA Modules:
  0.0 342.7 jit_solution(12901565715368429995)
XLA Ops:
  7.2 6.2 %all-to-all-start = ((bf16[16,128,128]{2,1,0:T(8,128)(2,1)}), bf16[16,128,128]{2,1,0:T(8,128)(2,1)S(1)}, u32[]{:S(2)}, u32[]{:S(2)}) async-start(bf16[16,128,128]{2,1,0:T(8,128)(2,1)} %param.22), calls=%async_computation | async-start | bytes 1048576 | tf_op jit(solution)/shard_map/all_to_all | solution.py:472
  13.4 9.4 %pack_rows.3 = (bf16[64,4,48,128]{3,2,1,0:T(8,128)(2,1)}, s32[4,4,2,256]{3,2,1,0:T(2,128)}) custom-call(s32[4,4,2,256]{3,2,1,0:T(2,128)} %bitcast.99, bf16[4,4,256,128]{3,2,1,0:T(8,128)(2,1)} %bitcast.88, bf16[384,384]{1,0:T(8,128)(2,1)} %constant.53.clone.swap_ref), custom_call_target="tpu_custom_call" | custom-call | flops 1000 | bytes 1000 | tf_op jit(solution)/shard_map/pack_rows/pallas_call | solution.py:115
  22.8 0.0 copy-start.4
  22.8 0.0 copy-start.13
  22.9 0.8 copy-done.4
  23.6 9.8 %all-to-all-start.1 = ((bf16[64,4,48,128]{3,2,1,0:T(8,128)(2,1)}), bf16[64,4,48,128]{3,2,1,0:T(8,128)(2,1)S(1)}, u32[]{:S(2)}, u32[]{:S(2)}) async-start(bf16[64,4,48,128]{3,2,1,0:T(8,128)(2,1)} %get-tuple-element.32), calls=%async_computation.1 | async-start | bytes 6291456 | tf_op jit(solution)/shard_map/all_to_all | solution.py:472
  33.5 0.0 all-gather.3.cloned.1.call-start
  33.5 0.6 pad_maximum_fusion
  34.2 0.0 all-gather.3.cloned.1.call-update
  34.2 4.3 %pack_rows.5 = bf16[64,2,48,128]{3,2,1,0:T(8,128)(2,1)} custom-call(s32[4,4,2,256]{3,2,1,0:T(2,128)} %get-tuple-element.30.rho_ref, bf16[4,4,256,128]{3,2,1,0:T(8,128)(2,1)} %bitcast.74, bf16[384,384]{1,0:T(8,128)(2,1)} %constant.53.clone.swap_ref), custom_call_target="tpu_custom_call" | custom-call | flops 1000 | bytes 1000 | tf_op jit(solution)/shard_map/pack_rows/pallas_call | solution.py:115
  38.5 4.3 %pack_rows.4 = bf16[64,2,48,128]{3,2,1,0:T(8,128)(2,1)} custom-call(s32[4,4,2,256]{3,2,1,0:T(2,128)} %get-tuple-element.30.rho_ref, bf16[4,4,256,128]{3,2,1,0:T(8,128)(2,1)} %bitcast.75, bf16[384,384]{1,0:T(8,128)(2,1)} %constant.53.clone.swap_ref), custom_call_target="tpu_custom_call" | custom-call | flops 1000 | bytes 1000 | tf_op jit(solution)/shard_map/pack_rows/pallas_call | solution.py:115
  42.9 0.6 copy.39
  43.5 0.6 compare_bitcast_fusion
  44.1 0.2 copy.44
  44.3 0.1 copy.32
  44.5 0.1 copy.34
  44.6 0.6 fusion.4.rho_row_ref
  45.2 0.7 fusion.3.rho_col_ref
  45.9 30.5 %all-to-all-done.1 = bf16[64,4,48,128]{3,2,1,0:T(8,128)(2,1)S(1)} async-done(((bf16[64,4,48,128]{3,2,1,0:T(8,128)(2,1)}), bf16[64,4,48,128]{3,2,1,0:T(8,128)(2,1)S(1)}, u32[]{:S(2)}, u32[]{:S(2)}) %all-to-all-start.1) | async-done | bytes 3145760 | tf_op jit(solution)/shard_map/all_to_all | solution.py:472
  76.4 1.6 copy-done
  78.0 4.8 %head_sums.1 = (bf16[8,48,128]{2,1,0:T(8,128)(2,1)}, bf16[8,48,128]{2,1,0:T(8,128)(2,1)}, bf16[8,48,128]{2,1,0:T(8,128)(2,1)}, bf16[8,48,128]{2,1,0:T(8,128)(2,1)}) custom-call(bf16[8,8,192,128]{3,2,1,0:T(8,128)(2,1)} %bitcast.69, bf16[8,256,128]{2,1,0:T(8,128)(2,1)} %bitcast.78), custom_call_target="tpu_custom_call" | custom-call | flops 1000 | bytes 1000 | tf_op jit(solution)/shard_map/head_sums/pallas_call | solution.py:144
  82.9 2.6 address_heads.1
  85.4 35.8 %all_to_all.50 = bf16[256,8,128]{2,1,0:T(8,128)(2,1)} all-to-all(bf16[256,8,128]{2,1,0:T(8,128)(2,1)} %bitcast.80), channel_id=1, replica_groups=mesh['x'=4,'zh'=4,'zl'=2,'node'=4,'dev'=2] {'x','zh','zl','node','dev'}, dimensions={0} | all-to-all | bytes 1048576 | tf_op jit(solution)/shard_map/all_to_all | solution.py:472
  121.2 6.0 %all-to-all-start.3 = ((bf16[64,2,48,128]{3,2,1,0:T(8,128)(2,1)}), bf16[64,2,48,128]{3,2,1,0:T(8,128)(2,1)S(1)}, u32[]{:S(2)}, u32[]{:S(2)}) async-start(bf16[64,2,48,128]{3,2,1,0:T(8,128)(2,1)} %pack_rows.4), calls=%async_computation.3 | async-start | bytes 3145728 | tf_op jit(solution)/shard_map/all_to_all | solution.py:472
  127.2 0.2 reduce-scatter.2.cloned.1.call-start
  127.5 0.8 copy.41.gate_ref
  128.3 0.6 pad_add_fusion.at_ref
  128.9 5.0 %attend_forward.1 = (bf16[256,4096]{1,0:T(8,128)(2,1)}, f32[256,128]{1,0:T(8,128)}, bf16[256,128]{1,0:T(8,128)(2,1)}) custom-call(s32[3]{0:T(128)} %pad_add_fusion.at_ref, bf16[256,128]{1,0:T(8,128)(2,1)} %bitcast.89, bf16[4096,256]{1,0:T(8,128)(2,1)} %all-gather.3.cloned.1.call-done.kv_ref, f32[256,1]{1,0:T(8,128)} %copy.41.gate_ref), custom_call_target="tpu_custom_call" | custom-call | flops 1000 | bytes 1000 | tf_op jit(solution)/shard_map/attend_forward/pallas_call | solution.py:207
  133.9 7.7 %attend_backward.1 = (bf16[512,256]{1,0:T(8,128)(2,1)}, bf16[4096,256]{1,0:T(8,128)(2,1)}) custom-call(bf16[2048,128]{1,0:T(8,128)(2,1)} %bitcast.81, s32[1,256]{1,0:T(1,128)} %fusion.4.rho_row_ref, s32[256,1]{1,0:T(8,128)} %fusion.3.rho_col_ref, f32[256,1]{1,0:T(8,128)} %copy.41.gate_ref, bf16[256,128]{1,0:T(8,128)(2,1)} %bitcast.90, ...), custom_call_target="tpu_custom_call" | custom-call | flops 1000 | bytes 1000 | tf_op jit(solution)/shard_map/attend_backward/pallas_call | solution.py:251
  141.6 0.0 reduce-scatter.2.cloned.1.call-update
  141.6 0.0 all-gather.5.cloned.1.call-start
  141.7 9.1 %all-to-all-done.3 = bf16[64,2,48,128]{3,2,1,0:T(8,128)(2,1)S(1)} async-done(((bf16[64,2,48,128]{3,2,1,0:T(8,128)(2,1)}), bf16[64,2,48,128]{3,2,1,0:T(8,128)(2,1)S(1)}, u32[]{:S(2)}, u32[]{:S(2)}) %all-to-all-start.3) | async-done | bytes 1572896 | tf_op jit(solution)/shard_map/all_to_all | solution.py:472
  150.7 14.4 %all_to_all.51 = bf16[64,8,256]{2,1,0:T(8,128)(2,1)} all-to-all(bf16[64,8,256]{2,1,0:T(8,128)(2,1)S(1)} %bitcast.92), channel_id=1, replica_groups=mesh['x'=4,'zh'=4,'zl'=2,'node'=4,'dev'=2] {'x','zl','node','dev'}, dimensions={0} | all-to-all | bytes 524288 | tf_op jit(solution)/shard_map/all_to_all | solution.py:472
  165.1 2.0 unpad_rows.1
  167.2 0.1 collective-permute-start.2
  167.3 3.9 %collective-permute-start.1 = (bf16[8,48,256]{2,1,0:T(8,128)(2,1)}, bf16[8,48,256]{2,1,0:T(8,128)(2,1)S(1)}, u32[]{:S(2)}, u32[]{:S(2)}) collective-permute-start(bf16[8,48,256]{2,1,0:T(8,128)(2,1)} %bitcast.83), channel_id=1, source_target_pairs={{0,32},{16,48},{32,0},{48,16},{1,33},{17,49},{33,1},{49,17},{2,34}... | collective-permute-start | bytes 589832 | tf_op jit(solution)/shard_map/ppermute | solution.py:477
  171.2 7.3 %collective-permute-done.2.d_ref = bf16[8,48,256]{2,1,0:T(8,128)(2,1)S(1)} collective-permute-done((bf16[8,48,256]{2,1,0:T(8,128)(2,1)}, bf16[8,48,256]{2,1,0:T(8,128)(2,1)S(1)}, u32[]{:S(2)}, u32[]{:S(2)}) %collective-permute-start.2) | collective-permute-done | bytes 196640 | tf_op jit(solution)/shard_map/ppermute | solution.py:477
  178.5 1.4 collective-permute-done.1.c_ref
  179.8 7.3 %collective-permute-done.b_ref = bf16[8,48,256]{2,1,0:T(8,128)(2,1)S(1)} collective-permute-done((bf16[8,48,256]{2,1,0:T(8,128)(2,1)}, bf16[8,48,256]{2,1,0:T(8,128)(2,1)S(1)}, u32[]{:S(2)}, u32[]{:S(2)}) %collective-permute-start) | collective-permute-done | bytes 196640 | tf_op jit(solution)/shard_map/ppermute | solution.py:477
  187.2 22.4 %all_to_all.52 = bf16[8,128,256]{2,1,0:T(8,128)(2,1)S(1)} all-to-all(bf16[8,128,256]{2,1,0:T(8,128)(2,1)} %bitcast.91), channel_id=1, replica_groups=mesh['x'=4,'zh'=4,'zl'=2,'node'=4,'dev'=2] {'zh','zl'}, dimensions={0} | all-to-all | bytes 1048576 | tf_op jit(solution)/shard_map/all_to_all | solution.py:472
  209.6 0.7 reduce_sum.12
  210.3 0.0 all-gather.5.cloned.1.call-update
  210.3 7.1 %all-to-all-start.6 = ((bf16[64,2,48,128]{3,2,1,0:T(8,128)(2,1)}), bf16[64,2,48,128]{3,2,1,0:T(8,128)(2,1)S(1)}, u32[]{:S(2)}, u32[]{:S(2)}) async-start(bf16[64,2,48,128]{3,2,1,0:T(8,128)(2,1)} %pack_rows.5), calls=%async_computation.7 | async-start | bytes 3145728 | tf_op jit(solution)/shard_map/all_to_all | solution.py:472
  217.5 0.0 copy-start.8
  217.5 7.5 %early_weights.1 = (f32[8,128,256]{2,1,0:T(8,128)}, f32[8,256,128]{2,1,0:T(8,128)}) custom-call(s32[3]{0:T(128)} %pad_add_fusion.at_ref, bf16[8,48,256]{2,1,0:T(8,128)(2,1)} %bitcast.85, bf16[8,48,256]{2,1,0:T(8,128)(2,1)} %copy-done.7, bf16[8,48,256]{2,1,0:T(8,128)(2,1)} %copy-done.6, bf16[8,48,256]{2,1,0:T(8,128)(2,1)} %copy-done.5, ...), custom_call_target="tpu_custom_call" | custom-call | flops 1000 | bytes 1000 | tf_op jit(solution)/shard_map/early_weights/pallas_call | solution.py:356
  225.0 17.8 %all-to-all-done.6 = bf16[64,2,48,128]{3,2,1,0:T(8,128)(2,1)S(1)} async-done(((bf16[64,2,48,128]{3,2,1,0:T(8,128)(2,1)}), bf16[64,2,48,128]{3,2,1,0:T(8,128)(2,1)S(1)}, u32[]{:S(2)}, u32[]{:S(2)}) %all-to-all-start.6) | async-done | bytes 1572896 | tf_op jit(solution)/shard_map/all_to_all | solution.py:472
  242.8 13.1 %all_to_all.53 = bf16[16,128,128]{2,1,0:T(8,128)(2,1)} all-to-all(bf16[16,128,128]{2,1,0:T(8,128)(2,1)S(1)} %copy-done.8), channel_id=1, replica_groups=mesh['x'=4,'zh'=4,'zl'=2,'node'=4,'dev'=2] {'x','zl'}, dimensions={0} | all-to-all | bytes 1048576 | tf_op jit(solution)/shard_map/all_to_all | solution.py:472
  255.9 5.0 %route_back.1 = bf16[8,8,192,128]{3,2,1,0:T(8,128)(2,1)} custom-call(s32[3]{0:T(128)} %pad_add_fusion.at_ref, bf16[8,48,256]{2,1,0:T(8,128)(2,1)} %bitcast.86, bf16[8,48,256]{2,1,0:T(8,128)(2,1)} %copy-done.7, bf16[8,48,256]{2,1,0:T(8,128)(2,1)} %copy-done.6, bf16[8,48,256]{2,1,0:T(8,128)(2,1)} %copy-done.5, bf16[8,2,128,128]{3,2,1,0:T(8,128)(2,1)} %bitcast.79), custom_call_target="tpu_custom_call" | custom-call | flops 1000 | bytes 1000 | tf_op jit(solution)/shard_map/route_back/pallas_call | solution.py:299
  261.0 5.2 %all-to-all-start.8 = ((bf16[64,4,48,128]{3,2,1,0:T(8,128)(2,1)}), bf16[64,4,48,128]{3,2,1,0:T(8,128)(2,1)S(1)}, u32[]{:S(2)}, u32[]{:S(2)}) async-start(bf16[64,4,48,128]{3,2,1,0:T(8,128)(2,1)} %bitcast.71), calls=%async_computation.9 | async-start | bytes 6291456 | tf_op jit(solution)/shard_map/all_to_all | solution.py:472
  266.2 5.7 %late_weights.1 = bf16[8,2,2,128,128]{4,3,2,1,0:T(8,128)(2,1)} custom-call(s32[3]{0:T(128)} %pad_add_fusion.at_ref, bf16[8,48,256]{2,1,0:T(8,128)(2,1)} %bitcast.87, bf16[8,48,256]{2,1,0:T(8,128)(2,1)} %copy-done.7, bf16[8,48,256]{2,1,0:T(8,128)(2,1)} %copy-done.6, bf16[8,48,256]{2,1,0:T(8,128)(2,1)} %copy-done.5, bf16[8,8,96,128]{3,2,1,0:T(8,128)(2,1)} %bitcast.73, ...), custom_call_target="tpu_custom_call" | custom-call | flops 1000 | bytes 1000 | tf_op jit(solution)/shard_map/late_weights/pallas_call | solution.py:356
  271.9 11.7 %all-gather.5.cloned.1.call-done.dkv_ref = bf16[4096,256]{1,0:T(8,128)(2,1)} async-done(((bf16[128,256]{1,0:T(8,128)(2,1)}), bf16[4096,256]{1,0:T(8,128)(2,1)}) %all-gather.5.cloned.1.call-update) | async-done | bytes 2097168 | tf_op jit(solution)/shard_map/all_gather | solution.py:523
  283.6 3.0 projection.1
  286.6 25.5 %all-to-all-done.8.back_ref = bf16[64,4,48,128]{3,2,1,0:T(8,128)(2,1)S(1)} async-done(((bf16[64,4,48,128]{3,2,1,0:T(8,128)(2,1)}), bf16[64,4,48,128]{3,2,1,0:T(8,128)(2,1)S(1)}, u32[]{:S(2)}, u32[]{:S(2)}) %all-to-all-start.8) | async-done | bytes 3145760 | tf_op jit(solution)/shard_map/all_to_all | solution.py:472
  312.2 4.2 %all-to-all-start.9 = ((bf16[16,2,128,128]{3,2,1,0:T(8,128)(2,1)}), bf16[16,2,128,128]{3,2,1,0:T(8,128)(2,1)}, u32[]{:S(2)}, u32[]{:S(2)}) async-start(bf16[16,2,128,128]{3,2,1,0:T(8,128)(2,1)} %bitcast.77), calls=%async_computation.10 | async-start | bytes 2097152 | tf_op jit(solution)/shard_map/all_to_all | solution.py:472
  316.4 0.1 collective-permute-start.3
  316.5 0.6 pad_maximum_fusion.1.wkv_ref
  317.2 0.6 collective-permute-done.3
  317.8 1.1 collective-permute-start.5
  318.9 0.4 collective-permute-start.4
  319.3 2.1 collective-permute-start.6
  321.4 6.8 %unpack_rows.1.rows_ref = f32[4,4,256,128]{3,2,1,0:T(8,128)} custom-call(s32[4,4,2,256]{3,2,1,0:T(2,128)} %get-tuple-element.30.rho_ref, bf16[64,4,48,128]{3,2,1,0:T(8,128)(2,1)} %copy-done.1, bf16[384,384]{1,0:T(8,128)(2,1)} %constant.53.clone.swap_ref), custom_call_target="tpu_custom_call" | custom-call | flops 1000 | bytes 1000 | tf_op jit(solution)/shard_map/unpack_rows/pallas_call | solution.py:431
  328.2 4.5 %finish_rows.1 = bf16[4,4,256,128]{3,2,1,0:T(8,128)(2,1)} custom-call(f32[4,4,256,128]{3,2,1,0:T(8,128)} %unpack_rows.1.rows_ref, bf16[4,4,256,256]{3,2,1,0:T(8,128)(2,1)} %bitcast.108, bf16[128,256]{1,0:T(8,128)(2,1)} %pad_maximum_fusion.1.wkv_ref), custom_call_target="tpu_custom_call" | custom-call | flops 5000000000 | bytes 10000000 | tf_op jit(solution)/shard_map/finish_rows/pallas_call | solution.py:455
  332.7 0.7 fusion.6
  333.4 2.8 fusion
  (41 shorter events, 0.1 us)
Async XLA Ops:
  7.2 15.7 %all-to-all-start = ((bf16[16,128,128]{2,1,0:T(8,128)(2,1)}), bf16[16,128,128]{2,1,0:T(8,128)(2,1)S(1)}, u32[]{:S(2)}, u32[]{:S(2)}) async-start(bf16[16,128,128]{2,1,0:T(8,128)(2,1)} %param.22), calls=%async_computation | async-start | bytes 1048576 | tf_op jit(solution)/shard_map/all_to_all | solution.py:472
  22.8 0.8 copy-start.4
  22.8 10.7 %copy-start.12 = (bf16[1,128,128]{2,1,0:T(8,128)(2,1)S(1)}, bf16[1,128,128]{2,1,0:T(8,128)(2,1)}, u32[]{:S(2)}) copy-start(bf16[1,128,128]{2,1,0:T(8,128)(2,1)} %param.18) | copy-start | bytes 98308
  22.8 10.7 %copy-start.13 = (bf16[1,128,128]{2,1,0:T(8,128)(2,1)S(1)}, bf16[1,128,128]{2,1,0:T(8,128)(2,1)}, u32[]{:S(2)}) copy-start(bf16[1,128,128]{2,1,0:T(8,128)(2,1)} %param.17) | copy-start | bytes 98308
  23.6 52.8 %all-to-all-start.1 = ((bf16[64,4,48,128]{3,2,1,0:T(8,128)(2,1)}), bf16[64,4,48,128]{3,2,1,0:T(8,128)(2,1)S(1)}, u32[]{:S(2)}, u32[]{:S(2)}) async-start(bf16[64,4,48,128]{3,2,1,0:T(8,128)(2,1)} %get-tuple-element.32), calls=%async_computation.1 | async-start | bytes 6291456 | tf_op jit(solution)/shard_map/all_to_all | solution.py:472
  33.5 95.4 %all-gather.3.cloned.1.call-start = ((), (), s32[]{:S(2)}) async-start(), calls=%async_computation.11 | async-start | bytes 2162688 | tf_op jit(solution)/shard_map/all_gather | solution.py:495
  38.5 4.3 %copy-start.11 = (bf16[1,128,2,128]{3,2,1,0:T(2,128)(2,1)S(1)}, bf16[1,128,2,128]{3,2,1,0:T(2,128)(2,1)}, u32[]{:S(2)}) copy-start(bf16[1,128,2,128]{3,2,1,0:T(2,128)(2,1)} %param.16) | copy-start | bytes 196612
  76.4 1.6 copy-start
  85.4 42.0 %copy-start.16 = (f32[1,128,2]{1,2,0:T(2,128)S(1)}, f32[1,128,2]{1,2,0:T(2,128)}, u32[]{:S(2)}) copy-start(f32[1,128,2]{1,2,0:T(2,128)} %param.20) | copy-start | bytes 3076
  121.2 29.5 %all-to-all-start.3 = ((bf16[64,2,48,128]{3,2,1,0:T(8,128)(2,1)}), bf16[64,2,48,128]{3,2,1,0:T(8,128)(2,1)S(1)}, u32[]{:S(2)}, u32[]{:S(2)}) async-start(bf16[64,2,48,128]{3,2,1,0:T(8,128)(2,1)} %pack_rows.4), calls=%async_computation.3 | async-start | bytes 3145728 | tf_op jit(solution)/shard_map/all_to_all | solution.py:472
  127.2 59.9 %reduce-scatter.2.cloned.1.call-start = ((), (), s32[]{:S(2)}) async-start(), calls=%async_computation.12 | async-start | bytes 2621440 | tf_op jit(solution)/shard_map/reduce_scatter | solution.py:517
  141.6 9.1 %copy-start.9 = (bf16[512,256]{1,0:T(8,128)(2,1)S(1)}, bf16[512,256]{1,0:T(8,128)(2,1)}, u32[]{:S(2)}) copy-start(bf16[512,256]{1,0:T(8,128)(2,1)} %get-tuple-element.44) | copy-start | bytes 786436
  141.6 142.0 %all-gather.5.cloned.1.call-start = ((), (), s32[]{:S(2)}) async-start(), calls=%async_computation.13 | async-start | bytes 2162688 | tf_op jit(solution)/shard_map/all_gather | solution.py:523
  150.7 16.4 %copy-start.2 = (bf16[64,2,48,128]{3,2,1,0:T(8,128)(2,1)}, bf16[64,2,48,128]{3,2,1,0:T(8,128)(2,1)S(1)}, u32[]{:S(2)}) copy-start(bf16[64,2,48,128]{3,2,1,0:T(8,128)(2,1)S(1)} %all-to-all-done.3) | copy-start | bytes 4718596
  167.2 11.3 %collective-permute-start.2 = (bf16[8,48,256]{2,1,0:T(8,128)(2,1)}, bf16[8,48,256]{2,1,0:T(8,128)(2,1)S(1)}, u32[]{:S(2)}, u32[]{:S(2)}) collective-permute-start(bf16[8,48,256]{2,1,0:T(8,128)(2,1)} %bitcast.82), channel_id=1, source_target_pairs={{0,48},{16,0},{32,16},{48,32},{1,49},{17,1},{33,17},{49,33},{2,50}... | collective-permute-start | bytes 589832 | tf_op jit(solution)/shard_map/ppermute | solution.py:477
  167.3 12.6 %collective-permute-start.1 = (bf16[8,48,256]{2,1,0:T(8,128)(2,1)}, bf16[8,48,256]{2,1,0:T(8,128)(2,1)S(1)}, u32[]{:S(2)}, u32[]{:S(2)}) collective-permute-start(bf16[8,48,256]{2,1,0:T(8,128)(2,1)} %bitcast.83), channel_id=1, source_target_pairs={{0,32},{16,48},{32,0},{48,16},{1,33},{17,49},{33,1},{49,17},{2,34}... | collective-permute-start | bytes 589832 | tf_op jit(solution)/shard_map/ppermute | solution.py:477
  171.2 16.0 %collective-permute-start = (bf16[8,48,256]{2,1,0:T(8,128)(2,1)}, bf16[8,48,256]{2,1,0:T(8,128)(2,1)S(1)}, u32[]{:S(2)}, u32[]{:S(2)}) collective-permute-start(bf16[8,48,256]{2,1,0:T(8,128)(2,1)} %bitcast.84), channel_id=1, source_target_pairs={{0,16},{16,32},{32,48},{48,0},{1,17},{17,33},{33,49},{49,1},{2,18}... | collective-permute-start | bytes 589832 | tf_op jit(solution)/shard_map/ppermute | solution.py:477
  178.5 31.9 %copy-start.5 = (bf16[8,48,256]{2,1,0:T(8,128)(2,1)}, bf16[8,48,256]{2,1,0:T(8,128)(2,1)S(1)}, u32[]{:S(2)}) copy-start(bf16[8,48,256]{2,1,0:T(8,128)(2,1)S(1)} %collective-permute-done.2.d_ref) | copy-start | bytes 589828
  179.8 30.5 %copy-start.6 = (bf16[8,48,256]{2,1,0:T(8,128)(2,1)}, bf16[8,48,256]{2,1,0:T(8,128)(2,1)S(1)}, u32[]{:S(2)}) copy-start(bf16[8,48,256]{2,1,0:T(8,128)(2,1)S(1)} %collective-permute-done.1.c_ref) | copy-start | bytes 589828
  187.2 23.2 %copy-start.7 = (bf16[8,48,256]{2,1,0:T(8,128)(2,1)}, bf16[8,48,256]{2,1,0:T(8,128)(2,1)S(1)}, u32[]{:S(2)}) copy-start(bf16[8,48,256]{2,1,0:T(8,128)(2,1)S(1)} %collective-permute-done.b_ref) | copy-start | bytes 589828
  210.3 32.5 %all-to-all-start.6 = ((bf16[64,2,48,128]{3,2,1,0:T(8,128)(2,1)}), bf16[64,2,48,128]{3,2,1,0:T(8,128)(2,1)S(1)}, u32[]{:S(2)}, u32[]{:S(2)}) async-start(bf16[64,2,48,128]{3,2,1,0:T(8,128)(2,1)} %pack_rows.5), calls=%async_computation.7 | async-start | bytes 3145728 | tf_op jit(solution)/shard_map/all_to_all | solution.py:472
  217.5 25.4 %copy-start.8 = (bf16[16,128,128]{2,1,0:T(8,128)(2,1)S(1)}, bf16[16,128,128]{2,1,0:T(8,128)(2,1)}, u32[]{:S(2)}) copy-start(bf16[16,128,128]{2,1,0:T(8,128)(2,1)} %param.21) | copy-start | bytes 1572868
  242.8 18.1 %copy-start.3 = (bf16[64,2,48,128]{3,2,1,0:T(8,128)(2,1)}, bf16[64,2,48,128]{3,2,1,0:T(8,128)(2,1)S(1)}, u32[]{:S(2)}) copy-start(bf16[64,2,48,128]{3,2,1,0:T(8,128)(2,1)S(1)} %all-to-all-done.6) | copy-start | bytes 4718596
  261.0 51.2 %all-to-all-start.8 = ((bf16[64,4,48,128]{3,2,1,0:T(8,128)(2,1)}), bf16[64,4,48,128]{3,2,1,0:T(8,128)(2,1)S(1)}, u32[]{:S(2)}, u32[]{:S(2)}) async-start(bf16[64,4,48,128]{3,2,1,0:T(8,128)(2,1)} %bitcast.71), calls=%async_computation.9 | async-start | bytes 6291456 | tf_op jit(solution)/shard_map/all_to_all | solution.py:472
  286.6 29.8 %copy-start.10 = (bf16[128,256]{1,0:T(8,128)(2,1)S(1)}, bf16[128,256]{1,0:T(8,128)(2,1)}, u32[]{:S(2)}) copy-start(bf16[128,256]{1,0:T(8,128)(2,1)} %projection.1) | copy-start | bytes 196612
  286.6 29.9 %copy-start.14 = (bf16[128,128]{1,0:T(8,128)(2,1)S(1)}, bf16[128,128]{1,0:T(8,128)(2,1)}, u32[]{:S(2)}) copy-start(bf16[128,128]{1,0:T(8,128)(2,1)} %param.24) | copy-start | bytes 98308
  286.6 29.9 %copy-start.15 = (bf16[128,128]{1,0:T(8,128)(2,1)S(1)}, bf16[128,128]{1,0:T(8,128)(2,1)}, u32[]{:S(2)}) copy-start(bf16[128,128]{1,0:T(8,128)(2,1)} %param.23) | copy-start | bytes 98308
  312.2 9.2 %copy-start.1 = (bf16[64,4,48,128]{3,2,1,0:T(8,128)(2,1)}, bf16[64,4,48,128]{3,2,1,0:T(8,128)(2,1)S(1)}, u32[]{:S(2)}) copy-start(bf16[64,4,48,128]{3,2,1,0:T(8,128)(2,1)S(1)} %all-to-all-done.8.back_ref) | copy-start | bytes 9437188
  312.2 21.2 %all-to-all-start.9 = ((bf16[16,2,128,128]{3,2,1,0:T(8,128)(2,1)}), bf16[16,2,128,128]{3,2,1,0:T(8,128)(2,1)}, u32[]{:S(2)}, u32[]{:S(2)}) async-start(bf16[16,2,128,128]{3,2,1,0:T(8,128)(2,1)} %bitcast.77), calls=%async_computation.10 | async-start | bytes 2097152 | tf_op jit(solution)/shard_map/all_to_all | solution.py:472
  316.4 1.3 collective-permute-start.3
  317.8 14.9 %collective-permute-start.5 = (bf16[128,256]{1,0:T(8,128)(2,1)S(1)}, bf16[128,256]{1,0:T(8,128)(2,1)S(1)}, u32[]{:S(2)}, u32[]{:S(2)}) collective-permute-start(bf16[128,256]{1,0:T(8,128)(2,1)S(1)} %get-tuple-element.56), channel_id=1, source_target_pairs={{0,2},{2,4},{4,6},{6,0},{1,3},{3,5},{5,7},{7,1},{8,10},{10,12},{12... | collective-permute-start | bytes 196616 | tf_op jit(solution)/shard_map/ppermute | solution.py:477
  318.9 13.8 %collective-permute-start.4 = (bf16[128,256]{1,0:T(8,128)(2,1)S(1)}, bf16[128,256]{1,0:T(8,128)(2,1)S(1)}, u32[]{:S(2)}, u32[]{:S(2)}) collective-permute-start(bf16[128,256]{1,0:T(8,128)(2,1)S(1)} %get-tuple-element.56), channel_id=1, source_target_pairs={{0,4},{2,6},{4,0},{6,2},{1,5},{3,7},{5,1},{7,3},{8,12},{10,14},{12... | collective-permute-start | bytes 196616 | tf_op jit(solution)/shard_map/ppermute | solution.py:477
  319.3 13.4 %collective-permute-start.6 = (bf16[128,256]{1,0:T(8,128)(2,1)S(1)}, bf16[128,256]{1,0:T(8,128)(2,1)S(1)}, u32[]{:S(2)}, u32[]{:S(2)}) collective-permute-start(bf16[128,256]{1,0:T(8,128)(2,1)S(1)} %get-tuple-element.56), channel_id=1, source_target_pairs={{0,6},{2,0},{4,2},{6,4},{1,7},{3,1},{5,3},{7,5},{8,14},{10,8},{12,... | collective-permute-start | bytes 196616 | tf_op jit(solution)/shard_map/ppermute | solution.py:477
Sparse Core Ops, SparseCore 0:
  37.5 86.2 all-gather.2
  141.7 32.5 reduce-scatter.1
  210.4 73.1 all-gather.4

commit v6 on v5

--- a/solution.py
+++ b/solution.py
@@ -518,15 +518,15 @@
     mine = exchange(after(slots, hid_a).reshape(64, PAD, 2 * HD), WIDE).reshape(64 * PAD, 2 * HD)
     dqg = unpad_rows(mine, unpad).reshape(8, 8 * ROWS, 2 * HD)
     dqg = gather(dqg, "zh")
-    dkv_z = exchange(after(dkv_x, *dqg).reshape(8, BLOCK, 2 * HD), ("zh", "zl"))
+    w_query_r = exchange(after(w_query, mine), SLAB).reshape(8, EPD, HD, HD)
+    dkv_z = exchange(after(dkv_x, w_query_r, *dqg).reshape(8, BLOCK, 2 * HD), ("zh", "zl"))
     dkv_own = dkv_z.astype(F32).sum(axis=0).astype(BF16)
     dkv = lax.all_gather(dkv_own, SEQ, axis=0, tiled=True)
     proj = projection(hidden[0], dkv)
     hid_b = exchange(after(hid_b, dkv_own), WIDE)
     wq, wo = early_weights(at, dqg, hid_a, grad_rows)
-    w_query_r = exchange(after(w_query, hid_b, wq), SLAB).reshape(8, EPD, HD, HD)
     back_rows = route_back(at, dqg, w_query_r).reshape(64, 4, 8 * ROWS, HD)
-    back = exchange(back_rows, WIDE)
+    back = exchange(after(back_rows, hid_b, wq), WIDE)
     dqg[0] = after(dqg[0], back_rows)
     grads = late_weights(at, dqg, hid_b, wq, wo).reshape(16, 2, HD, HD)
     grads = exchange(after(grads, back, proj), SLAB)

time: 344 us -> 345 us (level)
  blocking collectives: 85.7 us -> 72.5 us
  starting transfers between devices: 46.7 us -> 58.1 us
    all_gather x1, waiting for transfers between devices: 11.7 us -> 44.8 us  [per_device(): dkv = lax.all_gather(dkv_own, SEQ, axis=0, tiled=True)]
    all_to_all x6 -> x7, waiting for transfers between devices: 82.9 us -> 52.4 us  [exchange(): return lax.all_to_all(rows, axes, split_axis=0, concat_axis=0, tiled=True)]
    all_to_all x4 -> x3, blocking collectives: 85.7 us -> 72.5 us  [exchange(): return lax.all_to_all(rows, axes, split_axis=0, concat_axis=0, tiled=True)]
    all_to_all x6 -> x7, starting transfers between devices: 38.6 us -> 46 us  [exchange(): return lax.all_to_all(rows, axes, split_axis=0, concat_axis=0, tiled=True)]
    ppermute x7, starting transfers between devices: 7.72 us -> 11.8 us  [shifted(): return lax.ppermute(rows, axis, [(i, (i + s) % n) for i in range(n)])]
  transfers between devices with their start and end apart: 16 -> 17, of which waited for: 9 -> 8; matrix products, arithmetic and copies ran while one was open for 2% -> 2% of each run, Pallas kernels for 21% -> 21%
where the time goes in v6:
time: 345 us; the launch traced here: 343 us
  waiting for transfers between devices  113 us (33%)
  Pallas kernels  72.8 us (21%)
  blocking collectives  72.5 us (21%)
  starting transfers between devices  58.1 us (17%)
  between operations  14 us (4%)
  other arithmetic  7.34 us (2%)
  local copies, waits for them, and re-layouts  6.19 us (2%)
    all_to_all x3, blocking collectives, exchange(): return lax.all_to_all(rows, axes, split_axis=0, concat_axis=0, tiled=True)  72.5 us
    all_to_all x7, waiting for transfers between devices, exchange(): return lax.all_to_all(rows, axes, split_axis=0, concat_axis=0, tiled=True)  52.4 us
    all_to_all x7, starting transfers between devices, exchange(): return lax.all_to_all(rows, axes, split_axis=0, concat_axis=0, tiled=True)  46 us
    all_gather x1, waiting for transfers between devices, per_device(): dkv = lax.all_gather(dkv_own, SEQ, axis=0, tiled=True)  44.8 us
    pallas_call x3, Pallas kernels, pack(): pl.pallas_call(kernel, grid=(steps,), in_specs=[id_spec, slab, pl.BlockSp...  18.1 us
    ppermute x7, waiting for transfers between devices, shifted(): return lax.ppermute(rows, axis, [(i, (i + s) % n) for i in range(n)])  15.3 us
    pallas_call x2, Pallas kernels, weights_call(): pl.pallas_call(kernel, grid=(4,), in_specs=[pl.BlockSpec(memory_space=plt...  13.1 us
    ppermute x7, starting transfers between devices, shifted(): return lax.ppermute(rows, axis, [(i, (i + s) % n) for i in range(n)])  11.8 us
  transfers between devices with their start and end apart: 17, of which 8 were waited for; matrix products, arithmetic and copies ran while one was open for 2% of the time, Pallas kernels for 21%

profile of v6, /device:TPU:1, one launch (start us, length us, event | category | flops | bytes accessed | tf_op | source)
XLA Modules:
  0.0 343.5 jit_solution(2777530090609880520)
XLA Ops:
  7.2 6.2 %all-to-all-start = ((bf16[16,128,128]{2,1,0:T(8,128)(2,1)}), bf16[16,128,128]{2,1,0:T(8,128)(2,1)S(1)}, u32[]{:S(2)}, u32[]{:S(2)}) async-start(bf16[16,128,128]{2,1,0:T(8,128)(2,1)} %param.22), calls=%async_computation | async-start | bytes 1048576 | tf_op jit(solution)/shard_map/all_to_all | solution.py:472
  13.4 9.5 %pack_rows.3 = (bf16[64,4,48,128]{3,2,1,0:T(8,128)(2,1)}, s32[4,4,2,256]{3,2,1,0:T(2,128)}) custom-call(s32[4,4,2,256]{3,2,1,0:T(2,128)} %bitcast.99, bf16[4,4,256,128]{3,2,1,0:T(8,128)(2,1)} %bitcast.88, bf16[384,384]{1,0:T(8,128)(2,1)} %constant.53.clone.swap_ref), custom_call_target="tpu_custom_call" | custom-call | flops 1000 | bytes 1000 | tf_op jit(solution)/shard_map/pack_rows/pallas_call | solution.py:115
  22.8 0.0 copy-start.12
  22.9 0.0 copy-start.13
  22.9 0.8 copy-done.4
  23.6 9.8 %all-to-all-start.1 = ((bf16[64,4,48,128]{3,2,1,0:T(8,128)(2,1)}), bf16[64,4,48,128]{3,2,1,0:T(8,128)(2,1)S(1)}, u32[]{:S(2)}, u32[]{:S(2)}) async-start(bf16[64,4,48,128]{3,2,1,0:T(8,128)(2,1)} %get-tuple-element.33), calls=%async_computation.1 | async-start | bytes 6291456 | tf_op jit(solution)/shard_map/all_to_all | solution.py:472
  33.5 0.0 all-gather.3.cloned.1.call-start
  33.6 0.6 pad_maximum_fusion
  34.2 0.0 all-gather.3.cloned.1.call-update
  34.2 4.3 %pack_rows.5 = bf16[64,2,48,128]{3,2,1,0:T(8,128)(2,1)} custom-call(s32[4,4,2,256]{3,2,1,0:T(2,128)} %get-tuple-element.31.rho_ref, bf16[4,4,256,128]{3,2,1,0:T(8,128)(2,1)} %bitcast.74, bf16[384,384]{1,0:T(8,128)(2,1)} %constant.53.clone.swap_ref), custom_call_target="tpu_custom_call" | custom-call | flops 1000 | bytes 1000 | tf_op jit(solution)/shard_map/pack_rows/pallas_call | solution.py:115
  38.6 4.3 %pack_rows.4 = bf16[64,2,48,128]{3,2,1,0:T(8,128)(2,1)} custom-call(s32[4,4,2,256]{3,2,1,0:T(2,128)} %get-tuple-element.31.rho_ref, bf16[4,4,256,128]{3,2,1,0:T(8,128)(2,1)} %bitcast.75, bf16[384,384]{1,0:T(8,128)(2,1)} %constant.53.clone.swap_ref), custom_call_target="tpu_custom_call" | custom-call | flops 1000 | bytes 1000 | tf_op jit(solution)/shard_map/pack_rows/pallas_call | solution.py:115
  42.9 0.6 copy.39
  43.5 0.7 compare_bitcast_fusion
  44.2 0.2 copy.44
  44.4 0.1 copy.32
  44.5 0.1 copy.34
  44.7 0.6 fusion.4.rho_row_ref
  45.3 0.7 fusion.3.rho_col_ref
  46.0 30.4 %all-to-all-done.1 = bf16[64,4,48,128]{3,2,1,0:T(8,128)(2,1)S(1)} async-done(((bf16[64,4,48,128]{3,2,1,0:T(8,128)(2,1)}), bf16[64,4,48,128]{3,2,1,0:T(8,128)(2,1)S(1)}, u32[]{:S(2)}, u32[]{:S(2)}) %all-to-all-start.1) | async-done | bytes 3145760 | tf_op jit(solution)/shard_map/all_to_all | solution.py:472
  76.4 1.6 copy-done
  78.1 4.8 %head_sums.1 = (bf16[8,48,128]{2,1,0:T(8,128)(2,1)}, bf16[8,48,128]{2,1,0:T(8,128)(2,1)}, bf16[8,48,128]{2,1,0:T(8,128)(2,1)}, bf16[8,48,128]{2,1,0:T(8,128)(2,1)}) custom-call(bf16[8,8,192,128]{3,2,1,0:T(8,128)(2,1)} %bitcast.69, bf16[8,256,128]{2,1,0:T(8,128)(2,1)} %bitcast.78), custom_call_target="tpu_custom_call" | custom-call | flops 1000 | bytes 1000 | tf_op jit(solution)/shard_map/head_sums/pallas_call | solution.py:144
  82.9 2.6 address_heads.1
  85.4 35.7 %all_to_all.50 = bf16[256,8,128]{2,1,0:T(8,128)(2,1)} all-to-all(bf16[256,8,128]{2,1,0:T(8,128)(2,1)} %bitcast.80), channel_id=1, replica_groups=mesh['x'=4,'zh'=4,'zl'=2,'node'=4,'dev'=2] {'x','zh','zl','node','dev'}, dimensions={0} | all-to-all | bytes 1048576 | tf_op jit(solution)/shard_map/all_to_all | solution.py:472
  121.2 6.1 %all-to-all-start.3 = ((bf16[64,2,48,128]{3,2,1,0:T(8,128)(2,1)}), bf16[64,2,48,128]{3,2,1,0:T(8,128)(2,1)S(1)}, u32[]{:S(2)}, u32[]{:S(2)}) async-start(bf16[64,2,48,128]{3,2,1,0:T(8,128)(2,1)} %pack_rows.4), calls=%async_computation.3 | async-start | bytes 3145728 | tf_op jit(solution)/shard_map/all_to_all | solution.py:472
  127.3 0.2 reduce-scatter.2.cloned.1.call-start
  127.5 0.8 copy.41.gate_ref
  128.3 0.6 pad_add_fusion.at_ref
  128.9 5.0 %attend_forward.1 = (bf16[256,4096]{1,0:T(8,128)(2,1)}, f32[256,128]{1,0:T(8,128)}, bf16[256,128]{1,0:T(8,128)(2,1)}) custom-call(s32[3]{0:T(128)} %pad_add_fusion.at_ref, bf16[256,128]{1,0:T(8,128)(2,1)} %bitcast.89, bf16[4096,256]{1,0:T(8,128)(2,1)} %all-gather.3.cloned.1.call-done.kv_ref, f32[256,1]{1,0:T(8,128)} %copy.41.gate_ref), custom_call_target="tpu_custom_call" | custom-call | flops 1000 | bytes 1000 | tf_op jit(solution)/shard_map/attend_forward/pallas_call | solution.py:207
  133.9 7.7 %attend_backward.1 = (bf16[512,256]{1,0:T(8,128)(2,1)}, bf16[4096,256]{1,0:T(8,128)(2,1)}) custom-call(bf16[2048,128]{1,0:T(8,128)(2,1)} %bitcast.81, s32[1,256]{1,0:T(1,128)} %fusion.4.rho_row_ref, s32[256,1]{1,0:T(8,128)} %fusion.3.rho_col_ref, f32[256,1]{1,0:T(8,128)} %copy.41.gate_ref, bf16[256,128]{1,0:T(8,128)(2,1)} %bitcast.90, ...), custom_call_target="tpu_custom_call" | custom-call | flops 1000 | bytes 1000 | tf_op jit(solution)/shard_map/attend_backward/pallas_call | solution.py:251
  141.6 0.0 reduce-scatter.2.cloned.1.call-update
  141.6 9.1 %all-to-all-done.3 = bf16[64,2,48,128]{3,2,1,0:T(8,128)(2,1)S(1)} async-done(((bf16[64,2,48,128]{3,2,1,0:T(8,128)(2,1)}), bf16[64,2,48,128]{3,2,1,0:T(8,128)(2,1)S(1)}, u32[]{:S(2)}, u32[]{:S(2)}) %all-to-all-start.3) | async-done | bytes 1572896 | tf_op jit(solution)/shard_map/all_to_all | solution.py:472
  150.7 14.4 %all_to_all.51 = bf16[64,8,256]{2,1,0:T(8,128)(2,1)} all-to-all(bf16[64,8,256]{2,1,0:T(8,128)(2,1)S(1)} %bitcast.92), channel_id=1, replica_groups=mesh['x'=4,'zh'=4,'zl'=2,'node'=4,'dev'=2] {'x','zl','node','dev'}, dimensions={0} | all-to-all | bytes 524288 | tf_op jit(solution)/shard_map/all_to_all | solution.py:472
  165.1 3.5 %all-to-all-start.5 = ((bf16[16,128,128]{2,1,0:T(8,128)(2,1)}), bf16[16,128,128]{2,1,0:T(8,128)(2,1)S(1)}, u32[]{:S(2)}, u32[]{:S(2)}) async-start(bf16[16,128,128]{2,1,0:T(8,128)(2,1)} %param.21), calls=%async_computation.5 | async-start | bytes 1048576 | tf_op jit(solution)/shard_map/all_to_all | solution.py:472
  168.6 0.0 all-gather.5.cloned.1.call-start
  168.7 2.0 unpad_rows.1
  170.7 0.2 collective-permute-start.2
  170.9 3.8 %collective-permute-start.1 = (bf16[8,48,256]{2,1,0:T(8,128)(2,1)}, bf16[8,48,256]{2,1,0:T(8,128)(2,1)S(1)}, u32[]{:S(2)}, u32[]{:S(2)}) collective-permute-start(bf16[8,48,256]{2,1,0:T(8,128)(2,1)} %bitcast.83), channel_id=1, source_target_pairs={{0,32},{16,48},{32,0},{48,16},{1,33},{17,49},{33,1},{49,17},{2,34}... | collective-permute-start | bytes 589832 | tf_op jit(solution)/shard_map/ppermute | solution.py:477
  174.8 2.8 collective-permute-done.2.d_ref
  177.5 4.8 %collective-permute-done.1.c_ref = bf16[8,48,256]{2,1,0:T(8,128)(2,1)S(1)} collective-permute-done((bf16[8,48,256]{2,1,0:T(8,128)(2,1)}, bf16[8,48,256]{2,1,0:T(8,128)(2,1)S(1)}, u32[]{:S(2)}, u32[]{:S(2)}) %collective-permute-start.1) | collective-permute-done | bytes 196640 | tf_op jit(solution)/shard_map/ppermute | solution.py:477
  182.3 7.5 %collective-permute-done.b_ref = bf16[8,48,256]{2,1,0:T(8,128)(2,1)S(1)} collective-permute-done((bf16[8,48,256]{2,1,0:T(8,128)(2,1)}, bf16[8,48,256]{2,1,0:T(8,128)(2,1)S(1)}, u32[]{:S(2)}, u32[]{:S(2)}) %collective-permute-start) | collective-permute-done | bytes 196640 | tf_op jit(solution)/shard_map/ppermute | solution.py:477
  189.9 0.0 all-to-all-done.5
  189.9 22.4 %all_to_all.52 = bf16[8,128,256]{2,1,0:T(8,128)(2,1)S(1)} all-to-all(bf16[8,128,256]{2,1,0:T(8,128)(2,1)} %bitcast.91), channel_id=1, replica_groups=mesh['x'=4,'zh'=4,'zl'=2,'node'=4,'dev'=2] {'zh','zl'}, dimensions={0} | all-to-all | bytes 1048576 | tf_op jit(solution)/shard_map/all_to_all | solution.py:472
  212.2 0.7 reduce_sum.12
  213.0 0.0 all-gather.5.cloned.1.call-update
  213.0 11.2 %all-to-all-start.7 = ((bf16[64,2,48,128]{3,2,1,0:T(8,128)(2,1)}), bf16[64,2,48,128]{3,2,1,0:T(8,128)(2,1)S(1)}, u32[]{:S(2)}, u32[]{:S(2)}) async-start(bf16[64,2,48,128]{3,2,1,0:T(8,128)(2,1)} %pack_rows.5), calls=%async_computation.8 | async-start | bytes 3145728 | tf_op jit(solution)/shard_map/all_to_all | solution.py:472
  224.3 7.5 %early_weights.1 = (f32[8,128,256]{2,1,0:T(8,128)}, f32[8,256,128]{2,1,0:T(8,128)}) custom-call(s32[3]{0:T(128)} %pad_add_fusion.at_ref, bf16[8,48,256]{2,1,0:T(8,128)(2,1)} %bitcast.85, bf16[8,48,256]{2,1,0:T(8,128)(2,1)} %copy-done.8, bf16[8,48,256]{2,1,0:T(8,128)(2,1)} %copy-done.7, bf16[8,48,256]{2,1,0:T(8,128)(2,1)} %copy-done.6, ...), custom_call_target="tpu_custom_call" | custom-call | flops 1000 | bytes 1000 | tf_op jit(solution)/shard_map/early_weights/pallas_call | solution.py:356
  231.7 5.1 %route_back.1 = bf16[8,8,192,128]{3,2,1,0:T(8,128)(2,1)} custom-call(s32[3]{0:T(128)} %pad_add_fusion.at_ref, bf16[8,48,256]{2,1,0:T(8,128)(2,1)} %bitcast.86, bf16[8,48,256]{2,1,0:T(8,128)(2,1)} %copy-done.8, bf16[8,48,256]{2,1,0:T(8,128)(2,1)} %copy-done.7, bf16[8,48,256]{2,1,0:T(8,128)(2,1)} %copy-done.6, bf16[8,2,128,128]{3,2,1,0:T(8,128)(2,1)} %bitcast.79), custom_call_target="tpu_custom_call" | custom-call | flops 1000 | bytes 1000 | tf_op jit(solution)/shard_map/route_back/pallas_call | solution.py:299
  236.8 12.8 %all-to-all-done.7 = bf16[64,2,48,128]{3,2,1,0:T(8,128)(2,1)S(1)} async-done(((bf16[64,2,48,128]{3,2,1,0:T(8,128)(2,1)}), bf16[64,2,48,128]{3,2,1,0:T(8,128)(2,1)S(1)}, u32[]{:S(2)}, u32[]{:S(2)}) %all-to-all-start.7) | async-done | bytes 1572896 | tf_op jit(solution)/shard_map/all_to_all | solution.py:472
  249.6 1.2 copy-done.3
  250.8 4.7 %all-to-all-start.8 = ((bf16[64,4,48,128]{3,2,1,0:T(8,128)(2,1)}), bf16[64,4,48,128]{3,2,1,0:T(8,128)(2,1)S(1)}, u32[]{:S(2)}, u32[]{:S(2)}) async-start(bf16[64,4,48,128]{3,2,1,0:T(8,128)(2,1)} %bitcast.71), calls=%async_computation.9 | async-start | bytes 6291456 | tf_op jit(solution)/shard_map/all_to_all | solution.py:472
  255.5 5.7 %late_weights.1 = bf16[8,2,2,128,128]{4,3,2,1,0:T(8,128)(2,1)} custom-call(s32[3]{0:T(128)} %pad_add_fusion.at_ref, bf16[8,48,256]{2,1,0:T(8,128)(2,1)} %bitcast.87, bf16[8,48,256]{2,1,0:T(8,128)(2,1)} %copy-done.8, bf16[8,48,256]{2,1,0:T(8,128)(2,1)} %copy-done.7, bf16[8,48,256]{2,1,0:T(8,128)(2,1)} %copy-done.6, bf16[8,8,96,128]{3,2,1,0:T(8,128)(2,1)} %bitcast.73, ...), custom_call_target="tpu_custom_call" | custom-call | flops 1000 | bytes 1000 | tf_op jit(solution)/shard_map/late_weights/pallas_call | solution.py:356
  261.2 44.8 %all-gather.5.cloned.1.call-done.dkv_ref = bf16[4096,256]{1,0:T(8,128)(2,1)} async-done(((bf16[128,256]{1,0:T(8,128)(2,1)}), bf16[4096,256]{1,0:T(8,128)(2,1)}) %all-gather.5.cloned.1.call-update) | async-done | bytes 2097168 | tf_op jit(solution)/shard_map/all_gather | solution.py:524
  306.0 3.0 projection.1
  309.0 0.0 all-to-all-done.8.back_ref
  309.1 4.4 %all-to-all-start.9 = ((bf16[16,2,128,128]{3,2,1,0:T(8,128)(2,1)}), bf16[16,2,128,128]{3,2,1,0:T(8,128)(2,1)}, u32[]{:S(2)}, u32[]{:S(2)}) async-start(bf16[16,2,128,128]{3,2,1,0:T(8,128)(2,1)} %bitcast.77), calls=%async_computation.10 | async-start | bytes 2097152 | tf_op jit(solution)/shard_map/all_to_all | solution.py:472
  313.5 2.7 collective-permute-start.3
  316.1 0.6 pad_maximum_fusion.1.wkv_ref
  316.8 0.3 collective-permute-done.3
  317.1 0.1 collective-permute-start.5
  317.1 5.0 %collective-permute-start.4 = (bf16[128,256]{1,0:T(8,128)(2,1)S(1)}, bf16[128,256]{1,0:T(8,128)(2,1)S(1)}, u32[]{:S(2)}, u32[]{:S(2)}) collective-permute-start(bf16[128,256]{1,0:T(8,128)(2,1)S(1)} %get-tuple-element.58), channel_id=1, source_target_pairs={{0,4},{2,6},{4,0},{6,2},{1,5},{3,7},{5,1},{7,3},{8,12},{10,14},{12... | collective-permute-start | bytes 196616 | tf_op jit(solution)/shard_map/ppermute | solution.py:477
  322.2 6.8 %unpack_rows.1.rows_ref = f32[4,4,256,128]{3,2,1,0:T(8,128)} custom-call(s32[4,4,2,256]{3,2,1,0:T(2,128)} %get-tuple-element.31.rho_ref, bf16[64,4,48,128]{3,2,1,0:T(8,128)(2,1)} %copy-done.1, bf16[384,384]{1,0:T(8,128)(2,1)} %constant.53.clone.swap_ref), custom_call_target="tpu_custom_call" | custom-call | flops 1000 | bytes 1000 | tf_op jit(solution)/shard_map/unpack_rows/pallas_call | solution.py:431
  329.0 4.5 %finish_rows.1 = bf16[4,4,256,128]{3,2,1,0:T(8,128)(2,1)} custom-call(f32[4,4,256,128]{3,2,1,0:T(8,128)} %unpack_rows.1.rows_ref, bf16[4,4,256,256]{3,2,1,0:T(8,128)(2,1)} %bitcast.108, bf16[128,256]{1,0:T(8,128)(2,1)} %pad_maximum_fusion.1.wkv_ref), custom_call_target="tpu_custom_call" | custom-call | flops 5000000000 | bytes 10000000 | tf_op jit(solution)/shard_map/finish_rows/pallas_call | solution.py:455
  333.5 0.7 fusion.6
  334.2 2.8 fusion
  (42 shorter events, 0.1 us)
Async XLA Ops:
  7.2 15.7 %all-to-all-start = ((bf16[16,128,128]{2,1,0:T(8,128)(2,1)}), bf16[16,128,128]{2,1,0:T(8,128)(2,1)S(1)}, u32[]{:S(2)}, u32[]{:S(2)}) async-start(bf16[16,128,128]{2,1,0:T(8,128)(2,1)} %param.22), calls=%async_computation | async-start | bytes 1048576 | tf_op jit(solution)/shard_map/all_to_all | solution.py:472
  22.8 0.8 copy-start.4
  22.8 10.7 %copy-start.12 = (bf16[1,128,128]{2,1,0:T(8,128)(2,1)S(1)}, bf16[1,128,128]{2,1,0:T(8,128)(2,1)}, u32[]{:S(2)}) copy-start(bf16[1,128,128]{2,1,0:T(8,128)(2,1)} %param.18) | copy-start | bytes 98308
  22.9 10.7 %copy-start.13 = (bf16[1,128,128]{2,1,0:T(8,128)(2,1)S(1)}, bf16[1,128,128]{2,1,0:T(8,128)(2,1)}, u32[]{:S(2)}) copy-start(bf16[1,128,128]{2,1,0:T(8,128)(2,1)} %param.17) | copy-start | bytes 98308
  23.6 52.8 %all-to-all-start.1 = ((bf16[64,4,48,128]{3,2,1,0:T(8,128)(2,1)}), bf16[64,4,48,128]{3,2,1,0:T(8,128)(2,1)S(1)}, u32[]{:S(2)}, u32[]{:S(2)}) async-start(bf16[64,4,48,128]{3,2,1,0:T(8,128)(2,1)} %get-tuple-element.33), calls=%async_computation.1 | async-start | bytes 6291456 | tf_op jit(solution)/shard_map/all_to_all | solution.py:472
  33.5 95.4 %all-gather.3.cloned.1.call-start = ((), (), s32[]{:S(2)}) async-start(), calls=%async_computation.11 | async-start | bytes 2162688 | tf_op jit(solution)/shard_map/all_gather | solution.py:495
  38.6 4.3 %copy-start.11 = (bf16[1,128,2,128]{3,2,1,0:T(2,128)(2,1)S(1)}, bf16[1,128,2,128]{3,2,1,0:T(2,128)(2,1)}, u32[]{:S(2)}) copy-start(bf16[1,128,2,128]{3,2,1,0:T(2,128)(2,1)} %param.16) | copy-start | bytes 196612
  76.4 1.6 copy-start
  85.4 42.0 %copy-start.16 = (f32[1,128,2]{1,2,0:T(2,128)S(1)}, f32[1,128,2]{1,2,0:T(2,128)}, u32[]{:S(2)}) copy-start(f32[1,128,2]{1,2,0:T(2,128)} %param.20) | copy-start | bytes 3076
  121.2 29.5 %all-to-all-start.3 = ((bf16[64,2,48,128]{3,2,1,0:T(8,128)(2,1)}), bf16[64,2,48,128]{3,2,1,0:T(8,128)(2,1)S(1)}, u32[]{:S(2)}, u32[]{:S(2)}) async-start(bf16[64,2,48,128]{3,2,1,0:T(8,128)(2,1)} %pack_rows.4), calls=%async_computation.3 | async-start | bytes 3145728 | tf_op jit(solution)/shard_map/all_to_all | solution.py:472
  127.3 62.6 %reduce-scatter.2.cloned.1.call-start = ((), (), s32[]{:S(2)}) async-start(), calls=%async_computation.12 | async-start | bytes 2621440 | tf_op jit(solution)/shard_map/reduce_scatter | solution.py:517
  141.6 9.2 %copy-start.9 = (bf16[512,256]{1,0:T(8,128)(2,1)S(1)}, bf16[512,256]{1,0:T(8,128)(2,1)}, u32[]{:S(2)}) copy-start(bf16[512,256]{1,0:T(8,128)(2,1)} %get-tuple-element.45) | copy-start | bytes 786436
  150.7 20.0 %copy-start.2 = (bf16[64,2,48,128]{3,2,1,0:T(8,128)(2,1)}, bf16[64,2,48,128]{3,2,1,0:T(8,128)(2,1)S(1)}, u32[]{:S(2)}) copy-start(bf16[64,2,48,128]{3,2,1,0:T(8,128)(2,1)S(1)} %all-to-all-done.3) | copy-start | bytes 4718596
  165.1 24.7 %all-to-all-start.5 = ((bf16[16,128,128]{2,1,0:T(8,128)(2,1)}), bf16[16,128,128]{2,1,0:T(8,128)(2,1)S(1)}, u32[]{:S(2)}, u32[]{:S(2)}) async-start(bf16[16,128,128]{2,1,0:T(8,128)(2,1)} %param.21), calls=%async_computation.5 | async-start | bytes 1048576 | tf_op jit(solution)/shard_map/all_to_all | solution.py:472
  168.6 137.4 %all-gather.5.cloned.1.call-start = ((), (), s32[]{:S(2)}) async-start(), calls=%async_computation.13 | async-start | bytes 2162688 | tf_op jit(solution)/shard_map/all_gather | solution.py:524
  170.7 6.8 %collective-permute-start.2 = (bf16[8,48,256]{2,1,0:T(8,128)(2,1)}, bf16[8,48,256]{2,1,0:T(8,128)(2,1)S(1)}, u32[]{:S(2)}, u32[]{:S(2)}) collective-permute-start(bf16[8,48,256]{2,1,0:T(8,128)(2,1)} %bitcast.82), channel_id=1, source_target_pairs={{0,48},{16,0},{32,16},{48,32},{1,49},{17,1},{33,17},{49,33},{2,50}... | collective-permute-start | bytes 589832 | tf_op jit(solution)/shard_map/ppermute | solution.py:477
  170.9 11.4 %collective-permute-start.1 = (bf16[8,48,256]{2,1,0:T(8,128)(2,1)}, bf16[8,48,256]{2,1,0:T(8,128)(2,1)S(1)}, u32[]{:S(2)}, u32[]{:S(2)}) collective-permute-start(bf16[8,48,256]{2,1,0:T(8,128)(2,1)} %bitcast.83), channel_id=1, source_target_pairs={{0,32},{16,48},{32,0},{48,16},{1,33},{17,49},{33,1},{49,17},{2,34}... | collective-permute-start | bytes 589832 | tf_op jit(solution)/shard_map/ppermute | solution.py:477
  174.8 15.1 %collective-permute-start = (bf16[8,48,256]{2,1,0:T(8,128)(2,1)}, bf16[8,48,256]{2,1,0:T(8,128)(2,1)S(1)}, u32[]{:S(2)}, u32[]{:S(2)}) collective-permute-start(bf16[8,48,256]{2,1,0:T(8,128)(2,1)} %bitcast.84), channel_id=1, source_target_pairs={{0,16},{16,32},{32,48},{48,0},{1,17},{17,33},{33,49},{49,1},{2,18}... | collective-permute-start | bytes 589832 | tf_op jit(solution)/shard_map/ppermute | solution.py:477
  177.5 35.4 %copy-start.6 = (bf16[8,48,256]{2,1,0:T(8,128)(2,1)}, bf16[8,48,256]{2,1,0:T(8,128)(2,1)S(1)}, u32[]{:S(2)}) copy-start(bf16[8,48,256]{2,1,0:T(8,128)(2,1)S(1)} %collective-permute-done.2.d_ref) | copy-start | bytes 589828
  182.3 30.6 %copy-start.7 = (bf16[8,48,256]{2,1,0:T(8,128)(2,1)}, bf16[8,48,256]{2,1,0:T(8,128)(2,1)S(1)}, u32[]{:S(2)}) copy-start(bf16[8,48,256]{2,1,0:T(8,128)(2,1)S(1)} %collective-permute-done.1.c_ref) | copy-start | bytes 589828
  189.8 23.1 %copy-start.8 = (bf16[8,48,256]{2,1,0:T(8,128)(2,1)}, bf16[8,48,256]{2,1,0:T(8,128)(2,1)S(1)}, u32[]{:S(2)}) copy-start(bf16[8,48,256]{2,1,0:T(8,128)(2,1)S(1)} %collective-permute-done.b_ref) | copy-start | bytes 589828
  189.9 23.2 %copy-start.5 = (bf16[16,128,128]{2,1,0:T(8,128)(2,1)}, bf16[16,128,128]{2,1,0:T(8,128)(2,1)S(1)}, u32[]{:S(2)}) copy-start(bf16[16,128,128]{2,1,0:T(8,128)(2,1)S(1)} %all-to-all-done.5) | copy-start | bytes 1572868
  213.0 36.6 %all-to-all-start.7 = ((bf16[64,2,48,128]{3,2,1,0:T(8,128)(2,1)}), bf16[64,2,48,128]{3,2,1,0:T(8,128)(2,1)S(1)}, u32[]{:S(2)}, u32[]{:S(2)}) async-start(bf16[64,2,48,128]{3,2,1,0:T(8,128)(2,1)} %pack_rows.5), calls=%async_computation.8 | async-start | bytes 3145728 | tf_op jit(solution)/shard_map/all_to_all | solution.py:472
  249.6 1.2 copy-start.3
  250.8 58.2 %all-to-all-start.8 = ((bf16[64,4,48,128]{3,2,1,0:T(8,128)(2,1)}), bf16[64,4,48,128]{3,2,1,0:T(8,128)(2,1)S(1)}, u32[]{:S(2)}, u32[]{:S(2)}) async-start(bf16[64,4,48,128]{3,2,1,0:T(8,128)(2,1)} %bitcast.71), calls=%async_computation.9 | async-start | bytes 6291456 | tf_op jit(solution)/shard_map/all_to_all | solution.py:472
  309.0 4.4 %copy-start.10 = (bf16[128,256]{1,0:T(8,128)(2,1)S(1)}, bf16[128,256]{1,0:T(8,128)(2,1)}, u32[]{:S(2)}) copy-start(bf16[128,256]{1,0:T(8,128)(2,1)} %projection.1) | copy-start | bytes 196612
  309.0 7.1 %copy-start.14 = (bf16[128,128]{1,0:T(8,128)(2,1)S(1)}, bf16[128,128]{1,0:T(8,128)(2,1)}, u32[]{:S(2)}) copy-start(bf16[128,128]{1,0:T(8,128)(2,1)} %param.24) | copy-start | bytes 98308
  309.0 7.1 %copy-start.15 = (bf16[128,128]{1,0:T(8,128)(2,1)S(1)}, bf16[128,128]{1,0:T(8,128)(2,1)}, u32[]{:S(2)}) copy-start(bf16[128,128]{1,0:T(8,128)(2,1)} %param.23) | copy-start | bytes 98308
  309.0 13.1 %copy-start.1 = (bf16[64,4,48,128]{3,2,1,0:T(8,128)(2,1)}, bf16[64,4,48,128]{3,2,1,0:T(8,128)(2,1)S(1)}, u32[]{:S(2)}) copy-start(bf16[64,4,48,128]{3,2,1,0:T(8,128)(2,1)S(1)} %all-to-all-done.8.back_ref) | copy-start | bytes 9437188
  309.1 25.1 %all-to-all-start.9 = ((bf16[16,2,128,128]{3,2,1,0:T(8,128)(2,1)}), bf16[16,2,128,128]{3,2,1,0:T(8,128)(2,1)}, u32[]{:S(2)}, u32[]{:S(2)}) async-start(bf16[16,2,128,128]{3,2,1,0:T(8,128)(2,1)} %bitcast.77), calls=%async_computation.10 | async-start | bytes 2097152 | tf_op jit(solution)/shard_map/all_to_all | solution.py:472
  313.5 3.6 %collective-permute-start.3 = (bf16[128,256]{1,0:T(8,128)(2,1)S(1)}, bf16[128,256]{1,0:T(8,128)(2,1)S(1)}, u32[]{:S(2)}, u32[]{:S(2)}) collective-permute-start(bf16[128,256]{1,0:T(8,128)(2,1)S(1)} %copy-done.10), channel_id=1, source_target_pairs={{0,1},{1,0},{2,3},{3,2},{4,5},{5,4},{6,7},{7,6},{8,9},{9,8},{10,11... | collective-permute-start | bytes 196616 | tf_op jit(solution)/shard_map/ppermute | solution.py:477
  317.1 16.4 %collective-permute-start.5 = (bf16[128,256]{1,0:T(8,128)(2,1)S(1)}, bf16[128,256]{1,0:T(8,128)(2,1)S(1)}, u32[]{:S(2)}, u32[]{:S(2)}) collective-permute-start(bf16[128,256]{1,0:T(8,128)(2,1)S(1)} %get-tuple-element.58), channel_id=1, source_target_pairs={{0,2},{2,4},{4,6},{6,0},{1,3},{3,5},{5,7},{7,1},{8,10},{10,12},{12... | collective-permute-start | bytes 196616 | tf_op jit(solution)/shard_map/ppermute | solution.py:477
  317.1 16.3 %collective-permute-start.4 = (bf16[128,256]{1,0:T(8,128)(2,1)S(1)}, bf16[128,256]{1,0:T(8,128)(2,1)S(1)}, u32[]{:S(2)}, u32[]{:S(2)}) collective-permute-start(bf16[128,256]{1,0:T(8,128)(2,1)S(1)} %get-tuple-element.58), channel_id=1, source_target_pairs={{0,4},{2,6},{4,0},{6,2},{1,5},{3,7},{5,1},{7,3},{8,12},{10,14},{12... | collective-permute-start | bytes 196616 | tf_op jit(solution)/shard_map/ppermute | solution.py:477
  322.2 11.3 %collective-permute-start.6 = (bf16[128,256]{1,0:T(8,128)(2,1)S(1)}, bf16[128,256]{1,0:T(8,128)(2,1)S(1)}, u32[]{:S(2)}, u32[]{:S(2)}) collective-permute-start(bf16[128,256]{1,0:T(8,128)(2,1)S(1)} %get-tuple-element.58), channel_id=1, source_target_pairs={{0,6},{2,0},{4,2},{6,4},{1,7},{3,1},{5,3},{7,5},{8,14},{10,8},{12,... | collective-permute-start | bytes 196616 | tf_op jit(solution)/shard_map/ppermute | solution.py:477
Sparse Core Ops, SparseCore 0:
  37.5 86.1 all-gather.2
  141.7 32.6 reduce-scatter.1
  213.1 92.8 all-gather.4
